TPU v7x, 32 devices: a whole 2x2x4 slice. The times are simulated.
32 devices in a mesh: rep: 4 (over x, core), own: 8 (over z, y).
Axes of the slice: x: 2, y: 2, z: 4, core: 2. Of those that a mesh axis runs over, the one named last changes fastest.
Arguments:
- replica_delta: float32 [4, 8, 64, 1792], P('rep', None, 'own'), may hold values from -6 to 6
- layer_basis: float32 [4, 1792, 64], replicated, may hold values from -0.25 to 0.25
- layer_of: int32 [8], replicated, may hold values from 0 to 3
- owner_of: int32 [8], replicated, may hold values from 0 to 7, as said below
- weights_owned: float32 [16, 64, 1792], P('own'), may hold values from -6 to 6
- momentum_owned: float32 [16, 64, 1792], P('own'), may hold values from -4 to 4
Outputs:
- new_weights: float32 [16, 64, 1792], P('own')
- new_momentum: float32 [16, 64, 1792], P('own')
- replica_weights: float32 [8, 64, 1792], P(None, 'own')
Inputs may be any that keep to these rules, and one draw needn't show every extreme that they name: `owner_of`: no owner holds more than 2 blocks, and some owner holds exactly 2; the slots of an owner are taken in the order of the blocks.
All inputs are finite; a program needn't handle non-finite values.
Results may differ from a plain program's by a relative error of at most 0.00007.
Values sent between devices are 32-bit elements; how exact they have to be, the bound alone decides.
No kernel may reach another device: no remote copies, remote signals or barrier semaphores. Data moves between devices by JAX's collectives and lax.ppermute only.
A program may use at most 128 MiB of HBM per device.

v0:
```python
import jax
import jax.numpy as jnp
from jax import lax
from jax.sharding import PartitionSpec as P

momentum_decay = 0.9
outer_rate = 0.7


def slot_table(owner_of, capacity):
    blocks = owner_of.shape[0]
    same_owner = owner_of[None, :] == owner_of[:, None]
    positions = jnp.arange(blocks, dtype=jnp.int32)
    earlier = positions[None, :] < positions[:, None]
    rank_in = jnp.sum((same_owner & earlier).astype(jnp.int32), axis=1)
    return owner_of * capacity + rank_in


def local(replica_delta, layer_basis, layer_of, owner_of, weights_owned, momentum_owned):
    highest = lax.Precision.HIGHEST
    own_count = lax.axis_size("own")
    rep_count = lax.axis_size("rep")
    capacity = weights_owned.shape[0]
    slot_of = slot_table(owner_of, capacity)
    slot_total = capacity * own_count
    holding = (slot_of[None, :] == jnp.arange(slot_total, dtype=jnp.int32)[:, None]).astype(
        jnp.float32
    )
    chosen = jnp.take(layer_basis, layer_of, axis=0)
    coeffs = jnp.einsum("bnd,bdk->bnk", replica_delta[0], chosen, precision=highest)
    averaged = lax.psum(coeffs, "rep") / rep_count
    outer_grad = jnp.einsum("bnk,bdk->bnd", averaged, chosen, precision=highest)
    weights_rows, momentum_rows = (
        lax.all_to_all(weights_owned, "own", split_axis=1, concat_axis=0, tiled=True),
        lax.all_to_all(momentum_owned, "own", split_axis=1, concat_axis=0, tiled=True),
    )
    weights_rows = jnp.take(weights_rows, slot_of, axis=0)
    momentum_rows = jnp.take(momentum_rows, slot_of, axis=0)
    momentum_next = momentum_decay * momentum_rows + outer_grad
    replica_weights = weights_rows - outer_rate * (outer_grad + momentum_decay * momentum_next)
    placed_weights = jnp.einsum("sb,bnd->snd", holding, replica_weights, precision=highest)
    placed_momentum = jnp.einsum("sb,bnd->snd", holding, momentum_next, precision=highest)
    new_weights, new_momentum = (
        lax.all_to_all(placed_weights, "own", split_axis=0, concat_axis=1, tiled=True),
        lax.all_to_all(placed_momentum, "own", split_axis=0, concat_axis=1, tiled=True),
    )
    return (new_weights, new_momentum, replica_weights)


def solution(mesh):
    placed = (
        P("rep", None, "own", None),
        P(),
        P(),
        P(),
        P("own", None, None),
        P("own", None, None),
    )
    return jax.shard_map(
        local,
        mesh=mesh,
        in_specs=placed,
        out_specs=(P("own", None, None), P("own", None, None), P(None, "own", None)),
        check_vma=False,
    )
```

profile of v0, /device:TPU:0, one launch (start us, length us, event | category | flops | bytes accessed | tf_op | source)
XLA Modules:
  0.0 128.1 jit_solution(11364748045961691565)
XLA Ops:
  0.6 0.0 copy-start
  0.6 0.0 copy-start.4
  0.7 2.9 %copy.35 = f32[2,64,1792]{2,0,1:T(2,128)} copy(f32[2,64,1792]{2,1,0:T(8,128)} %param.12) | data formatting | bytes 1835008 | tf_op args[4]
  3.6 7.3 %all-to-all-start = ((f32[2,64,1792]{2,0,1:T(2,128)}), f32[2,64,1792]{2,0,1:T(2,128)S(1)}, u32[]{:S(2)}, u32[]{:S(2)}) async-start(f32[2,64,1792]{2,0,1:T(2,128)} %copy.35), calls=%async_computation | async-start | bytes 1835008 | tf_op jit(solution)/shard_map/all_to_all | solution.py:34
  10.9 2.8 %copy.38 = f32[2,64,1792]{2,0,1:T(2,128)} copy(f32[2,64,1792]{2,1,0:T(8,128)} %param.13) | data formatting | bytes 1835008 | tf_op args[5]
  13.7 20.2 %all-to-all-done = f32[2,64,1792]{2,0,1:T(2,128)S(1)} async-done(((f32[2,64,1792]{2,0,1:T(2,128)}), f32[2,64,1792]{2,0,1:T(2,128)S(1)}, u32[]{:S(2)}, u32[]{:S(2)}) %all-to-all-start) | async-done | bytes 917536 | tf_op jit(solution)/shard_map/all_to_all | solution.py:34
  33.9 4.2 %all-to-all-start.1 = ((f32[2,64,1792]{2,0,1:T(2,128)}), f32[2,64,1792]{2,0,1:T(2,128)}, u32[]{:S(2)}, u32[]{:S(2)}) async-start(f32[2,64,1792]{2,0,1:T(2,128)} %copy.38), calls=%async_computation.1 | async-start | bytes 1835008 | tf_op jit(solution)/shard_map/all_to_all | solution.py:35
  38.2 0.0 copy-done
  38.2 0.0 copy-start.2
  38.2 2.6 %gather_fusion = f32[8,1792,64]{1,2,0:T(8,128)} fusion(f32[4,1792,64]{1,2,0:T(8,128)S(1)} %copy-done, s32[1024]{0:T(1024)S(1)} %pad_clamp_fusion), kind=kCustom, calls=%fused_computation.2 | custom fusion | bytes 7340064 | tf_op jit(solution)/shard_map/jit(_take)/gather | solution.py:29
  40.8 5.4 %fusion.8 = f32[8,8,64]{2,1,0:T(8,128)S(1)} fusion(f32[8,1792,64]{1,2,0:T(8,128)} %gather_fusion, pred[8]{0:T(512)(128)(4,1)S(1)} %compare_and_fusion.1, f32[1,8,8,1792]{3,2,1,0:T(8,128)S(1)} %copy-done.2), kind=kOutput, calls=%fused_computation.11 | convolution fusion | flops 88997888 | bytes 4145160 | tf_op jit(solution)/shard_map/bnd,bdk->bnk/dot_general | solution.py:30
  46.2 10.3 %psum.7 = f32[8,8,64]{2,1,0:T(8,128)S(1)} all-reduce(f32[8,8,64]{2,1,0:T(8,128)S(1)} %fusion.8), channel_id=1, replica_groups=mesh['rep'=4,'own'=8] {'rep'}, use_global_device_ids=true, to_apply=%region_1.0 | all-reduce | flops 4096 | bytes 32768 | tf_op jit(solution)/shard_map/psum | solution.py:31
  56.5 0.0 copy-done.3
  56.5 0.2 convert_reduce_fusion
  56.7 0.1 copy.58
  56.8 0.1 copy.37
  56.9 4.0 %all-to-all-done.1 = f32[2,64,1792]{2,0,1:T(2,128)} async-done(((f32[2,64,1792]{2,0,1:T(2,128)}), f32[2,64,1792]{2,0,1:T(2,128)}, u32[]{:S(2)}, u32[]{:S(2)}) %all-to-all-start.1) | async-done | bytes 917536 | tf_op jit(solution)/shard_map/all_to_all | solution.py:35
  60.9 1.2 copy.57
  62.1 1.0 copy.40
  63.1 0.6 gather_fusion.1
  63.7 1.8 %gather_fusion.2 = f32[8,8,1792]{2,1,0:T(8,128)S(1)} fusion(f32[16,8,1792]{2,1,0:T(8,128)} %bitcast.37, s32[1024]{0:T(1024)S(1)} %pad_clamp_fusion.1), kind=kCustom, calls=%fused_computation.1.clone | custom fusion | bytes 917536 | tf_op jit(solution)/shard_map/jit(_take)/gather | solution.py:38
  65.5 4.8 %fusion.16 = (f32[8,8,1792]{2,1,0:T(8,128)S(1)}, f32[8,8,1792]{2,1,0:T(8,128)}) fusion(f32[8,8,1792]{2,1,0:T(8,128)S(1)} %gather_fusion.2, pred[8]{0:T(512)(128)(4,1)S(1)} %get-tuple-element.4, f32[8,8,1792]{2,1,0:T(8,128)S(1)} %gather_fusion.1, f32[8,1792,64]{1,2,0:T(8,128)} %gather_fusion, pred[8]{0:T(512)(128)(4,1)S(1)} %compare_and_fusion.1, ...), kind=kOutput, calls=%fused_computation.22 | convolution fusion | flops 89919488 | bytes 5521424 | tf_op jit(solution)/shard_map/bnk,bdk->bnd/dot_general | solution.py:32
  70.3 0.6 fusion.12
  70.9 1.5 %copy.45 = f32[16,8,1792]{2,1,0:T(8,128)} copy(f32[16,8,1792]{2,0,1:T(8,128)S(1)} %fusion.12) | data formatting | bytes 1835008 | tf_op jit(solution)/shard_map/sb,bnd->snd/dot_general | solution.py:42
  72.4 3.6 %all-to-all-start.3 = ((f32[16,8,1792]{2,1,0:T(8,128)}), f32[16,8,1792]{2,1,0:T(8,128)S(1)}, u32[]{:S(2)}, u32[]{:S(2)}) async-start(f32[16,8,1792]{2,1,0:T(8,128)} %copy.45), calls=%async_computation.3 | async-start | bytes 1835008 | tf_op jit(solution)/shard_map/all_to_all | solution.py:45
  75.9 0.6 fusion.14
  76.6 1.5 %copy.42 = f32[16,8,1792]{2,1,0:T(8,128)} copy(f32[16,8,1792]{2,0,1:T(8,128)S(1)} %fusion.14) | data formatting | bytes 1835008 | tf_op jit(solution)/shard_map/sb,bnd->snd/dot_general | solution.py:41
  78.1 20.9 %all-to-all-done.3 = f32[16,8,1792]{2,1,0:T(8,128)S(1)} async-done(((f32[16,8,1792]{2,1,0:T(8,128)}), f32[16,8,1792]{2,1,0:T(8,128)S(1)}, u32[]{:S(2)}, u32[]{:S(2)}) %all-to-all-start.3) | async-done | bytes 917536 | tf_op jit(solution)/shard_map/all_to_all | solution.py:45
  98.9 4.2 %all-to-all-start.2 = ((f32[16,8,1792]{2,1,0:T(8,128)}), f32[16,8,1792]{2,1,0:T(8,128)}, u32[]{:S(2)}, u32[]{:S(2)}) async-start(f32[16,8,1792]{2,1,0:T(8,128)} %copy.42), calls=%async_computation.2 | async-start | bytes 1835008 | tf_op jit(solution)/shard_map/all_to_all | solution.py:44
  103.2 1.0 copy.55
  104.2 21.8 %all-to-all-done.2 = f32[16,8,1792]{2,1,0:T(8,128)} async-done(((f32[16,8,1792]{2,1,0:T(8,128)}), f32[16,8,1792]{2,1,0:T(8,128)}, u32[]{:S(2)}, u32[]{:S(2)}) %all-to-all-start.2) | async-done | bytes 917536 | tf_op jit(solution)/shard_map/all_to_all | solution.py:44
  125.9 2.2 %copy.56 = f32[2,8,8,1792]{3,2,1,0:T(8,128)} copy(f32[2,8,8,1792]{3,2,0,1:T(8,128)} %bitcast.10) | data formatting | bytes 1835008 | tf_op jit(solution)/shard_map/all_to_all | solution.py:44
  (11 shorter events, 0.0 us)
Async XLA Ops:
  0.6 37.6 %copy-start = (f32[4,1792,64]{1,2,0:T(8,128)S(1)}, f32[4,1792,64]{1,2,0:T(8,128)}, u32[]{:S(2)}) copy-start(f32[4,1792,64]{1,2,0:T(8,128)} %param.9) | copy-start | bytes 5505028
  0.6 37.5 %copy-start.4 = (s32[8]{0:T(128)S(1)}, s32[8]{0:T(128)}, u32[]{:S(2)}) copy-start(s32[8]{0:T(128)} %param.10) | copy-start | bytes 100
  3.6 30.3 %all-to-all-start = ((f32[2,64,1792]{2,0,1:T(2,128)}), f32[2,64,1792]{2,0,1:T(2,128)S(1)}, u32[]{:S(2)}, u32[]{:S(2)}) async-start(f32[2,64,1792]{2,0,1:T(2,128)} %copy.35), calls=%async_computation | async-start | bytes 1835008 | tf_op jit(solution)/shard_map/all_to_all | solution.py:34
  33.9 27.0 %all-to-all-start.1 = ((f32[2,64,1792]{2,0,1:T(2,128)}), f32[2,64,1792]{2,0,1:T(2,128)}, u32[]{:S(2)}, u32[]{:S(2)}) async-start(f32[2,64,1792]{2,0,1:T(2,128)} %copy.38), calls=%async_computation.1 | async-start | bytes 1835008 | tf_op jit(solution)/shard_map/all_to_all | solution.py:35
  38.2 2.6 %copy-start.2 = (f32[1,8,8,1792]{3,2,1,0:T(8,128)S(1)}, f32[1,8,8,1792]{3,2,1,0:T(8,128)}, u32[]{:S(2)}) copy-start(f32[1,8,8,1792]{3,2,1,0:T(8,128)} %param.8) | copy-start | bytes 1376260
  40.8 15.7 %copy-start.3 = (s32[8]{0:T(128)S(1)}, s32[8]{0:T(128)}, u32[]{:S(2)}) copy-start(s32[8]{0:T(128)} %param.11) | copy-start | bytes 100
  70.3 5.7 %copy-start.1 = (f32[8,8,1792]{2,1,0:T(8,128)S(1)}, f32[8,8,1792]{2,1,0:T(8,128)}, u32[]{:S(2)}) copy-start(f32[8,8,1792]{2,1,0:T(8,128)} %get-tuple-element.7) | copy-start | bytes 1376260
  72.4 26.6 %all-to-all-start.3 = ((f32[16,8,1792]{2,1,0:T(8,128)}), f32[16,8,1792]{2,1,0:T(8,128)S(1)}, u32[]{:S(2)}, u32[]{:S(2)}) async-start(f32[16,8,1792]{2,1,0:T(8,128)} %copy.45), calls=%async_computation.3 | async-start | bytes 1835008 | tf_op jit(solution)/shard_map/all_to_all | solution.py:45
  98.9 27.0 %all-to-all-start.2 = ((f32[16,8,1792]{2,1,0:T(8,128)}), f32[16,8,1792]{2,1,0:T(8,128)}, u32[]{:S(2)}, u32[]{:S(2)}) async-start(f32[16,8,1792]{2,1,0:T(8,128)} %copy.42), calls=%async_computation.2 | async-start | bytes 1835008 | tf_op jit(solution)/shard_map/all_to_all | solution.py:44
where the time goes:
time: 129 us; the launch traced here: 128 us
  waiting for transfers between devices  66.9 us (52%)
  starting transfers between devices  19.3 us (15%)
  local copies, waits for them, and re-layouts  19.1 us (15%)
  matrix products  11.5 us (9%)
  blocking collectives  10.3 us (8%)
    all_to_all x1, waiting for transfers between devices, local(): lax.all_to_all(placed_weights, 'own', split_axis=0, concat_axis=1, tiled=...  21.8 us
    all_to_all x1, waiting for transfers between devices, local(): lax.all_to_all(placed_momentum, 'own', split_axis=0, concat_axis=1, tiled...  20.9 us
    all_to_all x1, waiting for transfers between devices, local(): lax.all_to_all(weights_owned, 'own', split_axis=1, concat_axis=0, tiled=T...  20.2 us
    psum x1, blocking collectives, local(): averaged = lax.psum(coeffs, 'rep') / rep_count  10.3 us
    all_to_all x1, starting transfers between devices, local(): lax.all_to_all(weights_owned, 'own', split_axis=1, concat_axis=0, tiled=T...  7.28 us
    unnamed x12, local copies, waits for them, and re-layouts  5.78 us
    dot_general x1, matrix products, local(): jnp.einsum('bnd,bdk->bnk', replica_delta[0], chosen, precision=highest)  5.38 us
    dot_general x1, matrix products, local(): outer_grad = jnp.einsum('bnk,bdk->bnd', averaged, chosen, precision=highest)  4.79 us
  transfers between devices with their start and end apart: 4, of which 4 were waited for; matrix products, arithmetic and copies ran while one was open for 11% of the time, Pallas kernels for 0%

commit v1 on v0

v1 whole, which is shorter than its diff:
```python
import math

import jax
import jax.numpy as jnp
from jax import lax
from jax.experimental import pallas as pl
from jax.experimental.pallas import tpu as pltpu
from jax.sharding import PartitionSpec as P

momentum_decay = 0.9
outer_rate = 0.7
carried = outer_rate * momentum_decay * momentum_decay
total_rate = outer_rate * (1.0 + momentum_decay)

HIGHEST = lax.Precision.HIGHEST
VMEM = pl.BlockSpec(memory_space=pltpu.VMEM)
SMEM = pl.BlockSpec(memory_space=pltpu.SMEM)


def params(*arrays):
    held = sum(4 * math.prod(array.shape) for array in arrays)
    return pltpu.CompilerParams(vmem_limit_bytes=2 * held + 4 * 1024 * 1024)


def half_index():
    return lax.rem(lax.axis_index("rep"), 2)


def place_of(owner_ref, block):
    owner = owner_ref[block]
    slot = jnp.int32(0)
    for earlier in range(block):
        slot = slot + jnp.where(owner_ref[earlier] == owner, 1, 0)
    return owner, slot


def mixed_kernel(rows, weights_ref, momentum_ref, mixed_ref):
    columns = mixed_ref.shape[-1]
    for half in range(2):

        @pl.when(half_index() == half)
        def _():
            part = pl.ds(half * columns, columns)
            for target in range(mixed_ref.shape[0]):
                here = pl.ds(target * rows, rows)
                mixed_ref[target] = (
                    weights_ref[:, here, part] - carried * momentum_ref[:, here, part]
                )


def project_kernel(owner_ref, layer_ref, delta_ref, basis_ref, coeffs_ref):
    blocks, rows, width = delta_ref.shape
    layers, rank, _ = basis_ref.shape
    products = lax.dot_general(
        delta_ref[...].reshape(blocks * rows, width),
        basis_ref[...].reshape(layers * rank, width),
        (((1,), (1,)), ((), ())),
        precision=HIGHEST,
        preferred_element_type=jnp.float32,
    )
    lane = lax.broadcasted_iota(jnp.int32, (rows, layers * rank), 1)
    coeffs_ref[...] = jnp.zeros_like(coeffs_ref)
    for block in range(blocks):
        owner, slot = place_of(owner_ref, block)
        own = products[block * rows:(block + 1) * rows]
        own = jnp.where(lane // rank == layer_ref[block], own, 0.0)
        folded = own[:, :2 * rank]
        for pair in range(1, layers // 2):
            folded = folded + own[:, 2 * rank * pair:2 * rank * (pair + 1)]
        folded = folded + pltpu.roll(folded, rank, 1)
        placed = jnp.where(lane[:, :2 * rank] // rank == slot, folded, 0.0)
        coeffs_ref[owner] = coeffs_ref[owner] + placed


def spread(pair, slot, layer, layers, rank):
    lane = lax.broadcasted_iota(jnp.int32, pair.shape, 1)
    both = jnp.where(lane // rank == slot, pair, 0.0)
    both = both + pltpu.roll(both, rank, 1)
    wide = jnp.concatenate([both] * (layers // 2), axis=1)
    lane = lax.broadcasted_iota(jnp.int32, wide.shape, 1)
    return jnp.where(lane // rank == layer, wide, 0.0)


def owner_kernel(
    reps, owner_ref, layer_ref, pieces_ref, basis_ref, weights_ref, momentum_ref,
    new_weights_ref, new_momentum_ref, whole_ref,
):
    layers, rank, width = basis_ref.shape
    slots, rows, _ = weights_ref.shape
    far, _, piece_rows, _ = pieces_ref.shape
    me = lax.axis_index("own")
    for step in range(far):
        for side in range(2):
            source = me ^ (2 * step + side)
            whole_ref[pl.ds(source * piece_rows, piece_rows), :] = pieces_ref[step, side]
    basis = basis_ref[...].reshape(layers * rank, width)
    averaged = whole_ref[...] * (1.0 / reps)
    for slot in range(slots):
        used = jnp.int32(0)
        layer = jnp.int32(-1)
        for block in range(owner_ref.shape[0]):
            owner, place = place_of(owner_ref, block)
            here = (owner == me) & (place == slot)
            layer = jnp.where(here, layer_ref[block], layer)
            used = jnp.where(here, 1, used)
        grad = jnp.dot(
            spread(averaged, slot, layer, layers, rank), basis,
            precision=HIGHEST, preferred_element_type=jnp.float32,
        )
        momentum = momentum_decay * momentum_ref[slot] + grad
        weights = weights_ref[slot] - outer_rate * (grad + momentum_decay * momentum)
        new_momentum_ref[slot] = jnp.where(used == 1, momentum, 0.0)
        new_weights_ref[slot] = jnp.where(used == 1, weights, 0.0)


def rows_kernel(
    reps, owner_ref, layer_ref, coeffs_ref, basis_ref, near_ref, other_ref,
    replica_ref, wide_ref, grad_ref,
):
    layers, rank, width = basis_ref.shape
    blocks, rows, _ = replica_ref.shape
    columns = near_ref.shape[-1]
    for block in range(blocks):
        owner, slot = place_of(owner_ref, block)
        wide_ref[pl.ds(block * rows, rows), :] = spread(
            coeffs_ref[owner], slot, layer_ref[block], layers, rank
        )
    basis = basis_ref[...].reshape(layers * rank, width)
    grad_ref[...] = jnp.dot(
        wide_ref[...] * (total_rate / reps), basis,
        precision=HIGHEST, preferred_element_type=jnp.float32,
    )
    for half in range(2):

        @pl.when(half_index() == half)
        def _():
            for block in range(blocks):
                owner, slot = place_of(owner_ref, block)
                for part, mixed_ref in ((half, near_ref), (1 - half, other_ref)):
                    here = pl.ds(part * columns, columns)
                    replica_ref[block, :, here] = (
                        mixed_ref[owner, slot] - grad_ref[pl.ds(block * rows, rows), here]
                    )


def local(replica_delta, layer_basis, layer_of, owner_of, weights_owned, momentum_owned):
    own_count = lax.axis_size("own")
    rep_count = lax.axis_size("rep")
    far = own_count // 2
    slots, owned_rows, width = weights_owned.shape
    blocks, rows = replica_delta.shape[1:3]
    layers, _, rank = layer_basis.shape
    f32 = jnp.float32
    basis = jnp.swapaxes(layer_basis, 1, 2)
    me = lax.axis_index("own")
    side, depth = lax.rem(me, 2), me // 2

    def swap(array, axes, rep_bits, own_bits):
        pairs = []
        for rep in range(rep_count):
            for own in range(own_count):
                source = rep * own_count + own
                pairs.append((source, (rep ^ rep_bits) * own_count + (own ^ own_bits)))
        return lax.ppermute(array, axes, pairs)

    both = ("rep", "own")
    mixed = pl.pallas_call(
        lambda *refs: mixed_kernel(rows, *refs),
        out_shape=jax.ShapeDtypeStruct((own_count, slots, rows, width // 2), f32),
        in_specs=[VMEM, VMEM],
        out_specs=VMEM,
        compiler_params=params(weights_owned, momentum_owned, weights_owned),
        name="mixed",
    )(weights_owned, momentum_owned)
    near = lax.all_to_all(mixed, "own", split_axis=0, concat_axis=0, tiled=True)
    other = swap(near, both, 1, 0)

    coeffs = pl.pallas_call(
        project_kernel,
        out_shape=jax.ShapeDtypeStruct((own_count, rows, slots * rank), f32),
        in_specs=[SMEM, SMEM, VMEM, VMEM],
        out_specs=VMEM,
        compiler_params=params(replica_delta, basis),
        name="project",
    )(owner_of, layer_of, replica_delta[0], basis)
    coeffs = coeffs + swap(coeffs, both, 1, 0)
    halves = coeffs.reshape(far, 2, rows, slots * rank)
    beside = lax.dynamic_index_in_dim(halves, 1 - side, 1, keepdims=False)
    across = swap(coeffs, both, 2, 0)
    arrived = swap(beside, both, 0, 1), swap(beside, both, 2, 1)
    coeffs = coeffs + across
    halves = coeffs.reshape(far, 2, rows, slots * rank)
    mine = lax.dynamic_index_in_dim(halves, side, 1, keepdims=False)
    pieces = jnp.stack([mine, arrived[0] + arrived[1]], axis=1)
    gathered = [lax.dynamic_index_in_dim(pieces, depth, 0, keepdims=False)]
    for step in range(1, far):
        sent = lax.dynamic_index_in_dim(pieces, depth ^ step, 0, keepdims=False)
        gathered.append(swap(sent, both, 0, 2 * step))
    gathered = jnp.stack(gathered)

    new_weights, new_momentum = pl.pallas_call(
        lambda *refs: owner_kernel(rep_count, *refs),
        out_shape=[jax.ShapeDtypeStruct(weights_owned.shape, f32)] * 2,
        in_specs=[SMEM, SMEM, VMEM, VMEM, VMEM, VMEM],
        out_specs=[VMEM, VMEM],
        scratch_shapes=[pltpu.VMEM((owned_rows, slots * rank), f32)],
        compiler_params=params(basis, *[weights_owned] * 4),
        name="owner",
    )(owner_of, layer_of, gathered, basis, weights_owned, momentum_owned)
    replica_weights = pl.pallas_call(
        lambda *refs: rows_kernel(rep_count, *refs),
        out_shape=jax.ShapeDtypeStruct((blocks, rows, width), f32),
        in_specs=[SMEM, SMEM, VMEM, VMEM, VMEM, VMEM],
        out_specs=VMEM,
        scratch_shapes=[
            pltpu.VMEM((blocks * rows, layers * rank), f32),
            pltpu.VMEM((blocks * rows, width), f32),
        ],
        compiler_params=params(basis, near, other, replica_delta),
        name="rows",
    )(owner_of, layer_of, coeffs, basis, near, other)
    return (new_weights, new_momentum, replica_weights)


def solution(mesh):
    placed = (
        P("rep", None, "own", None),
        P(),
        P(),
        P(),
        P("own", None, None),
        P("own", None, None),
    )
    return jax.shard_map(
        local,
        mesh=mesh,
        in_specs=placed,
        out_specs=(P("own", None, None), P("own", None, None), P(None, "own", None)),
        check_vma=False,
    )
```

time: 129 us -> 41.1 us (0.32)
  waiting for transfers between devices: 66.9 us -> 9.87 us
  local copies, waits for them, and re-layouts: 19.1 us -> 5.47 us
  matrix products: 11.5 us -> 0 us
  blocking collectives: 10.3 us -> 0 us
  Pallas kernels: 0 us -> 9.07 us
  starting transfers between devices: 19.3 us -> 15.6 us
    all_to_all x4 -> x1, waiting for transfers between devices: 66.9 us -> 4.68 us  [local(): near = lax.all_to_all(mixed, 'own', split_axis=0, concat_axis=0, tiled=True)]
    all_to_all x4 -> x1, starting transfers between devices: 19.3 us -> 7.41 us  [local(): near = lax.all_to_all(mixed, 'own', split_axis=0, concat_axis=0, tiled=True)]
    dot_general x4 -> x0, matrix products: 11.5 us -> none  [the longest x1 5.38 us: local(): jnp.einsum('bnd,bdk->bnk', replica_delta[0], chosen, precision=highest)]
    psum x1 -> x0, blocking collectives: 10.3 us -> none  [local(): averaged = lax.psum(coeffs, 'rep') / rep_count]
    pallas_call x0 -> x4, Pallas kernels: none -> 9.07 us  [the longest x1 4.09 us: local(): pl.pallas_call(lambda *refs: owner_kernel(rep_count, *refs), out_shape=[j...]
    ppermute x0 -> x8, starting transfers between devices: none -> 8.17 us  [swap(): return lax.ppermute(array, axes, pairs)]
    all_to_all x6 -> x0, local copies, waits for them, and re-layouts: 5.49 us -> none  [the longest x2 2.22 us: local(): lax.all_to_all(momentum_owned, 'own', split_axis=1, concat_axis=0, tiled=...]
    ppermute x0 -> x8, waiting for transfers between devices: none -> 5.19 us  [swap(): return lax.ppermute(array, axes, pairs)]
  transfers between devices with their start and end apart: 4 -> 9, of which waited for: 4 -> 4; matrix products, arithmetic and copies ran while one was open for 11% -> 0% of each run, Pallas kernels for 0% -> 16%
where the time goes in v1:
time: 41.1 us; the launch traced here: 40.8 us
  starting transfers between devices  15.6 us (38%)
  waiting for transfers between devices  9.87 us (24%)
  Pallas kernels  9.07 us (22%)
  local copies, waits for them, and re-layouts  5.47 us (13%)
  between operations  0.77 us (2%)
    ppermute x8, starting transfers between devices, swap(): return lax.ppermute(array, axes, pairs)  8.17 us
    all_to_all x1, starting transfers between devices, local(): near = lax.all_to_all(mixed, 'own', split_axis=0, concat_axis=0, tiled=True)  7.41 us
    unnamed x18, local copies, waits for them, and re-layouts  5.45 us
    ppermute x8, waiting for transfers between devices, swap(): return lax.ppermute(array, axes, pairs)  5.19 us
    all_to_all x1, waiting for transfers between devices, local(): near = lax.all_to_all(mixed, 'own', split_axis=0, concat_axis=0, tiled=True)  4.68 us
    pallas_call x1, Pallas kernels, local(): pl.pallas_call(lambda *refs: owner_kernel(rep_count, *refs), out_shape=[j...  4.09 us
    pallas_call x1, Pallas kernels, local(): pl.pallas_call(lambda *refs: rows_kernel(rep_count, *refs), out_shape=jax...  2.51 us
    pallas_call x1, Pallas kernels, local(): pl.pallas_call(project_kernel, out_shape=jax.ShapeDtypeStruct((own_count,...  2.42 us
  transfers between devices with their start and end apart: 9, of which 4 were waited for; matrix products, arithmetic and copies ran while one was open for 0% of the time, Pallas kernels for 16%

profile of v1, /device:TPU:0, one launch (start us, length us, event | category | flops | bytes accessed | tf_op | source)
XLA Modules:
  0.0 40.8 jit_solution(3586863899986566908)
XLA Ops:
  0.6 0.0 copy-start
  0.6 0.0 copy-start.1
  0.7 1.3 %copy-done.1 = f32[2,64,1792]{2,1,0:T(8,128)S(1)} copy-done((f32[2,64,1792]{2,1,0:T(8,128)S(1)}, f32[2,64,1792]{2,1,0:T(8,128)}, u32[]{:S(2)}) %copy-start.1) | copy-done | bytes 917528
  2.0 1.2 %copy-done.3 = f32[2,64,1792]{2,1,0:T(8,128)S(1)} copy-done((f32[2,64,1792]{2,1,0:T(8,128)S(1)}, f32[2,64,1792]{2,1,0:T(8,128)}, u32[]{:S(2)}) %copy-start.3) | copy-done | bytes 917528
  3.1 0.1 mixed.1
  3.2 0.0 copy-start.5
  3.2 0.8 %copy-done.5 = f32[8,2,8,896]{3,2,1,0:T(8,128)} copy-done((f32[8,2,8,896]{3,2,1,0:T(8,128)}, f32[8,2,8,896]{3,2,1,0:T(8,128)S(1)}, u32[]{:S(2)}) %copy-start.5) | copy-done | bytes 458776
  4.0 7.4 %all-to-all-start = ((f32[8,2,8,896]{3,2,1,0:T(8,128)}), f32[8,2,8,896]{3,2,1,0:T(8,128)S(1)}, u32[]{:S(2)}, u32[]{:S(2)}) async-start(f32[8,2,8,896]{3,2,1,0:T(8,128)} %copy-done.5), calls=%async_computation | async-start | bytes 917504 | tf_op jit(solution)/shard_map/all_to_all | solution.py:175
  11.4 0.0 copy-done
  11.4 0.0 copy-start.6
  11.4 1.0 %copy-done.6 = f32[1,8,8,1792]{3,2,1,0:T(8,128)S(1)} copy-done((f32[1,8,8,1792]{3,2,1,0:T(8,128)S(1)}, f32[1,8,8,1792]{3,2,1,0:T(8,128)}, u32[]{:S(2)}) %copy-start.6) | copy-done | bytes 458776
  12.4 2.4 %project.1 = f32[8,8,128]{2,1,0:T(8,128)S(1)} custom-call(s32[8]{0:T(128)S(1)} %copy-done.7, s32[8]{0:T(128)S(1)} %copy-done.8, f32[8,8,1792]{2,1,0:T(8,128)S(1)} %bitcast.20, f32[4,64,1792]{2,1,0:T(8,128)S(1)} %bitcast.17), custom_call_target="tpu_custom_call" | custom-call | tf_op jit(solution)/shard_map/project/pallas_call | solution.py:178
  14.9 0.1 collective-permute-start
  14.9 1.2 %collective-permute-done = f32[8,8,128]{2,1,0:T(8,128)S(1)} collective-permute-done((f32[8,8,128]{2,1,0:T(8,128)S(1)}, f32[8,8,128]{2,1,0:T(8,128)S(1)}, u32[]{:S(2)}, u32[]{:S(2)}) %collective-permute-start) | collective-permute-done | bytes 32800 | tf_op jit(solution)/shard_map/ppermute | solution.py:164
  16.1 3.0 %collective-permute-start.3 = (f32[4,8,128]{2,1,0:T(8,128)S(1)}, f32[4,8,128]{2,1,0:T(8,128)S(1)}, u32[]{:S(2)}, u32[]{:S(2)}) collective-permute-start(f32[4,8,128]{2,1,0:T(8,128)S(1)} %dynamic-slice_bitcast_fusion), channel_id=1, source_target_pairs={{0,17},{1,16},{2,19},{3,18},{4,21},{5,20},{6,23},{7,22},{8,25},{9,... | collective-permute-start | bytes 49160 | tf_op jit(solution)/shard_map/ppermute | solution.py:164
  19.1 0.0 collective-permute-start.2
  19.2 0.6 %collective-permute-start.1 = (f32[8,8,128]{2,1,0:T(8,128)S(1)}, f32[8,8,128]{2,1,0:T(8,128)S(1)}, u32[]{:S(2)}, u32[]{:S(2)}) collective-permute-start(f32[8,8,128]{2,1,0:T(8,128)S(1)} %add.31), channel_id=1, source_target_pairs={{0,16},{1,17},{2,18},{3,19},{4,20},{5,21},{6,22},{7,23},{8,24},{9,... | collective-permute-start | bytes 98312 | tf_op jit(solution)/shard_map/ppermute | solution.py:164
  19.8 4.7 %all-to-all-done.refs_4_ = f32[8,2,8,896]{3,2,1,0:T(8,128)S(1)} async-done(((f32[8,2,8,896]{3,2,1,0:T(8,128)}), f32[8,2,8,896]{3,2,1,0:T(8,128)S(1)}, u32[]{:S(2)}, u32[]{:S(2)}) %all-to-all-start) | async-done | bytes 458784 | tf_op jit(solution)/shard_map/all_to_all | solution.py:175
  24.5 0.0 collective-permute-start.7
  24.5 0.0 collective-permute-done.3
  24.5 0.0 collective-permute-done.2
  24.5 0.0 collective-permute-done.1
  24.6 0.9 %collective-permute-start.4 = (f32[2,8,128]{2,1,0:T(8,128)S(1)}, f32[2,8,128]{2,1,0:T(8,128)S(1)}, u32[]{:S(2)}, u32[]{:S(2)}) collective-permute-start(f32[2,8,128]{2,1,0:T(8,128)S(1)} %get-tuple-element.8), channel_id=1, source_target_pairs={{0,2},{1,3},{2,0},{3,1},{4,6},{5,7},{6,4},{7,5},{8,10},{9,11},{10,... | collective-permute-start | bytes 24584 | tf_op jit(solution)/shard_map/ppermute | solution.py:164
  25.5 2.1 %collective-permute-start.5 = (f32[2,8,128]{2,1,0:T(8,128)S(1)}, f32[2,8,128]{2,1,0:T(8,128)S(1)}, u32[]{:S(2)}, u32[]{:S(2)}) collective-permute-start(f32[2,8,128]{2,1,0:T(8,128)S(1)} %get-tuple-element.9), channel_id=1, source_target_pairs={{0,4},{1,5},{2,6},{3,7},{4,0},{5,1},{6,2},{7,3},{8,12},{9,13},{10,... | collective-permute-start | bytes 24584 | tf_op jit(solution)/shard_map/ppermute | solution.py:164
  27.6 1.5 %collective-permute-start.6 = (f32[2,8,128]{2,1,0:T(8,128)S(1)}, f32[2,8,128]{2,1,0:T(8,128)S(1)}, u32[]{:S(2)}, u32[]{:S(2)}) collective-permute-start(f32[2,8,128]{2,1,0:T(8,128)S(1)} %get-tuple-element.10), channel_id=1, source_target_pairs={{0,6},{1,7},{2,4},{3,5},{4,2},{5,3},{6,0},{7,1},{8,14},{9,15},{10,... | collective-permute-start | bytes 24584 | tf_op jit(solution)/shard_map/ppermute | solution.py:164
  29.0 0.0 collective-permute-done.4
  29.0 1.0 %collective-permute-done.5 = f32[2,8,128]{2,1,0:T(8,128)S(1)} collective-permute-done((f32[2,8,128]{2,1,0:T(8,128)S(1)}, f32[2,8,128]{2,1,0:T(8,128)S(1)}, u32[]{:S(2)}, u32[]{:S(2)}) %collective-permute-start.5) | collective-permute-done | bytes 8224 | tf_op jit(solution)/shard_map/ppermute | solution.py:164
  30.0 3.0 %collective-permute-done.6 = f32[2,8,128]{2,1,0:T(8,128)S(1)} collective-permute-done((f32[2,8,128]{2,1,0:T(8,128)S(1)}, f32[2,8,128]{2,1,0:T(8,128)S(1)}, u32[]{:S(2)}, u32[]{:S(2)}) %collective-permute-start.6) | collective-permute-done | bytes 8224 | tf_op jit(solution)/shard_map/ppermute | solution.py:164
  33.0 1.2 %copy-done.4 = f32[2,64,1792]{2,1,0:T(8,128)S(1)} copy-done((f32[2,64,1792]{2,1,0:T(8,128)S(1)}, f32[2,64,1792]{2,1,0:T(8,128)}, u32[]{:S(2)}) %copy-start.4) | copy-done | bytes 917528
  34.2 4.1 %owner.1 = (f32[2,64,1792]{2,1,0:T(8,128)}, f32[2,64,1792]{2,1,0:T(8,128)}) custom-call(s32[8]{0:T(128)S(1)} %copy-done.7, s32[8]{0:T(128)S(1)} %copy-done.8, f32[4,2,8,128]{3,2,1,0:T(8,128)S(1)} %pad_maximum_fusion.refs_2_, f32[4,64,1792]{2,1,0:T(8,128)S(1)} %bitcast.18, f32[2,64,1792]{2,1,0:T(8,128)S(1)} %copy-done.2, f32[2,64,1792]{2,1,0:T(8,128)S(1)} %copy-done.4), custom_call_target="tpu_custom_call" | custom-call | tf_op jit(solution)/shard_map/owner/pallas_call | solution.py:201
  38.3 0.0 collective-permute-done.7.refs_5_
  38.3 2.5 %rows.1 = f32[8,8,1792]{2,1,0:T(8,128)} custom-call(s32[8]{0:T(128)S(1)} %copy-done.7, s32[8]{0:T(128)S(1)} %copy-done.8, f32[8,8,128]{2,1,0:T(8,128)S(1)} %add.32.refs_2_, f32[4,64,1792]{2,1,0:T(8,128)S(1)} %bitcast.19, f32[8,2,8,896]{3,2,1,0:T(8,128)S(1)} %all-to-all-done.refs_4_, f32[8,2,8,896]{3,2,1,0:T(8,128)S(1)} %collective-permute-done.7.refs_5_), custom_call_target="tpu_custom_call" | custom-call | tf_op jit(solution)/shard_map/rows/pallas_call | solution.py:210
  (15 shorter events, 0.1 us)
Async XLA Ops:
  0.6 10.8 %copy-start = (f32[4,1792,64]{1,2,0:T(8,128)S(1)}, f32[4,1792,64]{1,2,0:T(8,128)}, u32[]{:S(2)}) copy-start(f32[4,1792,64]{1,2,0:T(8,128)} %param.7) | copy-start | bytes 5505028
  0.6 1.3 %copy-start.1 = (f32[2,64,1792]{2,1,0:T(8,128)S(1)}, f32[2,64,1792]{2,1,0:T(8,128)}, u32[]{:S(2)}) copy-start(f32[2,64,1792]{2,1,0:T(8,128)} %refs_0_.4) | copy-start | bytes 2752516
  2.0 1.2 %copy-start.3 = (f32[2,64,1792]{2,1,0:T(8,128)S(1)}, f32[2,64,1792]{2,1,0:T(8,128)}, u32[]{:S(2)}) copy-start(f32[2,64,1792]{2,1,0:T(8,128)} %refs_1_.4) | copy-start | bytes 2752516
  3.1 8.3 %copy-start.7 = (s32[8]{0:T(128)S(1)}, s32[8]{0:T(128)}, u32[]{:S(2)}) copy-start(s32[8]{0:T(128)} %refs_0_.5) | copy-start | bytes 100
  3.1 8.3 %copy-start.8 = (s32[8]{0:T(128)S(1)}, s32[8]{0:T(128)}, u32[]{:S(2)}) copy-start(s32[8]{0:T(128)} %refs_1_.5) | copy-start | bytes 100
  3.2 0.8 %copy-start.5 = (f32[8,2,8,896]{3,2,1,0:T(8,128)}, f32[8,2,8,896]{3,2,1,0:T(8,128)S(1)}, u32[]{:S(2)}) copy-start(f32[8,2,8,896]{3,2,1,0:T(8,128)S(1)} %mixed.1) | copy-start | bytes 1376260
  4.0 29.0 %copy-start.2 = (f32[2,64,1792]{2,1,0:T(8,128)S(1)}, f32[2,64,1792]{2,1,0:T(8,128)}, u32[]{:S(2)}) copy-start(f32[2,64,1792]{2,1,0:T(8,128)} %refs_0_.4) | copy-start | bytes 2752516
  4.0 20.5 %all-to-all-start = ((f32[8,2,8,896]{3,2,1,0:T(8,128)}), f32[8,2,8,896]{3,2,1,0:T(8,128)S(1)}, u32[]{:S(2)}, u32[]{:S(2)}) async-start(f32[8,2,8,896]{3,2,1,0:T(8,128)} %copy-done.5), calls=%async_computation | async-start | bytes 917504 | tf_op jit(solution)/shard_map/all_to_all | solution.py:175
  11.4 1.0 %copy-start.6 = (f32[1,8,8,1792]{3,2,1,0:T(8,128)S(1)}, f32[1,8,8,1792]{3,2,1,0:T(8,128)}, u32[]{:S(2)}) copy-start(f32[1,8,8,1792]{3,2,1,0:T(8,128)} %param.6) | copy-start | bytes 1376260
  14.9 1.3 %collective-permute-start = (f32[8,8,128]{2,1,0:T(8,128)S(1)}, f32[8,8,128]{2,1,0:T(8,128)S(1)}, u32[]{:S(2)}, u32[]{:S(2)}) collective-permute-start(f32[8,8,128]{2,1,0:T(8,128)S(1)} %project.1), channel_id=1, source_target_pairs={{0,8},{1,9},{2,10},{3,11},{4,12},{5,13},{6,14},{7,15},{8,0},{9,1},... | collective-permute-start | bytes 98312 | tf_op jit(solution)/shard_map/ppermute | solution.py:164
  16.1 8.3 %collective-permute-start.3 = (f32[4,8,128]{2,1,0:T(8,128)S(1)}, f32[4,8,128]{2,1,0:T(8,128)S(1)}, u32[]{:S(2)}, u32[]{:S(2)}) collective-permute-start(f32[4,8,128]{2,1,0:T(8,128)S(1)} %dynamic-slice_bitcast_fusion), channel_id=1, source_target_pairs={{0,17},{1,16},{2,19},{3,18},{4,21},{5,20},{6,23},{7,22},{8,25},{9,... | collective-permute-start | bytes 49160 | tf_op jit(solution)/shard_map/ppermute | solution.py:164
  19.1 5.3 %collective-permute-start.2 = (f32[4,8,128]{2,1,0:T(8,128)S(1)}, f32[4,8,128]{2,1,0:T(8,128)S(1)}, u32[]{:S(2)}, u32[]{:S(2)}) collective-permute-start(f32[4,8,128]{2,1,0:T(8,128)S(1)} %dynamic-slice_bitcast_fusion), channel_id=1, source_target_pairs={{0,1},{1,0},{2,3},{3,2},{4,5},{5,4},{6,7},{7,6},{8,9},{9,8},{10,11... | collective-permute-start | bytes 49160 | tf_op jit(solution)/shard_map/ppermute | solution.py:164
  19.2 5.3 %collective-permute-start.1 = (f32[8,8,128]{2,1,0:T(8,128)S(1)}, f32[8,8,128]{2,1,0:T(8,128)S(1)}, u32[]{:S(2)}, u32[]{:S(2)}) collective-permute-start(f32[8,8,128]{2,1,0:T(8,128)S(1)} %add.31), channel_id=1, source_target_pairs={{0,16},{1,17},{2,18},{3,19},{4,20},{5,21},{6,22},{7,23},{8,24},{9,... | collective-permute-start | bytes 98312 | tf_op jit(solution)/shard_map/ppermute | solution.py:164
  24.5 13.8 %collective-permute-start.7 = (f32[8,2,8,896]{3,2,1,0:T(8,128)S(1)}, f32[8,2,8,896]{3,2,1,0:T(8,128)S(1)}, u32[]{:S(2)}, u32[]{:S(2)}) collective-permute-start(f32[8,2,8,896]{3,2,1,0:T(8,128)S(1)} %all-to-all-done.refs_4_), channel_id=1, source_target_pairs={{0,8},{1,9},{2,10},{3,11},{4,12},{5,13},{6,14},{7,15},{8,0},{9,1},... | collective-permute-start | bytes 1376264 | tf_op jit(solution)/shard_map/ppermute | solution.py:164
  24.6 4.5 %collective-permute-start.4 = (f32[2,8,128]{2,1,0:T(8,128)S(1)}, f32[2,8,128]{2,1,0:T(8,128)S(1)}, u32[]{:S(2)}, u32[]{:S(2)}) collective-permute-start(f32[2,8,128]{2,1,0:T(8,128)S(1)} %get-tuple-element.8), channel_id=1, source_target_pairs={{0,2},{1,3},{2,0},{3,1},{4,6},{5,7},{6,4},{7,5},{8,10},{9,11},{10,... | collective-permute-start | bytes 24584 | tf_op jit(solution)/shard_map/ppermute | solution.py:164
  25.5 4.5 %collective-permute-start.5 = (f32[2,8,128]{2,1,0:T(8,128)S(1)}, f32[2,8,128]{2,1,0:T(8,128)S(1)}, u32[]{:S(2)}, u32[]{:S(2)}) collective-permute-start(f32[2,8,128]{2,1,0:T(8,128)S(1)} %get-tuple-element.9), channel_id=1, source_target_pairs={{0,4},{1,5},{2,6},{3,7},{4,0},{5,1},{6,2},{7,3},{8,12},{9,13},{10,... | collective-permute-start | bytes 24584 | tf_op jit(solution)/shard_map/ppermute | solution.py:164
  27.6 5.4 %collective-permute-start.6 = (f32[2,8,128]{2,1,0:T(8,128)S(1)}, f32[2,8,128]{2,1,0:T(8,128)S(1)}, u32[]{:S(2)}, u32[]{:S(2)}) collective-permute-start(f32[2,8,128]{2,1,0:T(8,128)S(1)} %get-tuple-element.10), channel_id=1, source_target_pairs={{0,6},{1,7},{2,4},{3,5},{4,2},{5,3},{6,0},{7,1},{8,14},{9,15},{10,... | collective-permute-start | bytes 24584 | tf_op jit(solution)/shard_map/ppermute | solution.py:164
  33.0 1.2 %copy-start.4 = (f32[2,64,1792]{2,1,0:T(8,128)S(1)}, f32[2,64,1792]{2,1,0:T(8,128)}, u32[]{:S(2)}) copy-start(f32[2,64,1792]{2,1,0:T(8,128)} %refs_1_.4) | copy-start | bytes 2752516

commit v2 on v0

v2 whole, which is shorter than its diff:
```python
import math

import jax
import jax.numpy as jnp
from jax import lax
from jax.experimental import pallas as pl
from jax.experimental.pallas import tpu as pltpu
from jax.sharding import PartitionSpec as P

momentum_decay = 0.9
outer_rate = 0.7
carried = outer_rate * momentum_decay * momentum_decay
total_rate = outer_rate * (1.0 + momentum_decay)

VMEM = pl.BlockSpec(memory_space=pltpu.VMEM)
SMEM = pl.BlockSpec(memory_space=pltpu.SMEM)
HBM = pl.BlockSpec(memory_space=pltpu.HBM)
ANY = pl.BlockSpec(memory_space=pl.ANY)


def params(*arrays):
    held = sum(4 * math.prod(array.shape) for array in arrays)
    return pltpu.CompilerParams(vmem_limit_bytes=2 * held + 4 * 1024 * 1024)


def position():
    rep = lax.axis_index("rep")
    return lax.rem(rep, 2), rep // 2


def split(array):
    high = array.astype(jnp.bfloat16)
    low = (array - high.astype(jnp.float32)).astype(jnp.bfloat16)
    return high, low


def product(left, right_high, right_low, contract):
    rows = left.shape[0]
    high, low = split(left)

    def dot(a, b):
        return lax.dot_general(
            a, b, (contract, ((), ())), preferred_element_type=jnp.float32
        )

    both = dot(jnp.concatenate([high, low], axis=0), right_high)
    return both[:rows] + (both[rows:] + dot(high, right_low))


def place_of(owner_ref, block):
    owner = owner_ref[block]
    slot = jnp.int32(0)
    for earlier in range(block):
        slot = slot + jnp.where(owner_ref[earlier] == owner, 1, 0)
    return owner, slot


def outset_kernel(
    owner_ref, layer_ref, delta_ref, basis_ref, weights_ref, momentum_ref,
    sent_ref, coeffs_ref,
    owner_smem, layer_smem, delta_vmem, basis_vmem, w_ref, m_ref, made_ref, in_sems, out_sems,
):
    across_count, owners, rows, total = sent_ref.shape
    blocks, _, width = delta_ref.shape
    layers, rank, _ = basis_ref.shape
    columns = width // 2
    core, across = position()
    part = pl.ds(pl.multiple_of(core * columns, 128), columns)
    loads = [
        pltpu.make_async_copy(source, target, in_sems.at[index])
        for index, (source, target) in enumerate((
            (weights_ref.at[across, :, part], w_ref),
            (momentum_ref.at[across, :, part], m_ref),
            (owner_ref, owner_smem),
            (layer_ref, layer_smem),
            (delta_ref, delta_vmem),
            *[(basis_ref.at[layer], basis_vmem.at[layer]) for layer in range(layers)],
        ))
    ]
    for load in loads:
        load.start()
    loads[0].wait()
    loads[1].wait()
    for owner in range(owners):
        here = pl.ds(owner * rows, rows)
        made_ref[owner, :, :columns] = w_ref[here, :] - carried * m_ref[here, :]
    for load in loads[2:]:
        load.wait()
    high, low = split(basis_vmem[...].reshape(layers * rank, width))
    products = product(
        delta_vmem[...].reshape(blocks * rows, width), high, low, ((1,), (1,))
    )
    lane = lax.broadcasted_iota(jnp.int32, (rows, layers * rank), 1)
    coeffs_ref[...] = jnp.zeros_like(coeffs_ref)
    for block in range(blocks):
        owner, slot = place_of(owner_smem, block)
        own = products[block * rows:(block + 1) * rows]
        own = jnp.where(lane // rank == layer_smem[block], own, 0.0)
        folded = own[:, :2 * rank]
        for pair in range(1, layers // 2):
            folded = folded + own[:, 2 * rank * pair:2 * rank * (pair + 1)]
        folded = folded + pltpu.roll(folded, rank, 1)
        placed = jnp.where(lane[:, :2 * rank] // rank == slot, folded, 0.0)
        coeffs_ref[owner] = coeffs_ref[owner] + placed
    made_ref[:, :, columns:] = coeffs_ref[...]
    stores = []
    for target in range(across_count):
        store = pltpu.make_async_copy(made_ref, sent_ref.at[target], out_sems.at[target])
        store.start()
        stores.append(store)
    for store in stores:
        store.wait()


def held_by(me, slot, owner_ref, layer_ref):
    used, layer = jnp.int32(0), jnp.int32(0)
    for block in range(owner_ref.shape[0]):
        owner, place = place_of(owner_ref, block)
        here = (owner == me) & (place == slot)
        layer = jnp.where(here, layer_ref[block], layer)
        used = jnp.where(here, 1, used)
    return used, layer


def prepare_kernel(
    reps, owner_ref, layer_ref, coeffs_ref, basis_ref, momentum_ref,
    grad_ref, high_ref, low_ref, held_ref, wide_ref, basis_vmem, sems, basis_sem,
):
    blocks, rows, width = grad_ref.shape
    layers, rank, _ = basis_ref.shape
    me = lax.axis_index("own")
    loads = []
    for slot in range(momentum_ref.shape[0]):
        load = pltpu.make_async_copy(momentum_ref.at[slot], held_ref.at[slot], sems.at[slot])
        load.start()
        loads.append(load)
    basis_load = pltpu.make_async_copy(basis_ref, basis_vmem, basis_sem)
    basis_load.start()
    lane = lax.broadcasted_iota(jnp.int32, (rows, 2 * rank), 1)
    wide_lane = lax.broadcasted_iota(jnp.int32, (rows, layers * rank), 1)
    for block in range(blocks):
        owner, slot = place_of(owner_ref, block)
        both = jnp.where(lane // rank == slot, coeffs_ref[owner], 0.0)
        both = both + pltpu.roll(both, rank, 1)
        wide = jnp.concatenate([both] * (layers // 2), axis=1)
        wide_ref[pl.ds(block * rows, rows), :] = jnp.where(
            wide_lane // rank == layer_ref[block], wide, 0.0
        )
    basis_load.wait()
    high, low = split(basis_vmem[...].reshape(layers * rank, width))
    grad = product(wide_ref[...] * (total_rate / reps), high, low, ((1,), (0,)))
    grad_ref[...] = grad.reshape(blocks, rows, width)
    for slot in range(momentum_ref.shape[0]):
        _, layer = held_by(me, slot, owner_ref, layer_ref)
        slot_high, slot_low = split(basis_vmem[layer])
        high_ref[slot] = slot_high
        low_ref[slot] = slot_low
    for load in loads:
        load.wait()


def after_kernel(near_ref, grad_ref, same_ref):
    pass


def final_kernel(
    reps, owner_ref, layer_ref, near_ref, far_ref, high_ref, low_ref, momentum_ref, grad_ref,
    weights_ref, new_weights_ref, new_momentum_ref, replica_ref,
    owner_smem, layer_smem, w_ref, m_ref, rows_ref, in_sems, out_sems, rows_sem,
):
    slots, rows, width = weights_ref.shape
    rank = high_ref.shape[1]
    blocks = replica_ref.shape[0]
    columns = width // 2
    me = lax.axis_index("own")
    core, _ = position()
    sources = [(owner_ref, owner_smem), (layer_ref, layer_smem)]
    sources += [(weights_ref.at[slot], w_ref.at[slot]) for slot in range(slots)]
    loads = [
        pltpu.make_async_copy(source, target, in_sems.at[index])
        for index, (source, target) in enumerate(sources)
    ]
    for load in loads:
        load.start()
    summed = (near_ref[0, :, :, columns:] + near_ref[1, :, :, columns:]) + (
        far_ref[0, :, :, columns:] + far_ref[1, :, :, columns:]
    )
    averaged = summed.reshape(rows, slots * rank) * (1.0 / reps)
    loads[0].wait()
    loads[1].wait()
    stores = []
    for slot in range(slots):
        used, _ = held_by(me, slot, owner_smem, layer_smem)
        grad = product(
            averaged[:, slot * rank:(slot + 1) * rank], high_ref[slot], low_ref[slot], ((1,), (0,))
        )
        momentum = momentum_decay * momentum_ref[slot] + grad
        m_ref[slot] = jnp.where(used == 1, momentum, 0.0)
        loads[2 + slot].wait()
        weights = w_ref[slot] - outer_rate * (grad + momentum_decay * momentum)
        w_ref[slot] = jnp.where(used == 1, weights, 0.0)
        for which, (source, target) in enumerate(((m_ref, new_momentum_ref), (w_ref, new_weights_ref))):
            store = pltpu.make_async_copy(source.at[slot], target.at[slot], out_sems.at[slot, which])
            store.start()
            stores.append(store)
    for half in range(2):

        @pl.when(core == half)
        def _():
            for block in range(blocks):
                owner, slot = place_of(owner_smem, block)
                for part, source in ((half, near_ref), (1 - half, far_ref)):
                    here = pl.ds(part * columns, columns)
                    rows_ref[block, :, here] = (
                        source[slot, owner, :, :columns] - grad_ref[block, :, here]
                    )

    store = pltpu.make_async_copy(rows_ref, replica_ref, rows_sem)
    store.start()
    stores.append(store)
    for store in stores:
        store.wait()


def local(replica_delta, layer_basis, layer_of, owner_of, weights_owned, momentum_owned):
    own_count = lax.axis_size("own")
    rep_count = lax.axis_size("rep")
    slots, owned_rows, width = weights_owned.shape
    blocks, rows = replica_delta.shape[1:3]
    layers, _, rank = layer_basis.shape
    f32, bf16 = jnp.float32, jnp.bfloat16
    shape = jax.ShapeDtypeStruct
    across_count = rep_count // 2
    columns = width // 2
    total = columns + slots * rank
    basis = jnp.swapaxes(layer_basis, 1, 2)

    def stay(array):
        return pltpu.with_memory_space_constraint(array, pltpu.HBM)

    weights, momentum = stay(weights_owned), stay(momentum_owned)

    def swap(array, bits):
        pairs = [(rep, rep ^ bits) for rep in range(rep_count)]
        return lax.ppermute(array, "rep", pairs)

    sent, coeffs = pl.pallas_call(
        outset_kernel,
        out_shape=[
            shape((across_count, own_count, rows, total), f32),
            shape((own_count, rows, slots * rank), f32),
        ],
        in_specs=[HBM] * 6,
        out_specs=[HBM, VMEM],
        scratch_shapes=[
            pltpu.SMEM(owner_of.shape, jnp.int32),
            pltpu.SMEM(layer_of.shape, jnp.int32),
            pltpu.VMEM(replica_delta.shape[1:], f32),
            pltpu.VMEM(basis.shape, f32),
            pltpu.VMEM((owned_rows, columns), f32),
            pltpu.VMEM((owned_rows, columns), f32),
            pltpu.VMEM((own_count, rows, total), f32),
            pltpu.SemaphoreType.DMA((5 + layers,)),
            pltpu.SemaphoreType.DMA((across_count,)),
        ],
        compiler_params=params(replica_delta, basis, basis, weights_owned),
        name="outset",
    )(stay(owner_of), stay(layer_of), stay(replica_delta[0]), stay(basis), weights, momentum)
    groups = [
        [(across * 2 + core) * own_count + own for across in range(across_count) for own in range(own_count)]
        for core in range(2)
    ]
    near = lax.all_to_all(
        sent.reshape(across_count * own_count, rows, total),
        ("rep", "own"), split_axis=0, concat_axis=0, axis_index_groups=groups, tiled=True,
    ).reshape(sent.shape)
    coeffs = coeffs + swap(coeffs, 1)
    coeffs = coeffs + swap(coeffs, 2)
    grad, high, low, held = pl.pallas_call(
        lambda *refs: prepare_kernel(rep_count, *refs),
        out_shape=[
            shape((blocks, rows, width), f32),
            shape((slots, rank, width), bf16),
            shape((slots, rank, width), bf16),
            shape(momentum_owned.shape, f32),
        ],
        in_specs=[SMEM, SMEM, VMEM, HBM, HBM],
        out_specs=[VMEM] * 4,
        scratch_shapes=[
            pltpu.VMEM((blocks * rows, layers * rank), f32),
            pltpu.VMEM(basis.shape, f32),
            pltpu.SemaphoreType.DMA((slots,)),
            pltpu.SemaphoreType.DMA(()),
        ],
        compiler_params=params(basis, replica_delta, replica_delta, momentum_owned),
        name="prepare",
    )(owner_of, layer_of, coeffs, stay(basis), momentum)
    near = pl.pallas_call(
        after_kernel,
        out_shape=shape(near.shape, f32),
        in_specs=[ANY, ANY],
        out_specs=ANY,
        input_output_aliases={0: 0},
        compiler_params=params(),
        name="after",
    )(near, grad)
    far = swap(near, 1)
    new_weights, new_momentum, replica_weights = pl.pallas_call(
        lambda *refs: final_kernel(rep_count, *refs),
        out_shape=[
            shape(weights_owned.shape, f32),
            shape(weights_owned.shape, f32),
            shape((blocks, rows, width), f32),
        ],
        in_specs=[HBM, HBM] + [VMEM] * 6 + [HBM],
        out_specs=[HBM] * 3,
        scratch_shapes=[
            pltpu.SMEM(owner_of.shape, jnp.int32),
            pltpu.SMEM(layer_of.shape, jnp.int32),
            pltpu.VMEM(weights_owned.shape, f32),
            pltpu.VMEM(weights_owned.shape, f32),
            pltpu.VMEM((blocks, rows, width), f32),
            pltpu.SemaphoreType.DMA((2 + slots,)),
            pltpu.SemaphoreType.DMA((slots, 2)),
            pltpu.SemaphoreType.DMA(()),
        ],
        compiler_params=params(basis, weights_owned, weights_owned, replica_delta, replica_delta),
        name="final",
    )(stay(owner_of), stay(layer_of), near, far, high, low, held, grad, weights)
    return (new_weights, new_momentum, replica_weights)


def solution(mesh):
    placed = (
        P("rep", None, "own", None),
        P(),
        P(),
        P(),
        P("own", None, None),
        P("own", None, None),
    )
    return jax.shard_map(
        local,
        mesh=mesh,
        in_specs=placed,
        out_specs=(P("own", None, None), P("own", None, None), P(None, "own", None)),
        check_vma=False,
    )
```

time: 129 us -> 32.8 us (0.25)
  waiting for transfers between devices: 66.9 us -> 12.1 us
  local copies, waits for them, and re-layouts: 19.1 us -> 0.01 us
  matrix products: 11.5 us -> 0 us
  blocking collectives: 10.3 us -> 0 us
  Pallas kernels: 0 us -> 9.43 us
  starting transfers between devices: 19.3 us -> 10.3 us
    all_to_all x4 -> x1, waiting for transfers between devices: 66.9 us -> 5.93 us  [local(): lax.all_to_all(sent.reshape(across_count * own_count, rows, total), ('rep...]
    dot_general x4 -> x0, matrix products: 11.5 us -> none  [the longest x1 5.38 us: local(): jnp.einsum('bnd,bdk->bnk', replica_delta[0], chosen, precision=highest)]
    all_to_all x4 -> x1, starting transfers between devices: 19.3 us -> 8.32 us  [local(): lax.all_to_all(sent.reshape(across_count * own_count, rows, total), ('rep...]
    psum x1 -> x0, blocking collectives: 10.3 us -> none  [local(): averaged = lax.psum(coeffs, 'rep') / rep_count]
    pallas_call x0 -> x4, Pallas kernels: none -> 9.43 us  [the longest x1 3.49 us: local(): pl.pallas_call(outset_kernel, out_shape=[shape((across_count, own_count,...]
    ppermute x0 -> x3, waiting for transfers between devices: none -> 6.15 us  [swap(): return lax.ppermute(array, 'rep', pairs)]
    unnamed x12 -> x4, local copies, waits for them, and re-layouts: 5.78 us -> 0.01 us
    all_to_all x6 -> x0, local copies, waits for them, and re-layouts: 5.49 us -> none  [the longest x2 2.22 us: local(): lax.all_to_all(momentum_owned, 'own', split_axis=1, concat_axis=0, tiled=...]
  transfers between devices with their start and end apart: 4 -> 4, of which waited for: 4 -> 4; matrix products, arithmetic and copies ran while one was open for 11% -> 0% of each run, Pallas kernels for 0% -> 10%
where the time goes in v2:
time: 32.8 us; the launch traced here: 32.5 us
  waiting for transfers between devices  12.1 us (37%)
  starting transfers between devices  10.3 us (31%)
  Pallas kernels  9.43 us (29%)
  between operations  0.69 us (2%)
    all_to_all x1, starting transfers between devices, local(): lax.all_to_all(sent.reshape(across_count * own_count, rows, total), ('rep...  8.32 us
    ppermute x3, waiting for transfers between devices, swap(): return lax.ppermute(array, 'rep', pairs)  6.15 us
    all_to_all x1, waiting for transfers between devices, local(): lax.all_to_all(sent.reshape(across_count * own_count, rows, total), ('rep...  5.93 us
    pallas_call x1, Pallas kernels, local(): pl.pallas_call(outset_kernel, out_shape=[shape((across_count, own_count,...  3.49 us
    pallas_call x1, Pallas kernels, local(): pl.pallas_call(lambda *refs: prepare_kernel(rep_count, *refs), out_shape=...  3.09 us
    pallas_call x1, Pallas kernels, local(): pl.pallas_call(lambda *refs: final_kernel(rep_count, *refs), out_shape=[s...  2.85 us
    ppermute x3, starting transfers between devices, swap(): return lax.ppermute(array, 'rep', pairs)  1.94 us
  transfers between devices with their start and end apart: 4, of which 4 were waited for; matrix products, arithmetic and copies ran while one was open for 0% of the time, Pallas kernels for 10%

profile of v2, /device:TPU:0, one launch (start us, length us, event | category | flops | bytes accessed | tf_op | source)
XLA Modules:
  0.0 32.5 jit_solution(4280541709864199025)
XLA Ops:
  0.6 0.0 copy-start
  0.6 0.0 copy-start.1
  0.7 3.5 %outset.1 = (f32[2,8,8,1024]{3,2,1,0:T(8,128)}, f32[8,8,128]{2,1,0:T(8,128)S(1)}) custom-call(s32[8]{0:T(128)} %refs_0_.3, s32[8]{0:T(128)} %refs_1_.3, f32[8,8,1792]{2,1,0:T(8,128)} %bitcast.7, f32[4,64,1792]{2,1,0:T(8,128)} %bitcast.5, f32[2,64,1792]{2,1,0:T(8,128)} %refs_8_.1, f32[2,64,1792]{2,1,0:T(8,128)} %refs_4_.1), custom_call_target="tpu_custom_call" | custom-call | tf_op jit(solution)/shard_map/outset/pallas_call | solution.py:247
  4.1 8.3 %all-to-all-start = ((f32[16,8,1024]{2,1,0:T(8,128)}), f32[16,8,1024]{2,1,0:T(8,128)S(1)}, u32[]{:S(2)}, u32[]{:S(2)}) async-start(f32[16,8,1024]{2,1,0:T(8,128)} %bitcast.2), calls=%async_computation | async-start | bytes 1048576 | tf_op jit(solution)/shard_map/all_to_all | solution.py:273
  12.5 0.1 collective-permute-start
  12.6 1.2 %collective-permute-done = f32[8,8,128]{2,1,0:T(8,128)S(1)} collective-permute-done((f32[8,8,128]{2,1,0:T(8,128)S(1)}, f32[8,8,128]{2,1,0:T(8,128)S(1)}, u32[]{:S(2)}, u32[]{:S(2)}) %collective-permute-start) | collective-permute-done | bytes 32800 | tf_op jit(solution)/shard_map/ppermute | solution.py:245
  13.8 1.9 %collective-permute-start.1 = (f32[8,8,128]{2,1,0:T(8,128)S(1)}, f32[8,8,128]{2,1,0:T(8,128)S(1)}, u32[]{:S(2)}, u32[]{:S(2)}) collective-permute-start(f32[8,8,128]{2,1,0:T(8,128)S(1)} %add.6), channel_id=1, source_target_pairs={{0,16},{8,24},{16,0},{24,8},{1,17},{9,25},{17,1},{25,9},{2,18},{10... | collective-permute-start | bytes 98312 | tf_op jit(solution)/shard_map/ppermute | solution.py:245
  15.6 3.0 %collective-permute-done.1 = f32[8,8,128]{2,1,0:T(8,128)S(1)} collective-permute-done((f32[8,8,128]{2,1,0:T(8,128)S(1)}, f32[8,8,128]{2,1,0:T(8,128)S(1)}, u32[]{:S(2)}, u32[]{:S(2)}) %collective-permute-start.1) | collective-permute-done | bytes 32800 | tf_op jit(solution)/shard_map/ppermute | solution.py:245
  18.7 0.0 copy-done
  18.7 0.0 copy-done.1
  18.7 3.1 %prepare.1 = (f32[8,8,1792]{2,1,0:T(8,128)S(1)}, bf16[2,64,1792]{2,1,0:T(8,128)(2,1)S(1)}, bf16[2,64,1792]{2,1,0:T(8,128)(2,1)S(1)}, f32[2,64,1792]{2,1,0:T(8,128)S(1)}) custom-call(s32[8]{0:T(128)S(1)} %copy-done, s32[8]{0:T(128)S(1)} %copy-done.1, f32[8,8,128]{2,1,0:T(8,128)S(1)} %add.7.refs_2_, f32[4,64,1792]{2,1,0:T(8,128)} %bitcast.6, ...), custom_call_target="tpu_custom_call" | custom-call | tf_op jit(solution)/shard_map/prepare/pallas_call | solution.py:279
  21.8 5.9 %all-to-all-done = f32[16,8,1024]{2,1,0:T(8,128)S(1)} async-done(((f32[16,8,1024]{2,1,0:T(8,128)}), f32[16,8,1024]{2,1,0:T(8,128)S(1)}, u32[]{:S(2)}, u32[]{:S(2)}) %all-to-all-start) | async-done | bytes 524320 | tf_op jit(solution)/shard_map/all_to_all | solution.py:273
  27.7 0.0 collective-permute-start.2
  27.7 1.9 %collective-permute-done.2.refs_3_ = f32[2,8,8,1024]{3,2,1,0:T(8,128)S(1)} collective-permute-done((f32[2,8,8,1024]{3,2,1,0:T(8,128)S(1)}, f32[2,8,8,1024]{3,2,1,0:T(8,128)S(1)}, u32[]{:S(2)}, u32[]{:S(2)}) %collective-permute-start.2) | collective-permute-done | bytes 524320 | tf_op jit(solution)/shard_map/ppermute | solution.py:245
  29.6 2.8 %final.1 = (f32[2,64,1792]{2,1,0:T(8,128)}, f32[2,64,1792]{2,1,0:T(8,128)}, f32[8,8,1792]{2,1,0:T(8,128)}) custom-call(s32[8]{0:T(128)} %refs_0_.3, s32[8]{0:T(128)} %refs_1_.3, f32[2,8,8,1024]{3,2,1,0:T(8,128)S(1)} %after.1.refs_2_, f32[2,8,8,1024]{3,2,1,0:T(8,128)S(1)} %collective-permute-done.2.refs_3_, ...), custom_call_target="tpu_custom_call" | custom-call | tf_op jit(solution)/shard_map/final/pallas_call | solution.py:308
  (3 shorter events, 0.0 us)
Async XLA Ops:
  0.6 18.1 %copy-start = (s32[8]{0:T(128)S(1)}, s32[8]{0:T(128)}, u32[]{:S(2)}) copy-start(s32[8]{0:T(128)} %refs_0_.3) | copy-start | bytes 100
  0.6 18.0 %copy-start.1 = (s32[8]{0:T(128)S(1)}, s32[8]{0:T(128)}, u32[]{:S(2)}) copy-start(s32[8]{0:T(128)} %refs_1_.3) | copy-start | bytes 100
  4.1 23.6 %all-to-all-start = ((f32[16,8,1024]{2,1,0:T(8,128)}), f32[16,8,1024]{2,1,0:T(8,128)S(1)}, u32[]{:S(2)}, u32[]{:S(2)}) async-start(f32[16,8,1024]{2,1,0:T(8,128)} %bitcast.2), calls=%async_computation | async-start | bytes 1048576 | tf_op jit(solution)/shard_map/all_to_all | solution.py:273
  12.5 1.3 %collective-permute-start = (f32[8,8,128]{2,1,0:T(8,128)S(1)}, f32[8,8,128]{2,1,0:T(8,128)S(1)}, u32[]{:S(2)}, u32[]{:S(2)}) collective-permute-start(f32[8,8,128]{2,1,0:T(8,128)S(1)} %get-tuple-element.10), channel_id=1, source_target_pairs={{0,8},{8,0},{16,24},{24,16},{1,9},{9,1},{17,25},{25,17},{2,10},{10... | collective-permute-start | bytes 98312 | tf_op jit(solution)/shard_map/ppermute | solution.py:245
  13.8 4.9 %collective-permute-start.1 = (f32[8,8,128]{2,1,0:T(8,128)S(1)}, f32[8,8,128]{2,1,0:T(8,128)S(1)}, u32[]{:S(2)}, u32[]{:S(2)}) collective-permute-start(f32[8,8,128]{2,1,0:T(8,128)S(1)} %add.6), channel_id=1, source_target_pairs={{0,16},{8,24},{16,0},{24,8},{1,17},{9,25},{17,1},{25,9},{2,18},{10... | collective-permute-start | bytes 98312 | tf_op jit(solution)/shard_map/ppermute | solution.py:245
  27.7 1.9 %collective-permute-start.2 = (f32[2,8,8,1024]{3,2,1,0:T(8,128)S(1)}, f32[2,8,8,1024]{3,2,1,0:T(8,128)S(1)}, u32[]{:S(2)}, u32[]{:S(2)}) collective-permute-start(f32[2,8,8,1024]{3,2,1,0:T(8,128)S(1)} %after.1.refs_2_), channel_id=1, source_target_pairs={{0,8},{8,0},{16,24},{24,16},{1,9},{9,1},{17,25},{25,17},{2,10},{10... | collective-permute-start | bytes 1572872 | tf_op jit(solution)/shard_map/ppermute | solution.py:245

commit v3 on v2

v3 whole, which is shorter than its diff:
```python
import math

import jax
import jax.numpy as jnp
from jax import lax
from jax.experimental import pallas as pl
from jax.experimental.pallas import tpu as pltpu
from jax.sharding import PartitionSpec as P

momentum_decay = 0.9
outer_rate = 0.7
carried = outer_rate * momentum_decay * momentum_decay
total_rate = outer_rate * (1.0 + momentum_decay)

VMEM = pl.BlockSpec(memory_space=pltpu.VMEM)
SMEM = pl.BlockSpec(memory_space=pltpu.SMEM)
HBM = pl.BlockSpec(memory_space=pltpu.HBM)
ANY = pl.BlockSpec(memory_space=pl.ANY)


def params(*arrays):
    held = sum(4 * math.prod(array.shape) for array in arrays)
    return pltpu.CompilerParams(vmem_limit_bytes=2 * held + 4 * 1024 * 1024)


def position():
    rep = lax.axis_index("rep")
    return lax.rem(rep, 2), rep // 2


def split(array):
    high = array.astype(jnp.bfloat16)
    low = (array - high.astype(jnp.float32)).astype(jnp.bfloat16)
    return high, low


def product(left, right_high, right_low, contract=((1,), (0,))):
    rows = left.shape[0]
    high, low = split(left)

    def dot(a, b):
        return lax.dot_general(
            a, b, (contract, ((), ())), preferred_element_type=jnp.float32
        )

    both = dot(jnp.concatenate([high, low], axis=0), right_high)
    return both[:rows] + (both[rows:] + dot(high, right_low))


def place_of(owner_ref, block):
    owner = owner_ref[block]
    slot = jnp.int32(0)
    for earlier in range(block):
        slot = slot + jnp.where(owner_ref[earlier] == owner, 1, 0)
    return owner, slot


def outset_kernel(
    owner_ref, layer_ref, delta_ref, basis_ref, weights_ref, momentum_ref,
    sent_ref, coeffs_ref,
    owner_smem, layer_smem, delta_vmem, basis_vmem, w_ref, m_ref, made_ref, in_sems, out_sems,
):
    owners, rows, total = sent_ref.shape
    blocks, _, width = delta_ref.shape
    layers, rank, _ = basis_ref.shape
    slots, _, window = w_ref.shape
    half = width // 2
    core, across = position()
    part = pl.ds(pl.multiple_of(core * half + across * (half - window), 128), window)
    loads = [
        pltpu.make_async_copy(source, target, in_sems.at[index])
        for index, (source, target) in enumerate((
            (weights_ref.at[:, :, part], w_ref),
            (momentum_ref.at[:, :, part], m_ref),
            (owner_ref, owner_smem),
            (layer_ref, layer_smem),
            (delta_ref, delta_vmem),
            *[(basis_ref.at[layer], basis_vmem.at[layer]) for layer in range(layers)],
        ))
    ]
    for load in loads:
        load.start()
    loads[0].wait()
    loads[1].wait()
    for owner in range(owners):
        here = pl.ds(owner * rows, rows)
        for slot in range(slots):
            made_ref[owner, :, slot * window:(slot + 1) * window] = (
                w_ref[slot, here, :] - carried * m_ref[slot, here, :]
            )
    mixed = slots * window
    early = pltpu.make_async_copy(
        made_ref.at[:, :, :mixed], sent_ref.at[:, :, :mixed], out_sems.at[0]
    )
    early.start()
    for load in loads[2:5]:
        load.wait()
    for load in loads[5:]:
        load.wait()
    high, low = split(basis_vmem[...].reshape(layers * rank, width))
    products = product(delta_vmem[...].reshape(blocks * rows, width), high, low, ((1,), (1,)))
    lane = lax.broadcasted_iota(jnp.int32, (rows, 2 * rank), 1)
    coeffs_ref[...] = jnp.zeros_like(coeffs_ref)
    for block in range(blocks):
        owner, slot = place_of(owner_smem, block)
        folded = jnp.zeros((rows, 2 * rank), jnp.float32)
        for pair in range(layers // 2):
            own = products[block * rows:(block + 1) * rows, 2 * rank * pair:2 * rank * (pair + 1)]
            folded = folded + jnp.where(2 * pair + lane // rank == layer_smem[block], own, 0.0)
        folded = folded + pltpu.roll(folded, rank, 1)
        placed = jnp.where(lane // rank == slot, folded, 0.0)
        coeffs_ref[owner] = coeffs_ref[owner] + placed
    made_ref[:, :, mixed:] = coeffs_ref[...]
    late = pltpu.make_async_copy(
        made_ref.at[:, :, mixed:], sent_ref.at[:, :, mixed:], out_sems.at[1]
    )
    late.start()
    early.wait()
    late.wait()


def held_by(me, slot, owner_ref, layer_ref):
    used, layer = jnp.int32(0), jnp.int32(0)
    for block in range(owner_ref.shape[0]):
        owner, place = place_of(owner_ref, block)
        here = (owner == me) & (place == slot)
        layer = jnp.where(here, layer_ref[block], layer)
        used = jnp.where(here, 1, used)
    return used, layer


def prepare_kernel(
    reps, owner_ref, layer_ref, coeffs_ref, basis_ref, momentum_ref,
    grad_ref, high_ref, low_ref, held_ref, wide_ref, basis_vmem, sems, basis_sem,
):
    blocks, rows, width = grad_ref.shape
    layers, rank, _ = basis_ref.shape
    slots = momentum_ref.shape[0]
    me = lax.axis_index("own")
    basis_load = pltpu.make_async_copy(basis_ref, basis_vmem, basis_sem)
    basis_load.start()
    loads = []
    for slot in range(slots):
        load = pltpu.make_async_copy(momentum_ref.at[slot], held_ref.at[slot], sems.at[slot])
        load.start()
        loads.append(load)
    lane = lax.broadcasted_iota(jnp.int32, (rows, 2 * rank), 1)
    wide_lane = lax.broadcasted_iota(jnp.int32, (rows, layers * rank), 1)
    for block in range(blocks):
        owner, slot = place_of(owner_ref, block)
        both = jnp.where(lane // rank == slot, coeffs_ref[owner], 0.0)
        both = both + pltpu.roll(both, rank, 1)
        wide = jnp.concatenate([both] * (layers // 2), axis=1)
        wide_ref[pl.ds(block * rows, rows), :] = jnp.where(
            wide_lane // rank == layer_ref[block], wide, 0.0
        )
    basis_load.wait()
    high, low = split(basis_vmem[...].reshape(layers * rank, width))
    grad = product(wide_ref[...] * (total_rate / reps), high, low)
    grad_ref[...] = grad.reshape(blocks, rows, width)
    for slot in range(slots):
        _, layer = held_by(me, slot, owner_ref, layer_ref)
        slot_high, slot_low = split(basis_vmem[layer])
        high_ref[slot] = slot_high
        low_ref[slot] = slot_low
    for load in loads:
        load.wait()


def select_kernel(owner_ref, near_ref, grad_ref, chosen_ref, partial_ref):
    window = chosen_ref.shape[-1]
    slots = (near_ref.shape[-1] - partial_ref.shape[-1]) // window
    partial_ref[...] = near_ref[:, :, slots * window:]
    for block in range(chosen_ref.shape[0]):
        owner, slot = place_of(owner_ref, block)
        for place in range(slots):

            @pl.when(slot == place)
            def _():
                chosen_ref[block] = near_ref[owner, :, place * window:(place + 1) * window]


def owner_kernel(
    reps, owner_ref, layer_ref, coeffs_ref, high_ref, low_ref, momentum_ref, weights_ref,
    new_weights_ref, new_momentum_ref,
    owner_smem, layer_smem, w_ref, m_ref, change_ref, in_sems, out_sems,
):
    slots, rows, width = weights_ref.shape
    rank = high_ref.shape[1]
    me = lax.axis_index("own")
    sources = [(owner_ref, owner_smem), (layer_ref, layer_smem)]
    sources += [(weights_ref.at[slot], w_ref.at[slot]) for slot in range(slots)]
    loads = [
        pltpu.make_async_copy(source, target, in_sems.at[index])
        for index, (source, target) in enumerate(sources)
    ]
    for load in loads:
        load.start()
    averaged = coeffs_ref[...].reshape(rows, slots * rank) * (1.0 / reps)
    loads[0].wait()
    loads[1].wait()
    stores = []

    def send(source, target, slot, which):
        store = pltpu.make_async_copy(source.at[slot], target.at[slot], out_sems.at[slot, which])
        store.start()
        stores.append(store)

    for slot in range(slots):
        used, _ = held_by(me, slot, owner_smem, layer_smem)
        grad = product(
            averaged[:, slot * rank:(slot + 1) * rank], high_ref[slot], low_ref[slot]
        )
        momentum = momentum_decay * momentum_ref[slot] + grad
        m_ref[slot] = jnp.where(used == 1, momentum, 0.0)
        send(m_ref, new_momentum_ref, slot, 0)
        change_ref[slot] = outer_rate * (grad + momentum_decay * momentum)
    for slot in range(slots):
        used, _ = held_by(me, slot, owner_smem, layer_smem)
        loads[2 + slot].wait()
        w_ref[slot] = jnp.where(used == 1, w_ref[slot] - change_ref[slot], 0.0)
        send(w_ref, new_weights_ref, slot, 1)
    for store in stores:
        store.wait()


def rows_kernel(
    near_ref, near_across_ref, far_ref, far_across_ref, grad_ref, replica_ref, rows_ref, sems
):
    window = near_ref.shape[-1]
    width = grad_ref.shape[-1]
    half = width // 2
    core, across = position()
    for near_core in range(2):
        for near_across in range(2):

            @pl.when((core == near_core) & (across == near_across))
            def _():
                stores = []
                for which, (part, sources) in enumerate((
                    (near_core, (near_ref, near_across_ref)),
                    (1 - near_core, (far_ref, far_across_ref)),
                )):
                    left, right = sources if near_across == 0 else sources[::-1]
                    start, seam, end = part * half, part * half + window, (part + 1) * half
                    rows_ref[:, :, start:seam] = left[...] - grad_ref[:, :, start:seam]
                    rows_ref[:, :, seam:end] = (
                        right[:, :, 2 * window - half:] - grad_ref[:, :, seam:end]
                    )
                    store = pltpu.make_async_copy(
                        rows_ref.at[:, :, start:end], replica_ref.at[:, :, start:end], sems.at[which]
                    )
                    store.start()
                    stores.append(store)
                for store in stores:
                    store.wait()


def local(replica_delta, layer_basis, layer_of, owner_of, weights_owned, momentum_owned):
    own_count = lax.axis_size("own")
    rep_count = lax.axis_size("rep")
    slots, owned_rows, width = weights_owned.shape
    blocks, rows = replica_delta.shape[1:3]
    layers, _, rank = layer_basis.shape
    f32, bf16 = jnp.float32, jnp.bfloat16
    shape = jax.ShapeDtypeStruct
    window = -(-width // 512) * 128
    total = slots * window + slots * rank
    basis = jnp.swapaxes(layer_basis, 1, 2)

    def stay(array):
        return pltpu.with_memory_space_constraint(array, pltpu.HBM)

    weights, momentum = stay(weights_owned), stay(momentum_owned)

    def swap(array, bits):
        pairs = [(rep, rep ^ bits) for rep in range(rep_count)]
        return lax.ppermute(array, "rep", pairs)

    sent, coeffs = pl.pallas_call(
        outset_kernel,
        out_shape=[
            shape((own_count, rows, total), f32),
            shape((own_count, rows, slots * rank), f32),
        ],
        in_specs=[HBM] * 6,
        out_specs=[HBM, VMEM],
        scratch_shapes=[
            pltpu.SMEM(owner_of.shape, jnp.int32),
            pltpu.SMEM(layer_of.shape, jnp.int32),
            pltpu.VMEM(replica_delta.shape[1:], f32),
            pltpu.VMEM(basis.shape, f32),
            pltpu.VMEM((slots, owned_rows, window), f32),
            pltpu.VMEM((slots, owned_rows, window), f32),
            pltpu.VMEM((own_count, rows, total), f32),
            pltpu.SemaphoreType.DMA((5 + layers,)),
            pltpu.SemaphoreType.DMA((2,)),
        ],
        compiler_params=params(replica_delta, basis, basis, weights_owned),
        name="outset",
    )(stay(owner_of), stay(layer_of), stay(replica_delta[0]), stay(basis), weights, momentum)
    near = lax.all_to_all(sent, "own", split_axis=0, concat_axis=0, tiled=True)

    coeffs = coeffs + swap(coeffs, 1)
    coeffs = coeffs + swap(coeffs, 2)
    grad, high, low, held = pl.pallas_call(
        lambda *refs: prepare_kernel(rep_count, *refs),
        out_shape=[
            shape((blocks, rows, width), f32),
            shape((slots, rank, width), bf16),
            shape((slots, rank, width), bf16),
            shape(momentum_owned.shape, f32),
        ],
        in_specs=[SMEM, SMEM, VMEM, HBM, HBM],
        out_specs=[VMEM] * 4,
        scratch_shapes=[
            pltpu.VMEM((blocks * rows, layers * rank), f32),
            pltpu.VMEM(basis.shape, f32),
            pltpu.SemaphoreType.DMA((slots,)),
            pltpu.SemaphoreType.DMA(()),
        ],
        compiler_params=params(basis, replica_delta, replica_delta, momentum_owned),
        name="prepare",
    )(owner_of, layer_of, coeffs, stay(basis), momentum)

    chosen, partial = pl.pallas_call(
        select_kernel,
        out_shape=[
            shape((blocks, rows, window), f32),
            shape((own_count, rows, slots * rank), f32),
        ],
        in_specs=[SMEM, VMEM, ANY],
        out_specs=[VMEM, VMEM],
        compiler_params=params(near, near),
        name="select",
    )(owner_of, near, grad)
    chosen_across = swap(chosen, 2)
    far = swap(chosen, 1)
    partial = (partial + swap(partial, 1)) + (swap(partial, 2) + swap(partial, 3))
    far_across = swap(chosen_across, 1)
    new_weights, new_momentum = pl.pallas_call(
        lambda *refs: owner_kernel(rep_count, *refs),
        out_shape=[shape(weights_owned.shape, f32)] * 2,
        in_specs=[HBM, HBM] + [VMEM] * 4 + [HBM],
        out_specs=[HBM] * 2,
        scratch_shapes=[
            pltpu.SMEM(owner_of.shape, jnp.int32),
            pltpu.SMEM(layer_of.shape, jnp.int32),
            pltpu.VMEM(weights_owned.shape, f32),
            pltpu.VMEM(weights_owned.shape, f32),
            pltpu.VMEM(weights_owned.shape, f32),
            pltpu.SemaphoreType.DMA((2 + slots,)),
            pltpu.SemaphoreType.DMA((slots, 2)),
        ],
        compiler_params=params(basis, weights_owned, weights_owned, weights_owned),
        name="owner",
    )(stay(owner_of), stay(layer_of), partial, high, low, held, weights)
    replica_weights = pl.pallas_call(
        rows_kernel,
        out_shape=shape((blocks, rows, width), f32),
        in_specs=[VMEM] * 5,
        out_specs=HBM,
        scratch_shapes=[pltpu.VMEM((blocks, rows, width), f32), pltpu.SemaphoreType.DMA((2,))],
        compiler_params=params(replica_delta, replica_delta, replica_delta),
        name="rows",
    )(chosen, chosen_across, far, far_across, grad)
    return (new_weights, new_momentum, replica_weights)


def solution(mesh):
    placed = (
        P("rep", None, "own", None),
        P(),
        P(),
        P(),
        P("own", None, None),
        P("own", None, None),
    )
    return jax.shard_map(
        local,
        mesh=mesh,
        in_specs=placed,
        out_specs=(P("own", None, None), P("own", None, None), P(None, "own", None)),
        check_vma=False,
    )
```

time: 32.8 us -> 31.1 us (0.948)
  waiting for transfers between devices: 12.1 us -> 7.52 us
  starting transfers between devices: 10.3 us -> 12.5 us
  Pallas kernels: 9.43 us -> 10 us
    all_to_all x1, waiting for transfers between devices: 5.93 us -> 1.51 us  [local(): near = lax.all_to_all(sent, 'own', split_axis=0, concat_axis=0, tiled=True)]
    ppermute x3 -> x8, starting transfers between devices: 1.94 us -> 5.19 us  [swap(): return lax.ppermute(array, 'rep', pairs)]
    all_to_all x1, starting transfers between devices: 8.32 us -> 7.3 us  [local(): near = lax.all_to_all(sent, 'own', split_axis=0, concat_axis=0, tiled=True)]
    pallas_call x3 -> x4, Pallas kernels: 6.34 us -> 7.07 us  [the longest x1 3.24 us: local(): pl.pallas_call(outset_kernel, out_shape=[shape((own_count, rows, total),...]
    ppermute x3 -> x8, waiting for transfers between devices: 6.15 us -> 6.01 us  [swap(): return lax.ppermute(array, 'rep', pairs)]
  transfers between devices with their start and end apart: 4 -> 9, of which waited for: 4 -> 5; matrix products, arithmetic and copies ran while one was open for 0% -> 0% of each run, Pallas kernels for 10% -> 17%
where the time goes in v3:
time: 31.1 us; the launch traced here: 30.8 us
  starting transfers between devices  12.5 us (40%)
  Pallas kernels  10 us (32%)
  waiting for transfers between devices  7.52 us (24%)
  between operations  0.72 us (2%)
    all_to_all x1, starting transfers between devices, local(): near = lax.all_to_all(sent, 'own', split_axis=0, concat_axis=0, tiled=True)  7.3 us
    ppermute x8, waiting for transfers between devices, swap(): return lax.ppermute(array, 'rep', pairs)  6.01 us
    ppermute x8, starting transfers between devices, swap(): return lax.ppermute(array, 'rep', pairs)  5.19 us
    pallas_call x1, Pallas kernels, local(): pl.pallas_call(outset_kernel, out_shape=[shape((own_count, rows, total),...  3.24 us
    pallas_call x1, Pallas kernels, local(): pl.pallas_call(lambda *refs: prepare_kernel(rep_count, *refs), out_shape=...  2.95 us
    pallas_call x1, Pallas kernels, local(): pl.pallas_call(lambda *refs: owner_kernel(rep_count, *refs), out_shape=[s...  2.34 us
    all_to_all x1, waiting for transfers between devices, local(): near = lax.all_to_all(sent, 'own', split_axis=0, concat_axis=0, tiled=True)  1.51 us
    pallas_call x1, Pallas kernels, local(): pl.pallas_call(rows_kernel, out_shape=shape((blocks, rows, width), f32),...  0.82 us
  transfers between devices with their start and end apart: 9, of which 5 were waited for; matrix products, arithmetic and copies ran while one was open for 0% of the time, Pallas kernels for 17%

profile of v3, /device:TPU:0, one launch (start us, length us, event | category | flops | bytes accessed | tf_op | source)
XLA Modules:
  0.0 30.8 jit_solution(2638441413856945179)
XLA Ops:
  0.6 0.0 copy-start
  0.6 0.0 copy-start.1
  0.7 3.2 %outset.1 = (f32[8,8,1152]{2,1,0:T(8,128)}, f32[8,8,128]{2,1,0:T(8,128)S(1)}) custom-call(s32[8]{0:T(128)} %refs_0_.3, s32[8]{0:T(128)} %refs_1_.3, f32[8,8,1792]{2,1,0:T(8,128)} %bitcast.4, f32[4,64,1792]{2,1,0:T(8,128)} %bitcast.2, f32[2,64,1792]{2,1,0:T(8,128)} %refs_6_.1, f32[2,64,1792]{2,1,0:T(8,128)} %refs_4_.1), custom_call_target="tpu_custom_call" | custom-call | tf_op jit(solution)/shard_map/outset/pallas_call | solution.py:280
  3.9 7.3 %all-to-all-start = ((f32[8,8,1152]{2,1,0:T(8,128)}), f32[8,8,1152]{2,1,0:T(8,128)S(1)}, u32[]{:S(2)}, u32[]{:S(2)}) async-start(f32[8,8,1152]{2,1,0:T(8,128)} %get-tuple-element.13), calls=%async_computation | async-start | bytes 589824 | tf_op jit(solution)/shard_map/all_to_all | solution.py:302
  11.2 0.0 collective-permute-start
  11.2 1.2 %collective-permute-done = f32[8,8,128]{2,1,0:T(8,128)S(1)} collective-permute-done((f32[8,8,128]{2,1,0:T(8,128)S(1)}, f32[8,8,128]{2,1,0:T(8,128)S(1)}, u32[]{:S(2)}, u32[]{:S(2)}) %collective-permute-start) | collective-permute-done | bytes 32800 | tf_op jit(solution)/shard_map/ppermute | solution.py:278
  12.4 1.5 %collective-permute-start.1 = (f32[8,8,128]{2,1,0:T(8,128)S(1)}, f32[8,8,128]{2,1,0:T(8,128)S(1)}, u32[]{:S(2)}, u32[]{:S(2)}) collective-permute-start(f32[8,8,128]{2,1,0:T(8,128)S(1)} %add.15), channel_id=1, source_target_pairs={{0,16},{8,24},{16,0},{24,8},{1,17},{9,25},{17,1},{25,9},{2,18},{10... | collective-permute-start | bytes 98312 | tf_op jit(solution)/shard_map/ppermute | solution.py:278
  13.9 2.4 %collective-permute-done.1 = f32[8,8,128]{2,1,0:T(8,128)S(1)} collective-permute-done((f32[8,8,128]{2,1,0:T(8,128)S(1)}, f32[8,8,128]{2,1,0:T(8,128)S(1)}, u32[]{:S(2)}, u32[]{:S(2)}) %collective-permute-start.1) | collective-permute-done | bytes 32800 | tf_op jit(solution)/shard_map/ppermute | solution.py:278
  16.3 0.0 copy-done
  16.3 0.0 copy-done.1
  16.4 3.0 %prepare.1 = (f32[8,8,1792]{2,1,0:T(8,128)S(1)}, bf16[2,64,1792]{2,1,0:T(8,128)(2,1)S(1)}, bf16[2,64,1792]{2,1,0:T(8,128)(2,1)S(1)}, f32[2,64,1792]{2,1,0:T(8,128)S(1)}) custom-call(s32[8]{0:T(128)S(1)} %copy-done, s32[8]{0:T(128)S(1)} %copy-done.1, f32[8,8,128]{2,1,0:T(8,128)S(1)} %add.16.refs_2_, f32[4,64,1792]{2,1,0:T(8,128)} %bitcast.3, ...), custom_call_target="tpu_custom_call" | custom-call | tf_op jit(solution)/shard_map/prepare/pallas_call | solution.py:306
  19.3 1.5 %all-to-all-done.near_ref = f32[8,8,1152]{2,1,0:T(8,128)S(1)} async-done(((f32[8,8,1152]{2,1,0:T(8,128)}), f32[8,8,1152]{2,1,0:T(8,128)S(1)}, u32[]{:S(2)}, u32[]{:S(2)}) %all-to-all-start) | async-done | bytes 294944 | tf_op jit(solution)/shard_map/all_to_all | solution.py:302
  20.8 0.7 %select.1 = (f32[8,8,512]{2,1,0:T(8,128)S(1)}, f32[8,8,128]{2,1,0:T(8,128)S(1)}) custom-call(s32[8]{0:T(128)S(1)} %copy-done, f32[8,8,1152]{2,1,0:T(8,128)S(1)} %all-to-all-done.near_ref, f32[8,8,1792]{2,1,0:T(8,128)S(1)} %get-tuple-element.15.grad_ref), custom_call_target="tpu_custom_call" | custom-call | tf_op jit(solution)/shard_map/select/pallas_call | solution.py:326
  21.5 1.6 %collective-permute-start.5 = (f32[8,8,512]{2,1,0:T(8,128)S(1)}, f32[8,8,512]{2,1,0:T(8,128)S(1)}, u32[]{:S(2)}, u32[]{:S(2)}) collective-permute-start(f32[8,8,512]{2,1,0:T(8,128)S(1)} %get-tuple-element.22.near_ref), channel_id=1, source_target_pairs={{0,16},{8,24},{16,0},{24,8},{1,17},{9,25},{17,1},{25,9},{2,18},{10... | collective-permute-start | bytes 393224 | tf_op jit(solution)/shard_map/ppermute | solution.py:278
  23.0 0.0 collective-permute-start.2
  23.1 0.5 %collective-permute-start.3 = (f32[8,8,128]{2,1,0:T(8,128)S(1)}, f32[8,8,128]{2,1,0:T(8,128)S(1)}, u32[]{:S(2)}, u32[]{:S(2)}) collective-permute-start(f32[8,8,128]{2,1,0:T(8,128)S(1)} %get-tuple-element.16), channel_id=1, source_target_pairs={{0,16},{8,24},{16,0},{24,8},{1,17},{9,25},{17,1},{25,9},{2,18},{10... | collective-permute-start | bytes 98312 | tf_op jit(solution)/shard_map/ppermute | solution.py:278
  23.6 1.3 %collective-permute-start.4 = (f32[8,8,128]{2,1,0:T(8,128)S(1)}, f32[8,8,128]{2,1,0:T(8,128)S(1)}, u32[]{:S(2)}, u32[]{:S(2)}) collective-permute-start(f32[8,8,128]{2,1,0:T(8,128)S(1)} %get-tuple-element.16), channel_id=1, source_target_pairs={{0,24},{8,16},{16,8},{24,0},{1,25},{9,17},{17,9},{25,1},{2,26},{10... | collective-permute-start | bytes 98312 | tf_op jit(solution)/shard_map/ppermute | solution.py:278
  24.9 0.3 collective-permute-start.6
  25.2 1.7 %collective-permute-done.5.near_across_ref = f32[8,8,512]{2,1,0:T(8,128)S(1)} collective-permute-done((f32[8,8,512]{2,1,0:T(8,128)S(1)}, f32[8,8,512]{2,1,0:T(8,128)S(1)}, u32[]{:S(2)}, u32[]{:S(2)}) %collective-permute-start.5) | collective-permute-done | bytes 131104 | tf_op jit(solution)/shard_map/ppermute | solution.py:278
  26.9 0.0 collective-permute-start.7
  26.9 0.0 collective-permute-done.2
  26.9 0.7 %collective-permute-done.3 = f32[8,8,128]{2,1,0:T(8,128)S(1)} collective-permute-done((f32[8,8,128]{2,1,0:T(8,128)S(1)}, f32[8,8,128]{2,1,0:T(8,128)S(1)}, u32[]{:S(2)}, u32[]{:S(2)}) %collective-permute-start.3) | collective-permute-done | bytes 32800 | tf_op jit(solution)/shard_map/ppermute | solution.py:278
  27.6 0.0 collective-permute-done.4
  27.6 2.3 %owner.1 = (f32[2,64,1792]{2,1,0:T(8,128)}, f32[2,64,1792]{2,1,0:T(8,128)}) custom-call(s32[8]{0:T(128)} %refs_0_.3, s32[8]{0:T(128)} %refs_1_.3, f32[8,8,128]{2,1,0:T(8,128)S(1)} %add_add_fusion.refs_2_, bf16[2,64,1792]{2,1,0:T(8,128)(2,1)S(1)} %get-tuple-element.17.refs_3_, bf16[2,64,1792]{2,1,0:T(8,128)(2,1)S(1)} %get-tuple-element.18.refs_4_, ...), custom_call_target="tpu_custom_call" | custom-call | tf_op jit(solution)/shard_map/owner/pallas_call | solution.py:341
  29.9 0.0 collective-permute-done.6.far_ref
  30.0 0.0 collective-permute-done.7.far_across_ref
  30.0 0.8 %rows.1 = f32[8,8,1792]{2,1,0:T(8,128)} custom-call(f32[8,8,512]{2,1,0:T(8,128)S(1)} %get-tuple-element.22.near_ref, f32[8,8,512]{2,1,0:T(8,128)S(1)} %collective-permute-done.5.near_across_ref, f32[8,8,512]{2,1,0:T(8,128)S(1)} %collective-permute-done.6.far_ref, f32[8,8,512]{2,1,0:T(8,128)S(1)} %collective-permute-done.7.far_across_ref, ...), custom_call_target="tpu_custom_call" | custom-call | tf_op jit(solution)/shard_map/rows/pallas_call | solution.py:358
  (3 shorter events, 0.0 us)
Async XLA Ops:
  0.6 15.7 %copy-start = (s32[8]{0:T(128)S(1)}, s32[8]{0:T(128)}, u32[]{:S(2)}) copy-start(s32[8]{0:T(128)} %refs_0_.3) | copy-start | bytes 100
  0.6 15.7 %copy-start.1 = (s32[8]{0:T(128)S(1)}, s32[8]{0:T(128)}, u32[]{:S(2)}) copy-start(s32[8]{0:T(128)} %refs_1_.3) | copy-start | bytes 100
  3.9 16.9 %all-to-all-start = ((f32[8,8,1152]{2,1,0:T(8,128)}), f32[8,8,1152]{2,1,0:T(8,128)S(1)}, u32[]{:S(2)}, u32[]{:S(2)}) async-start(f32[8,8,1152]{2,1,0:T(8,128)} %get-tuple-element.13), calls=%async_computation | async-start | bytes 589824 | tf_op jit(solution)/shard_map/all_to_all | solution.py:302
  11.2 1.2 %collective-permute-start = (f32[8,8,128]{2,1,0:T(8,128)S(1)}, f32[8,8,128]{2,1,0:T(8,128)S(1)}, u32[]{:S(2)}, u32[]{:S(2)}) collective-permute-start(f32[8,8,128]{2,1,0:T(8,128)S(1)} %get-tuple-element.14), channel_id=1, source_target_pairs={{0,8},{8,0},{16,24},{24,16},{1,9},{9,1},{17,25},{25,17},{2,10},{10... | collective-permute-start | bytes 98312 | tf_op jit(solution)/shard_map/ppermute | solution.py:278
  12.4 3.9 %collective-permute-start.1 = (f32[8,8,128]{2,1,0:T(8,128)S(1)}, f32[8,8,128]{2,1,0:T(8,128)S(1)}, u32[]{:S(2)}, u32[]{:S(2)}) collective-permute-start(f32[8,8,128]{2,1,0:T(8,128)S(1)} %add.15), channel_id=1, source_target_pairs={{0,16},{8,24},{16,0},{24,8},{1,17},{9,25},{17,1},{25,9},{2,18},{10... | collective-permute-start | bytes 98312 | tf_op jit(solution)/shard_map/ppermute | solution.py:278
  21.5 5.4 %collective-permute-start.5 = (f32[8,8,512]{2,1,0:T(8,128)S(1)}, f32[8,8,512]{2,1,0:T(8,128)S(1)}, u32[]{:S(2)}, u32[]{:S(2)}) collective-permute-start(f32[8,8,512]{2,1,0:T(8,128)S(1)} %get-tuple-element.22.near_ref), channel_id=1, source_target_pairs={{0,16},{8,24},{16,0},{24,8},{1,17},{9,25},{17,1},{25,9},{2,18},{10... | collective-permute-start | bytes 393224 | tf_op jit(solution)/shard_map/ppermute | solution.py:278
  23.0 3.9 %collective-permute-start.2 = (f32[8,8,128]{2,1,0:T(8,128)S(1)}, f32[8,8,128]{2,1,0:T(8,128)S(1)}, u32[]{:S(2)}, u32[]{:S(2)}) collective-permute-start(f32[8,8,128]{2,1,0:T(8,128)S(1)} %get-tuple-element.16), channel_id=1, source_target_pairs={{0,8},{8,0},{16,24},{24,16},{1,9},{9,1},{17,25},{25,17},{2,10},{10... | collective-permute-start | bytes 98312 | tf_op jit(solution)/shard_map/ppermute | solution.py:278
  23.1 4.5 %collective-permute-start.3 = (f32[8,8,128]{2,1,0:T(8,128)S(1)}, f32[8,8,128]{2,1,0:T(8,128)S(1)}, u32[]{:S(2)}, u32[]{:S(2)}) collective-permute-start(f32[8,8,128]{2,1,0:T(8,128)S(1)} %get-tuple-element.16), channel_id=1, source_target_pairs={{0,16},{8,24},{16,0},{24,8},{1,17},{9,25},{17,1},{25,9},{2,18},{10... | collective-permute-start | bytes 98312 | tf_op jit(solution)/shard_map/ppermute | solution.py:278
  23.6 4.0 %collective-permute-start.4 = (f32[8,8,128]{2,1,0:T(8,128)S(1)}, f32[8,8,128]{2,1,0:T(8,128)S(1)}, u32[]{:S(2)}, u32[]{:S(2)}) collective-permute-start(f32[8,8,128]{2,1,0:T(8,128)S(1)} %get-tuple-element.16), channel_id=1, source_target_pairs={{0,24},{8,16},{16,8},{24,0},{1,25},{9,17},{17,9},{25,1},{2,26},{10... | collective-permute-start | bytes 98312 | tf_op jit(solution)/shard_map/ppermute | solution.py:278
  24.9 5.0 %collective-permute-start.6 = (f32[8,8,512]{2,1,0:T(8,128)S(1)}, f32[8,8,512]{2,1,0:T(8,128)S(1)}, u32[]{:S(2)}, u32[]{:S(2)}) collective-permute-start(f32[8,8,512]{2,1,0:T(8,128)S(1)} %get-tuple-element.22.near_ref), channel_id=1, source_target_pairs={{0,8},{8,0},{16,24},{24,16},{1,9},{9,1},{17,25},{25,17},{2,10},{10... | collective-permute-start | bytes 393224 | tf_op jit(solution)/shard_map/ppermute | solution.py:278
  26.9 3.1 %collective-permute-start.7 = (f32[8,8,512]{2,1,0:T(8,128)S(1)}, f32[8,8,512]{2,1,0:T(8,128)S(1)}, u32[]{:S(2)}, u32[]{:S(2)}) collective-permute-start(f32[8,8,512]{2,1,0:T(8,128)S(1)} %collective-permute-done.5.near_across_ref), channel_id=1, source_target_pairs={{0,8},{8,0},{16,24},{24,16},{1,9},{9,1},{17,25},{25,17},{2,10},{10... | collective-permute-start | bytes 393224 | tf_op jit(solution)/shard_map/ppermute | solution.py:278

commit v4 on v3

--- a/solution.py
+++ b/solution.py
@@ -58,7 +58,8 @@
 def outset_kernel(
     owner_ref, layer_ref, delta_ref, basis_ref, weights_ref, momentum_ref,
     sent_ref, coeffs_ref,
-    owner_smem, layer_smem, delta_vmem, basis_vmem, w_ref, m_ref, made_ref, in_sems, out_sems,
+    owner_smem, layer_smem, delta_vmem, basis_vmem, high_ref, low_ref, w_ref, m_ref, made_ref,
+    in_sems, out_sems,
 ):
     owners, rows, total = sent_ref.shape
     blocks, _, width = delta_ref.shape
@@ -93,12 +94,15 @@
         made_ref.at[:, :, :mixed], sent_ref.at[:, :, :mixed], out_sems.at[0]
     )
     early.start()
+    for layer in range(layers):
+        loads[5 + layer].wait()
+        here = pl.ds(layer * rank, rank)
+        high_ref[here, :], low_ref[here, :] = split(basis_vmem[layer])
     for load in loads[2:5]:
         load.wait()
-    for load in loads[5:]:
-        load.wait()
-    high, low = split(basis_vmem[...].reshape(layers * rank, width))
-    products = product(delta_vmem[...].reshape(blocks * rows, width), high, low, ((1,), (1,)))
+    products = product(
+        delta_vmem[...].reshape(blocks * rows, width), high_ref[...], low_ref[...], ((1,), (1,))
+    )
     lane = lax.broadcasted_iota(jnp.int32, (rows, 2 * rank), 1)
     coeffs_ref[...] = jnp.zeros_like(coeffs_ref)
     for block in range(blocks):
@@ -131,21 +135,29 @@
 
 def prepare_kernel(
     reps, owner_ref, layer_ref, coeffs_ref, basis_ref, momentum_ref,
-    grad_ref, high_ref, low_ref, held_ref, wide_ref, basis_vmem, sems, basis_sem,
+    grad_ref, high_ref, low_ref, held_ref, marks_ref,
+    wide_ref, basis_vmem, slot_vmem, sems,
 ):
-    blocks, rows, width = grad_ref.shape
-    layers, rank, _ = basis_ref.shape
+    blocks, rows, window = grad_ref.shape
+    layers, rank, width = basis_ref.shape
     slots = momentum_ref.shape[0]
+    places = coeffs_ref.shape[0] * slots
+    half = width // 2
     me = lax.axis_index("own")
-    basis_load = pltpu.make_async_copy(basis_ref, basis_vmem, basis_sem)
-    basis_load.start()
-    loads = []
+    core, across = position()
+    part = pl.ds(pl.multiple_of(core * half + across * (half - window), 128), window)
+    found = [held_by(me, slot, owner_ref, layer_ref) for slot in range(slots)]
+    loads = [pltpu.make_async_copy(basis_ref.at[:, :, part], basis_vmem, sems.at[0])]
     for slot in range(slots):
-        load = pltpu.make_async_copy(momentum_ref.at[slot], held_ref.at[slot], sems.at[slot])
+        loads.append(
+            pltpu.make_async_copy(basis_ref.at[found[slot][1]], slot_vmem.at[slot], sems.at[1 + slot])
+        )
+    loads.append(pltpu.make_async_copy(momentum_ref, held_ref, sems.at[1 + slots]))
+    for load in loads:
         load.start()
-        loads.append(load)
     lane = lax.broadcasted_iota(jnp.int32, (rows, 2 * rank), 1)
     wide_lane = lax.broadcasted_iota(jnp.int32, (rows, layers * rank), 1)
+    place_row = lax.broadcasted_iota(jnp.int32, (places, marks_ref.shape[1]), 0)
     for block in range(blocks):
         owner, slot = place_of(owner_ref, block)
         both = jnp.where(lane // rank == slot, coeffs_ref[owner], 0.0)
@@ -154,40 +166,65 @@
         wide_ref[pl.ds(block * rows, rows), :] = jnp.where(
             wide_lane // rank == layer_ref[block], wide, 0.0
         )
-    basis_load.wait()
-    high, low = split(basis_vmem[...].reshape(layers * rank, width))
+        marks_ref[pl.ds(block * places, places), :] = jnp.where(
+            place_row == owner * slots + slot, 1.0, 0.0
+        )
+    loads[0].wait()
+    high, low = split(basis_vmem[...].reshape(layers * rank, window))
     grad = product(wide_ref[...] * (total_rate / reps), high, low)
-    grad_ref[...] = grad.reshape(blocks, rows, width)
+    grad_ref[...] = grad.reshape(blocks, rows, window)
     for slot in range(slots):
-        _, layer = held_by(me, slot, owner_ref, layer_ref)
-        slot_high, slot_low = split(basis_vmem[layer])
+        loads[1 + slot].wait()
+        slot_high, slot_low = split(slot_vmem[slot])
         high_ref[slot] = slot_high
         low_ref[slot] = slot_low
-    for load in loads:
-        load.wait()
-
-
-def select_kernel(owner_ref, near_ref, grad_ref, chosen_ref, partial_ref):
-    window = chosen_ref.shape[-1]
-    slots = (near_ref.shape[-1] - partial_ref.shape[-1]) // window
-    partial_ref[...] = near_ref[:, :, slots * window:]
-    for block in range(chosen_ref.shape[0]):
-        owner, slot = place_of(owner_ref, block)
-        for place in range(slots):
-
-            @pl.when(slot == place)
-            def _():
-                chosen_ref[block] = near_ref[owner, :, place * window:(place + 1) * window]
-
-
-def owner_kernel(
-    reps, owner_ref, layer_ref, coeffs_ref, high_ref, low_ref, momentum_ref, weights_ref,
-    new_weights_ref, new_momentum_ref,
-    owner_smem, layer_smem, w_ref, m_ref, change_ref, in_sems, out_sems,
+    loads[-1].wait()
+
+
+def select_kernel(near_ref, grad_ref, marks_ref, chosen_ref, given_ref):
+    blocks, rows, window = chosen_ref.shape
+    owners = near_ref.shape[0]
+    slots = near_ref.shape[-1] // window
+    places = owners * slots
+    rest = given_ref.shape[-1]
+    lanes = marks_ref.shape[1]
+    _, across = position()
+
+    def one(block, carry):
+        total = -grad_ref[block]
+        for owner in range(owners):
+            for slot in range(slots):
+                mark = marks_ref[pl.ds(block * places + owner * slots + slot, 1), :]
+                mark = jnp.concatenate([mark] * (window // lanes), axis=1)
+                total = total + mark * near_ref[owner, :, slot * window:(slot + 1) * window]
+        chosen_ref[block] = total
+        return carry
+
+    lax.fori_loop(0, blocks, one, 0, unroll=blocks <= 8)
+    for side in range(2):
+
+        @pl.when(across == side)
+        def _():
+            first = side * (window - rest)
+            given_ref[...] = chosen_ref[:, :, first:first + rest]
+
+
+def after_kernel(rows_ref, done_ref, same_ref):
+    pass
+
+
+def final_kernel(
+    reps, owner_ref, layer_ref, coeffs_ref, high_ref, low_ref, momentum_ref,
+    near_ref, near_rest_ref, far_ref, far_rest_ref, weights_ref,
+    new_weights_ref, new_momentum_ref, replica_ref,
+    owner_smem, layer_smem, w_ref, m_ref, change_ref, in_sems, out_sems, rows_sems,
 ):
     slots, rows, width = weights_ref.shape
     rank = high_ref.shape[1]
+    window, rest = near_ref.shape[-1], near_rest_ref.shape[-1]
+    half = window + rest
     me = lax.axis_index("own")
+    core, across = position()
     sources = [(owner_ref, owner_smem), (layer_ref, layer_smem)]
     sources += [(weights_ref.at[slot], w_ref.at[slot]) for slot in range(slots)]
     loads = [
@@ -196,10 +233,24 @@
     ]
     for load in loads:
         load.start()
+    stores = []
+    for which, (side, whole, other) in enumerate((
+        (core, near_ref, near_rest_ref), (1 - core, far_ref, far_rest_ref),
+    )):
+        for index, (source, first) in enumerate((
+            (whole, side * half + across * rest),
+            (other, side * half + (1 - across) * window),
+        )):
+            here = pl.ds(pl.multiple_of(first, 128), source.shape[-1])
+            store = pltpu.make_async_copy(
+                source, replica_ref.at[:, :, here], rows_sems.at[which, index]
+            )
+            store.start()
+            stores.append(store)
     averaged = coeffs_ref[...].reshape(rows, slots * rank) * (1.0 / reps)
     loads[0].wait()
     loads[1].wait()
-    stores = []
+    used = [held_by(me, slot, owner_smem, layer_smem)[0] for slot in range(slots)]
 
     def send(source, target, slot, which):
         store = pltpu.make_async_copy(source.at[slot], target.at[slot], out_sems.at[slot, which])
@@ -207,53 +258,19 @@
         stores.append(store)
 
     for slot in range(slots):
-        used, _ = held_by(me, slot, owner_smem, layer_smem)
         grad = product(
             averaged[:, slot * rank:(slot + 1) * rank], high_ref[slot], low_ref[slot]
         )
         momentum = momentum_decay * momentum_ref[slot] + grad
-        m_ref[slot] = jnp.where(used == 1, momentum, 0.0)
+        m_ref[slot] = jnp.where(used[slot] == 1, momentum, 0.0)
         send(m_ref, new_momentum_ref, slot, 0)
         change_ref[slot] = outer_rate * (grad + momentum_decay * momentum)
     for slot in range(slots):
-        used, _ = held_by(me, slot, owner_smem, layer_smem)
         loads[2 + slot].wait()
-        w_ref[slot] = jnp.where(used == 1, w_ref[slot] - change_ref[slot], 0.0)
+        w_ref[slot] = jnp.where(used[slot] == 1, w_ref[slot] - change_ref[slot], 0.0)
         send(w_ref, new_weights_ref, slot, 1)
     for store in stores:
         store.wait()
-
-
-def rows_kernel(
-    near_ref, near_across_ref, far_ref, far_across_ref, grad_ref, replica_ref, rows_ref, sems
-):
-    window = near_ref.shape[-1]
-    width = grad_ref.shape[-1]
-    half = width // 2
-    core, across = position()
-    for near_core in range(2):
-        for near_across in range(2):
-
-            @pl.when((core == near_core) & (across == near_across))
-            def _():
-                stores = []
-                for which, (part, sources) in enumerate((
-                    (near_core, (near_ref, near_across_ref)),
-                    (1 - near_core, (far_ref, far_across_ref)),
-                )):
-                    left, right = sources if near_across == 0 else sources[::-1]
-                    start, seam, end = part * half, part * half + window, (part + 1) * half
-                    rows_ref[:, :, start:seam] = left[...] - grad_ref[:, :, start:seam]
-                    rows_ref[:, :, seam:end] = (
-                        right[:, :, 2 * window - half:] - grad_ref[:, :, seam:end]
-                    )
-                    store = pltpu.make_async_copy(
-                        rows_ref.at[:, :, start:end], replica_ref.at[:, :, start:end], sems.at[which]
-                    )
-                    store.start()
-                    stores.append(store)
-                for store in stores:
-                    store.wait()
 
 
 def local(replica_delta, layer_basis, layer_of, owner_of, weights_owned, momentum_owned):
@@ -265,6 +282,7 @@
     f32, bf16 = jnp.float32, jnp.bfloat16
     shape = jax.ShapeDtypeStruct
     window = -(-width // 512) * 128
+    rest = width // 2 - window
     total = slots * window + slots * rank
     basis = jnp.swapaxes(layer_basis, 1, 2)
 
@@ -290,6 +308,8 @@
             pltpu.SMEM(layer_of.shape, jnp.int32),
             pltpu.VMEM(replica_delta.shape[1:], f32),
             pltpu.VMEM(basis.shape, f32),
+            pltpu.VMEM((layers * rank, width), bf16),
+            pltpu.VMEM((layers * rank, width), bf16),
             pltpu.VMEM((slots, owned_rows, window), f32),
             pltpu.VMEM((slots, owned_rows, window), f32),
             pltpu.VMEM((own_count, rows, total), f32),
@@ -303,46 +323,64 @@
 
     coeffs = coeffs + swap(coeffs, 1)
     coeffs = coeffs + swap(coeffs, 2)
-    grad, high, low, held = pl.pallas_call(
+    grad, high, low, held, marks = pl.pallas_call(
         lambda *refs: prepare_kernel(rep_count, *refs),
         out_shape=[
-            shape((blocks, rows, width), f32),
+            shape((blocks, rows, window), f32),
             shape((slots, rank, width), bf16),
             shape((slots, rank, width), bf16),
             shape(momentum_owned.shape, f32),
+            shape((blocks * own_count * slots, 128), f32),
         ],
         in_specs=[SMEM, SMEM, VMEM, HBM, HBM],
-        out_specs=[VMEM] * 4,
+        out_specs=[VMEM] * 5,
         scratch_shapes=[
             pltpu.VMEM((blocks * rows, layers * rank), f32),
-            pltpu.VMEM(basis.shape, f32),
-            pltpu.SemaphoreType.DMA((slots,)),
-            pltpu.SemaphoreType.DMA(()),
+            pltpu.VMEM((layers, rank, window), f32),
+            pltpu.VMEM((slots, rank, width), f32),
+            pltpu.SemaphoreType.DMA((2 + slots,)),
         ],
         compiler_params=params(basis, replica_delta, replica_delta, momentum_owned),
         name="prepare",
     )(owner_of, layer_of, coeffs, stay(basis), momentum)
 
-    chosen, partial = pl.pallas_call(
+    def after(array, done):
+        return pl.pallas_call(
+            after_kernel,
+            out_shape=shape(array.shape, f32),
+            in_specs=[ANY, ANY],
+            out_specs=ANY,
+            input_output_aliases={0: 0},
+            compiler_params=params(),
+            name="after",
+        )(array, done)
+
+    near = after(near, grad)
+    partial = near[:, :, slots * window:]
+    partial = (partial + swap(partial, 1)) + (swap(partial, 2) + swap(partial, 3))
+    chosen, given = pl.pallas_call(
         select_kernel,
         out_shape=[
             shape((blocks, rows, window), f32),
-            shape((own_count, rows, slots * rank), f32),
-        ],
-        in_specs=[SMEM, VMEM, ANY],
-        out_specs=[VMEM, VMEM],
-        compiler_params=params(near, near),
+            shape((blocks, rows, rest), f32),
+        ],
+        in_specs=[VMEM] * 3,
+        out_specs=[VMEM] * 2,
+        compiler_params=params(near, near, marks),
         name="select",
-    )(owner_of, near, grad)
-    chosen_across = swap(chosen, 2)
+    )(near, grad, marks)
     far = swap(chosen, 1)
-    partial = (partial + swap(partial, 1)) + (swap(partial, 2) + swap(partial, 3))
-    far_across = swap(chosen_across, 1)
-    new_weights, new_momentum = pl.pallas_call(
-        lambda *refs: owner_kernel(rep_count, *refs),
-        out_shape=[shape(weights_owned.shape, f32)] * 2,
-        in_specs=[HBM, HBM] + [VMEM] * 4 + [HBM],
-        out_specs=[HBM] * 2,
+    near_rest = swap(given, 2)
+    far_rest = swap(near_rest, 1)
+    new_weights, new_momentum, replica_weights = pl.pallas_call(
+        lambda *refs: final_kernel(rep_count, *refs),
+        out_shape=[
+            shape(weights_owned.shape, f32),
+            shape(weights_owned.shape, f32),
+            shape((blocks, rows, width), f32),
+        ],
+        in_specs=[HBM, HBM] + [VMEM] * 8 + [HBM],
+        out_specs=[HBM] * 3,
         scratch_shapes=[
             pltpu.SMEM(owner_of.shape, jnp.int32),
             pltpu.SMEM(layer_of.shape, jnp.int32),
@@ -351,19 +389,14 @@
             pltpu.VMEM(weights_owned.shape, f32),
             pltpu.SemaphoreType.DMA((2 + slots,)),
             pltpu.SemaphoreType.DMA((slots, 2)),
+            pltpu.SemaphoreType.DMA((2, 2)),
         ],
         compiler_params=params(basis, weights_owned, weights_owned, weights_owned),
-        name="owner",
-    )(stay(owner_of), stay(layer_of), partial, high, low, held, weights)
-    replica_weights = pl.pallas_call(
-        rows_kernel,
-        out_shape=shape((blocks, rows, width), f32),
-        in_specs=[VMEM] * 5,
-        out_specs=HBM,
-        scratch_shapes=[pltpu.VMEM((blocks, rows, width), f32), pltpu.SemaphoreType.DMA((2,))],
-        compiler_params=params(replica_delta, replica_delta, replica_delta),
-        name="rows",
-    )(chosen, chosen_across, far, far_across, grad)
+        name="final",
+    )(
+        stay(owner_of), stay(layer_of), partial, high, low, held,
+        chosen, near_rest, far, far_rest, weights,
+    )
     return (new_weights, new_momentum, replica_weights)
 
 

time: 31.1 us -> 29.7 us (0.955)
  Pallas kernels: 10 us -> 8.13 us
  waiting for transfers between devices: 7.52 us -> 8.06 us
    pallas_call x2, Pallas kernels: 3.16 us -> 2.37 us  [the longest x1 2.37 us: local(): pl.pallas_call(lambda *refs: final_kernel(rep_count, *refs), out_shape=[s...]
    all_to_all x1, waiting for transfers between devices: 1.51 us -> 2.19 us  [local(): near = lax.all_to_all(sent, 'own', split_axis=0, concat_axis=0, tiled=True)]
    pallas_call x1, Pallas kernels: 2.95 us -> 2.27 us  [local(): pl.pallas_call(lambda *refs: prepare_kernel(rep_count, *refs), out_shape=...]
    pallas_call x1, Pallas kernels: 0.66 us -> 0.16 us  [local(): pl.pallas_call(select_kernel, out_shape=[shape((blocks, rows, window), f3...]
  transfers between devices with their start and end apart: 9 -> 9, of which waited for: 5 -> 6; matrix products, arithmetic and copies ran while one was open for 0% -> 0% of each run, Pallas kernels for 17% -> 8%
where the time goes in v4:
time: 29.7 us; the launch traced here: 29.4 us
  starting transfers between devices  12.5 us (42%)
  Pallas kernels  8.13 us (27%)
  waiting for transfers between devices  8.06 us (27%)
  between operations  0.71 us (2%)
    all_to_all x1, starting transfers between devices, local(): near = lax.all_to_all(sent, 'own', split_axis=0, concat_axis=0, tiled=True)  7.29 us
    ppermute x8, waiting for transfers between devices, swap(): return lax.ppermute(array, 'rep', pairs)  5.87 us
    ppermute x8, starting transfers between devices, swap(): return lax.ppermute(array, 'rep', pairs)  5.19 us
    pallas_call x1, Pallas kernels, local(): pl.pallas_call(outset_kernel, out_shape=[shape((own_count, rows, total),...  3.32 us
    pallas_call x1, Pallas kernels, local(): pl.pallas_call(lambda *refs: final_kernel(rep_count, *refs), out_shape=[s...  2.37 us
    pallas_call x1, Pallas kernels, local(): pl.pallas_call(lambda *refs: prepare_kernel(rep_count, *refs), out_shape=...  2.27 us
    all_to_all x1, waiting for transfers between devices, local(): near = lax.all_to_all(sent, 'own', split_axis=0, concat_axis=0, tiled=True)  2.19 us
  transfers between devices with their start and end apart: 9, of which 6 were waited for; matrix products, arithmetic and copies ran while one was open for 0% of the time, Pallas kernels for 8%

profile of v4, /device:TPU:0, one launch (start us, length us, event | category | flops | bytes accessed | tf_op | source)
XLA Modules:
  0.0 29.4 jit_solution(16342351491854278085)
XLA Ops:
  0.6 0.0 copy-start
  0.6 0.0 copy-start.1
  0.7 3.3 %outset.1 = (f32[8,8,1152]{2,1,0:T(8,128)}, f32[8,8,128]{2,1,0:T(8,128)S(1)}) custom-call(s32[8]{0:T(128)} %refs_0_.3, s32[8]{0:T(128)} %refs_1_.3, f32[8,8,1792]{2,1,0:T(8,128)} %bitcast.4, f32[4,64,1792]{2,1,0:T(8,128)} %bitcast.2, f32[2,64,1792]{2,1,0:T(8,128)} %refs_10_.1, f32[2,64,1792]{2,1,0:T(8,128)} %refs_4_.1), custom_call_target="tpu_custom_call" | custom-call | tf_op jit(solution)/shard_map/outset/pallas_call | solution.py:298
  4.0 7.3 %all-to-all-start = ((f32[8,8,1152]{2,1,0:T(8,128)}), f32[8,8,1152]{2,1,0:T(8,128)S(1)}, u32[]{:S(2)}, u32[]{:S(2)}) async-start(f32[8,8,1152]{2,1,0:T(8,128)} %get-tuple-element.12), calls=%async_computation | async-start | bytes 589824 | tf_op jit(solution)/shard_map/all_to_all | solution.py:322
  11.3 0.0 collective-permute-start
  11.3 1.2 %collective-permute-done = f32[8,8,128]{2,1,0:T(8,128)S(1)} collective-permute-done((f32[8,8,128]{2,1,0:T(8,128)S(1)}, f32[8,8,128]{2,1,0:T(8,128)S(1)}, u32[]{:S(2)}, u32[]{:S(2)}) %collective-permute-start) | collective-permute-done | bytes 32800 | tf_op jit(solution)/shard_map/ppermute | solution.py:296
  12.5 1.5 %collective-permute-start.1 = (f32[8,8,128]{2,1,0:T(8,128)S(1)}, f32[8,8,128]{2,1,0:T(8,128)S(1)}, u32[]{:S(2)}, u32[]{:S(2)}) collective-permute-start(f32[8,8,128]{2,1,0:T(8,128)S(1)} %add.15), channel_id=1, source_target_pairs={{0,16},{8,24},{16,0},{24,8},{1,17},{9,25},{17,1},{25,9},{2,18},{10... | collective-permute-start | bytes 98312 | tf_op jit(solution)/shard_map/ppermute | solution.py:296
  14.0 2.4 %collective-permute-done.1 = f32[8,8,128]{2,1,0:T(8,128)S(1)} collective-permute-done((f32[8,8,128]{2,1,0:T(8,128)S(1)}, f32[8,8,128]{2,1,0:T(8,128)S(1)}, u32[]{:S(2)}, u32[]{:S(2)}) %collective-permute-start.1) | collective-permute-done | bytes 32800 | tf_op jit(solution)/shard_map/ppermute | solution.py:296
  16.4 0.0 copy-done
  16.4 0.0 copy-done.1
  16.4 2.3 %prepare.1 = (f32[8,8,512]{2,1,0:T(8,128)S(1)}, bf16[2,64,1792]{2,1,0:T(8,128)(2,1)S(1)}, bf16[2,64,1792]{2,1,0:T(8,128)(2,1)S(1)}, f32[2,64,1792]{2,1,0:T(8,128)S(1)}, f32[128,128]{1,0:T(8,128)S(1)}) custom-call(s32[8]{0:T(128)S(1)} %copy-done, s32[8]{0:T(128)S(1)} %copy-done.1, f32[8,8,128]{2,1,0:T(8,128)S(1)} %add.16.refs_2_, f32[4,64,1792]{2,1,0:T(8,128)} %bitcast.3, ...), custom_call_target="tpu_custom_call" | custom-call | tf_op jit(solution)/shard_map/prepare/pallas_call | solution.py:326
  18.7 2.2 %all-to-all-done.rows_ref = f32[8,8,1152]{2,1,0:T(8,128)S(1)} async-done(((f32[8,8,1152]{2,1,0:T(8,128)}), f32[8,8,1152]{2,1,0:T(8,128)S(1)}, u32[]{:S(2)}, u32[]{:S(2)}) %all-to-all-start) | async-done | bytes 294944 | tf_op jit(solution)/shard_map/all_to_all | solution.py:322
  20.9 0.2 select.1
  21.1 1.6 %collective-permute-start.5 = (f32[8,8,384]{2,1,0:T(8,128)S(1)}, f32[8,8,384]{2,1,0:T(8,128)S(1)}, u32[]{:S(2)}, u32[]{:S(2)}) collective-permute-start(f32[8,8,384]{2,1,0:T(8,128)S(1)} %get-tuple-element.20), channel_id=1, source_target_pairs={{0,16},{8,24},{16,0},{24,8},{1,17},{9,25},{17,1},{25,9},{2,18},{10... | collective-permute-start | bytes 294920 | tf_op jit(solution)/shard_map/ppermute | solution.py:296
  22.6 0.5 %collective-permute-start.3 = (f32[8,8,128]{2,1,0:T(8,128)S(1)}, f32[8,8,128]{2,1,0:T(8,128)S(1)}, u32[]{:S(2)}, u32[]{:S(2)}) collective-permute-start(f32[8,8,128]{2,1,0:T(8,128)S(1)} %slice.4), channel_id=1, source_target_pairs={{0,16},{8,24},{16,0},{24,8},{1,17},{9,25},{17,1},{25,9},{2,18},{10... | collective-permute-start | bytes 98312 | tf_op jit(solution)/shard_map/ppermute | solution.py:296
  23.2 0.0 collective-permute-start.4
  23.2 1.6 %collective-permute-start.2 = (f32[8,8,128]{2,1,0:T(8,128)S(1)}, f32[8,8,128]{2,1,0:T(8,128)S(1)}, u32[]{:S(2)}, u32[]{:S(2)}) collective-permute-start(f32[8,8,128]{2,1,0:T(8,128)S(1)} %slice.4), channel_id=1, source_target_pairs={{0,8},{8,0},{16,24},{24,16},{1,9},{9,1},{17,25},{25,17},{2,10},{10... | collective-permute-start | bytes 98312 | tf_op jit(solution)/shard_map/ppermute | solution.py:296
  24.8 0.0 collective-permute-start.6
  24.8 1.0 %collective-permute-done.5.refs_7_ = f32[8,8,384]{2,1,0:T(8,128)S(1)} collective-permute-done((f32[8,8,384]{2,1,0:T(8,128)S(1)}, f32[8,8,384]{2,1,0:T(8,128)S(1)}, u32[]{:S(2)}, u32[]{:S(2)}) %collective-permute-start.5) | collective-permute-done | bytes 98336 | tf_op jit(solution)/shard_map/ppermute | solution.py:296
  25.7 0.0 collective-permute-start.7
  25.7 1.1 %collective-permute-done.3 = f32[8,8,128]{2,1,0:T(8,128)S(1)} collective-permute-done((f32[8,8,128]{2,1,0:T(8,128)S(1)}, f32[8,8,128]{2,1,0:T(8,128)S(1)}, u32[]{:S(2)}, u32[]{:S(2)}) %collective-permute-start.3) | collective-permute-done | bytes 32800 | tf_op jit(solution)/shard_map/ppermute | solution.py:296
  26.8 0.0 collective-permute-done.4
  26.9 0.0 collective-permute-done.2
  26.9 0.0 collective-permute-done.6.refs_8_
  26.9 0.2 collective-permute-done.7.refs_9_
  27.0 2.4 %final.1 = (f32[2,64,1792]{2,1,0:T(8,128)}, f32[2,64,1792]{2,1,0:T(8,128)}, f32[8,8,1792]{2,1,0:T(8,128)}) custom-call(s32[8]{0:T(128)} %refs_0_.3, s32[8]{0:T(128)} %refs_1_.3, f32[8,8,128]{2,1,0:T(8,128)S(1)} %add_add_fusion.refs_2_, bf16[2,64,1792]{2,1,0:T(8,128)(2,1)S(1)} %get-tuple-element.15.refs_3_, ...), custom_call_target="tpu_custom_call" | custom-call | tf_op jit(solution)/shard_map/final/pallas_call | solution.py:375
  (5 shorter events, 0.0 us)
Async XLA Ops:
  0.6 15.8 %copy-start = (s32[8]{0:T(128)S(1)}, s32[8]{0:T(128)}, u32[]{:S(2)}) copy-start(s32[8]{0:T(128)} %refs_0_.3) | copy-start | bytes 100
  0.6 15.8 %copy-start.1 = (s32[8]{0:T(128)S(1)}, s32[8]{0:T(128)}, u32[]{:S(2)}) copy-start(s32[8]{0:T(128)} %refs_1_.3) | copy-start | bytes 100
  4.0 16.9 %all-to-all-start = ((f32[8,8,1152]{2,1,0:T(8,128)}), f32[8,8,1152]{2,1,0:T(8,128)S(1)}, u32[]{:S(2)}, u32[]{:S(2)}) async-start(f32[8,8,1152]{2,1,0:T(8,128)} %get-tuple-element.12), calls=%async_computation | async-start | bytes 589824 | tf_op jit(solution)/shard_map/all_to_all | solution.py:322
  11.3 1.2 %collective-permute-start = (f32[8,8,128]{2,1,0:T(8,128)S(1)}, f32[8,8,128]{2,1,0:T(8,128)S(1)}, u32[]{:S(2)}, u32[]{:S(2)}) collective-permute-start(f32[8,8,128]{2,1,0:T(8,128)S(1)} %get-tuple-element.13), channel_id=1, source_target_pairs={{0,8},{8,0},{16,24},{24,16},{1,9},{9,1},{17,25},{25,17},{2,10},{10... | collective-permute-start | bytes 98312 | tf_op jit(solution)/shard_map/ppermute | solution.py:296
  12.5 3.9 %collective-permute-start.1 = (f32[8,8,128]{2,1,0:T(8,128)S(1)}, f32[8,8,128]{2,1,0:T(8,128)S(1)}, u32[]{:S(2)}, u32[]{:S(2)}) collective-permute-start(f32[8,8,128]{2,1,0:T(8,128)S(1)} %add.15), channel_id=1, source_target_pairs={{0,16},{8,24},{16,0},{24,8},{1,17},{9,25},{17,1},{25,9},{2,18},{10... | collective-permute-start | bytes 98312 | tf_op jit(solution)/shard_map/ppermute | solution.py:296
  21.1 4.7 %collective-permute-start.5 = (f32[8,8,384]{2,1,0:T(8,128)S(1)}, f32[8,8,384]{2,1,0:T(8,128)S(1)}, u32[]{:S(2)}, u32[]{:S(2)}) collective-permute-start(f32[8,8,384]{2,1,0:T(8,128)S(1)} %get-tuple-element.20), channel_id=1, source_target_pairs={{0,16},{8,24},{16,0},{24,8},{1,17},{9,25},{17,1},{25,9},{2,18},{10... | collective-permute-start | bytes 294920 | tf_op jit(solution)/shard_map/ppermute | solution.py:296
  22.6 4.2 %collective-permute-start.3 = (f32[8,8,128]{2,1,0:T(8,128)S(1)}, f32[8,8,128]{2,1,0:T(8,128)S(1)}, u32[]{:S(2)}, u32[]{:S(2)}) collective-permute-start(f32[8,8,128]{2,1,0:T(8,128)S(1)} %slice.4), channel_id=1, source_target_pairs={{0,16},{8,24},{16,0},{24,8},{1,17},{9,25},{17,1},{25,9},{2,18},{10... | collective-permute-start | bytes 98312 | tf_op jit(solution)/shard_map/ppermute | solution.py:296
  23.2 3.7 %collective-permute-start.4 = (f32[8,8,128]{2,1,0:T(8,128)S(1)}, f32[8,8,128]{2,1,0:T(8,128)S(1)}, u32[]{:S(2)}, u32[]{:S(2)}) collective-permute-start(f32[8,8,128]{2,1,0:T(8,128)S(1)} %slice.4), channel_id=1, source_target_pairs={{0,24},{8,16},{16,8},{24,0},{1,25},{9,17},{17,9},{25,1},{2,26},{10... | collective-permute-start | bytes 98312 | tf_op jit(solution)/shard_map/ppermute | solution.py:296
  23.2 3.7 %collective-permute-start.2 = (f32[8,8,128]{2,1,0:T(8,128)S(1)}, f32[8,8,128]{2,1,0:T(8,128)S(1)}, u32[]{:S(2)}, u32[]{:S(2)}) collective-permute-start(f32[8,8,128]{2,1,0:T(8,128)S(1)} %slice.4), channel_id=1, source_target_pairs={{0,8},{8,0},{16,24},{24,16},{1,9},{9,1},{17,25},{25,17},{2,10},{10... | collective-permute-start | bytes 98312 | tf_op jit(solution)/shard_map/ppermute | solution.py:296
  24.8 2.1 %collective-permute-start.6 = (f32[8,8,512]{2,1,0:T(8,128)S(1)}, f32[8,8,512]{2,1,0:T(8,128)S(1)}, u32[]{:S(2)}, u32[]{:S(2)}) collective-permute-start(f32[8,8,512]{2,1,0:T(8,128)S(1)} %get-tuple-element.19.refs_6_), channel_id=1, source_target_pairs={{0,8},{8,0},{16,24},{24,16},{1,9},{9,1},{17,25},{25,17},{2,10},{10... | collective-permute-start | bytes 393224 | tf_op jit(solution)/shard_map/ppermute | solution.py:296
  25.7 1.3 %collective-permute-start.7 = (f32[8,8,384]{2,1,0:T(8,128)S(1)}, f32[8,8,384]{2,1,0:T(8,128)S(1)}, u32[]{:S(2)}, u32[]{:S(2)}) collective-permute-start(f32[8,8,384]{2,1,0:T(8,128)S(1)} %collective-permute-done.5.refs_7_), channel_id=1, source_target_pairs={{0,8},{8,0},{16,24},{24,16},{1,9},{9,1},{17,25},{25,17},{2,10},{10... | collective-permute-start | bytes 294920 | tf_op jit(solution)/shard_map/ppermute | solution.py:296

commit v5 on v4

v5 whole, which is shorter than its diff:
```python
import math

import jax
import jax.numpy as jnp
from jax import lax
from jax.experimental import pallas as pl
from jax.experimental.pallas import tpu as pltpu
from jax.sharding import PartitionSpec as P

momentum_decay = 0.9
outer_rate = 0.7
carried = outer_rate * momentum_decay * momentum_decay
total_rate = outer_rate * (1.0 + momentum_decay)

VMEM = pl.BlockSpec(memory_space=pltpu.VMEM)
SMEM = pl.BlockSpec(memory_space=pltpu.SMEM)
HBM = pl.BlockSpec(memory_space=pltpu.HBM)
ANY = pl.BlockSpec(memory_space=pl.ANY)


def params(*arrays):
    held = sum(4 * math.prod(array.shape) for array in arrays)
    return pltpu.CompilerParams(vmem_limit_bytes=2 * held + 4 * 1024 * 1024)


def position():
    rep = lax.axis_index("rep")
    return lax.rem(rep, 2), rep // 2


def split(array):
    high = array.astype(jnp.bfloat16)
    low = (array - high.astype(jnp.float32)).astype(jnp.bfloat16)
    return high, low


def product(left, right_high, right_low, contract=((1,), (0,))):
    rows = left.shape[0]
    high, low = split(left)

    def dot(a, b):
        return lax.dot_general(
            a, b, (contract, ((), ())), preferred_element_type=jnp.float32
        )

    both = dot(jnp.concatenate([high, low], axis=0), right_high)
    return both[:rows] + (both[rows:] + dot(high, right_low))


def place_of(owner_ref, block):
    owner = owner_ref[block]
    slot = jnp.int32(0)
    for earlier in range(block):
        slot = slot + jnp.where(owner_ref[earlier] == owner, 1, 0)
    return owner, slot


def outset_kernel(
    owner_ref, layer_ref, delta_ref, basis_ref, weights_ref, momentum_ref,
    sent_ref, coeffs_ref,
    owner_smem, layer_smem, delta_vmem, basis_vmem, w_ref, m_ref, made_ref, in_sems, out_sems,
):
    owners, rows, total = sent_ref.shape
    blocks, _, width = delta_ref.shape
    layers, rank, _ = basis_ref.shape
    columns = width // 2
    core, across = position()
    part = pl.ds(pl.multiple_of(core * columns, 128), columns)
    loads = [
        pltpu.make_async_copy(source, target, in_sems.at[index])
        for index, (source, target) in enumerate((
            (owner_ref, owner_smem),
            (layer_ref, layer_smem),
            (delta_ref, delta_vmem),
            *[(basis_ref.at[layer], basis_vmem.at[layer]) for layer in range(layers)],
            (weights_ref.at[:, :, part], w_ref),
            (momentum_ref.at[:, :, part], m_ref),
        ))
    ]
    for load in loads:
        load.start()
    for load in loads[2:-2]:
        load.wait()
    high, low = split(basis_vmem[...].reshape(layers * rank, width))
    products = product(delta_vmem[...].reshape(blocks * rows, width), high, low, ((1,), (1,)))
    loads[-2].wait()
    loads[-1].wait()
    upper = lax.broadcasted_iota(jnp.int32, (rows, columns), 0) < rows // 2
    for owner in range(owners):
        here = pl.ds(owner * rows, rows)
        first, second = [
            w_ref[slot, here, :] - carried * m_ref[slot, here, :] for slot in range(2)
        ]
        for side in range(2):

            @pl.when(across == side)
            def _():
                if side == 0:
                    tile = jnp.where(upper, first, pltpu.roll(second, rows // 2, 0))
                else:
                    tile = jnp.where(upper, pltpu.roll(first, rows // 2, 0), second)
                made_ref[owner, :, :columns] = tile
    early = pltpu.make_async_copy(
        made_ref.at[:, :, :columns], sent_ref.at[:, :, :columns], out_sems.at[0]
    )
    early.start()
    loads[0].wait()
    loads[1].wait()
    lane = lax.broadcasted_iota(jnp.int32, (rows, 2 * rank), 1)
    coeffs_ref[...] = jnp.zeros_like(coeffs_ref)
    for block in range(blocks):
        owner, slot = place_of(owner_smem, block)
        folded = jnp.zeros((rows, 2 * rank), jnp.float32)
        for pair in range(layers // 2):
            own = products[block * rows:(block + 1) * rows, 2 * rank * pair:2 * rank * (pair + 1)]
            folded = folded + jnp.where(2 * pair + lane // rank == layer_smem[block], own, 0.0)
        folded = folded + pltpu.roll(folded, rank, 1)
        placed = jnp.where(lane // rank == slot, folded, 0.0)
        coeffs_ref[owner] = coeffs_ref[owner] + placed
    made_ref[:, :, columns:] = coeffs_ref[...]
    late = pltpu.make_async_copy(
        made_ref.at[:, :, columns:], sent_ref.at[:, :, columns:], out_sems.at[1]
    )
    late.start()
    early.wait()
    late.wait()


def held_by(me, slot, owner_ref, layer_ref):
    used, layer = jnp.int32(0), jnp.int32(0)
    for block in range(owner_ref.shape[0]):
        owner, place = place_of(owner_ref, block)
        here = (owner == me) & (place == slot)
        layer = jnp.where(here, layer_ref[block], layer)
        used = jnp.where(here, 1, used)
    return used, layer


def prepare_kernel(
    reps, owner_ref, layer_ref, coeffs_ref, basis_ref, momentum_ref, weights_ref,
    grad_ref, high_ref, low_ref, held_ref, first_ref, marks_ref,
    wide_ref, basis_vmem, slot_vmem, sems,
):
    pairs, rows, columns = grad_ref.shape
    blocks = owner_ref.shape[0]
    layers, rank, width = basis_ref.shape
    slots = momentum_ref.shape[0]
    places = coeffs_ref.shape[0] * slots
    me = lax.axis_index("own")
    core, across = position()
    part = pl.ds(pl.multiple_of(core * columns, 128), columns)
    found = [held_by(me, slot, owner_ref, layer_ref) for slot in range(slots)]
    loads = [pltpu.make_async_copy(basis_ref.at[:, :, part], basis_vmem, sems.at[0])]
    for slot in range(slots):
        loads.append(
            pltpu.make_async_copy(basis_ref.at[found[slot][1]], slot_vmem.at[slot], sems.at[1 + slot])
        )
    loads.append(pltpu.make_async_copy(momentum_ref, held_ref, sems.at[1 + slots]))
    loads.append(pltpu.make_async_copy(weights_ref.at[0], first_ref, sems.at[2 + slots]))
    for load in loads:
        load.start()
    lane = lax.broadcasted_iota(jnp.int32, (rows, 2 * rank), 1)
    wide_lane = lax.broadcasted_iota(jnp.int32, (rows, layers * rank), 1)
    place_row = lax.broadcasted_iota(jnp.int32, (places, marks_ref.shape[1]), 0)
    upper = lax.broadcasted_iota(jnp.int32, (rows, layers * rank), 0) < rows // 2
    for pair in range(pairs):
        parts = []
        for odd in range(2):
            block = 2 * pair + odd
            owner, slot = place_of(owner_ref, block)
            both = jnp.where(lane // rank == slot, coeffs_ref[owner], 0.0)
            both = both + pltpu.roll(both, rank, 1)
            wide = jnp.concatenate([both] * (layers // 2), axis=1)
            wide = jnp.where(wide_lane // rank == layer_ref[block], wide, 0.0)
            parts.append(jnp.where(across == odd, wide, pltpu.roll(wide, rows // 2, 0)))
            marks_ref[pl.ds(block * places, places), :] = jnp.where(
                place_row == owner * slots + slot, 1.0, 0.0
            )
        wide_ref[pl.ds(pair * rows, rows), :] = jnp.where(upper, parts[0], parts[1])
    loads[0].wait()
    high, low = split(basis_vmem[...].reshape(layers * rank, columns))
    grad = product(wide_ref[...] * (total_rate / reps), high, low)
    grad_ref[...] = grad.reshape(pairs, rows, columns)
    for slot in range(slots):
        loads[1 + slot].wait()
        slot_high, slot_low = split(slot_vmem[slot])
        high_ref[slot] = slot_high
        low_ref[slot] = slot_low
    loads[-2].wait()
    loads[-1].wait()


def select_kernel(near_ref, grad_ref, marks_ref, chosen_ref):
    pairs, rows, columns = chosen_ref.shape
    owners = near_ref.shape[0]
    lanes = marks_ref.shape[1]
    upper = lax.broadcasted_iota(jnp.int32, (rows, columns), 0) < rows // 2

    def one(pair, carry):
        parts = []
        for odd in range(2):
            first = (2 * pair + odd) * 2 * owners
            sums = []
            for slot in range(2):
                total = jnp.zeros((rows, columns), jnp.float32)
                for owner in range(owners):
                    mark = marks_ref[pl.ds(first + 2 * owner + slot, 1), :]
                    mark = jnp.concatenate([mark] * (columns // lanes), axis=1)
                    total = total + mark * near_ref[owner, :, :columns]
                sums.append(total)
            parts.append(sums[odd] + pltpu.roll(sums[1 - odd], rows // 2, 0))
        chosen_ref[pair] = jnp.where(upper, parts[0], parts[1]) - grad_ref[pair]
        return carry

    lax.fori_loop(0, pairs, one, 0, unroll=pairs <= 4)


def after_kernel(rows_ref, done_ref, same_ref):
    pass


def final_kernel(
    reps, owner_ref, layer_ref, coeffs_ref, high_ref, low_ref, momentum_ref, first_ref,
    near_ref, near_across_ref, far_ref, far_across_ref, weights_ref,
    new_weights_ref, new_momentum_ref, replica_ref,
    owner_smem, layer_smem, w_ref, m_ref, change_ref, rows_ref, in_sems, out_sems, rows_sem,
):
    slots, rows, width = weights_ref.shape
    rank = high_ref.shape[1]
    pairs, tile, columns = near_ref.shape
    me = lax.axis_index("own")
    core, across = position()
    sources = [(owner_ref, owner_smem), (layer_ref, layer_smem)]
    sources += [(weights_ref.at[slot], w_ref.at[slot]) for slot in range(1, slots)]
    loads = [
        pltpu.make_async_copy(source, target, in_sems.at[index])
        for index, (source, target) in enumerate(sources)
    ]
    for load in loads:
        load.start()
    upper = lax.broadcasted_iota(jnp.int32, (tile, columns), 0) < tile // 2
    for near_core in range(2):
        for near_across in range(2):

            @pl.when((core == near_core) & (across == near_across))
            def _():
                for side, sources in (
                    (near_core, (near_ref, near_across_ref)),
                    (1 - near_core, (far_ref, far_across_ref)),
                ):
                    top, bottom = sources if near_across == 0 else sources[::-1]
                    here = pl.ds(side * columns, columns)
                    for pair in range(pairs):
                        above, below = top[pair], bottom[pair]
                        rows_ref[2 * pair, :, here] = jnp.where(
                            upper, above, pltpu.roll(below, tile // 2, 0)
                        )
                        rows_ref[2 * pair + 1, :, here] = jnp.where(
                            upper, pltpu.roll(above, tile // 2, 0), below
                        )

    store = pltpu.make_async_copy(rows_ref, replica_ref, rows_sem)
    store.start()
    stores = [store]
    averaged = coeffs_ref[...].reshape(rows, slots * rank) * (1.0 / reps)
    loads[0].wait()
    loads[1].wait()
    used = [held_by(me, slot, owner_smem, layer_smem)[0] for slot in range(slots)]

    def send(source, target, slot, which):
        store = pltpu.make_async_copy(source.at[slot], target.at[slot], out_sems.at[slot, which])
        store.start()
        stores.append(store)

    for slot in range(slots):
        grad = product(
            averaged[:, slot * rank:(slot + 1) * rank], high_ref[slot], low_ref[slot]
        )
        momentum = momentum_decay * momentum_ref[slot] + grad
        m_ref[slot] = jnp.where(used[slot] == 1, momentum, 0.0)
        send(m_ref, new_momentum_ref, slot, 0)
        change = outer_rate * (grad + momentum_decay * momentum)
        if slot == 0:
            w_ref[0] = jnp.where(used[0] == 1, first_ref[...] - change, 0.0)
            send(w_ref, new_weights_ref, 0, 1)
        else:
            change_ref[slot] = change
    for slot in range(1, slots):
        loads[1 + slot].wait()
        w_ref[slot] = jnp.where(used[slot] == 1, w_ref[slot] - change_ref[slot], 0.0)
        send(w_ref, new_weights_ref, slot, 1)
    for store in stores:
        store.wait()


def local(replica_delta, layer_basis, layer_of, owner_of, weights_owned, momentum_owned):
    own_count = lax.axis_size("own")
    rep_count = lax.axis_size("rep")
    slots, owned_rows, width = weights_owned.shape
    blocks, rows = replica_delta.shape[1:3]
    layers, _, rank = layer_basis.shape
    f32, bf16 = jnp.float32, jnp.bfloat16
    shape = jax.ShapeDtypeStruct
    columns = width // 2
    total = columns + slots * rank
    basis = jnp.swapaxes(layer_basis, 1, 2)

    def stay(array):
        return pltpu.with_memory_space_constraint(array, pltpu.HBM)

    weights, momentum = stay(weights_owned), stay(momentum_owned)

    def swap(array, bits):
        pairs = [(rep, rep ^ bits) for rep in range(rep_count)]
        return lax.ppermute(array, "rep", pairs)

    sent, coeffs = pl.pallas_call(
        outset_kernel,
        out_shape=[
            shape((own_count, rows, total), f32),
            shape((own_count, rows, slots * rank), f32),
        ],
        in_specs=[HBM] * 6,
        out_specs=[HBM, VMEM],
        scratch_shapes=[
            pltpu.SMEM(owner_of.shape, jnp.int32),
            pltpu.SMEM(layer_of.shape, jnp.int32),
            pltpu.VMEM(replica_delta.shape[1:], f32),
            pltpu.VMEM(basis.shape, f32),
            pltpu.VMEM((slots, owned_rows, columns), f32),
            pltpu.VMEM((slots, owned_rows, columns), f32),
            pltpu.VMEM((own_count, rows, total), f32),
            pltpu.SemaphoreType.DMA((5 + layers,)),
            pltpu.SemaphoreType.DMA((2,)),
        ],
        compiler_params=params(replica_delta, basis, basis, weights_owned),
        name="outset",
    )(stay(owner_of), stay(layer_of), stay(replica_delta[0]), stay(basis), weights, momentum)
    near = lax.all_to_all(sent, "own", split_axis=0, concat_axis=0, tiled=True)

    coeffs = coeffs + swap(coeffs, 1)
    coeffs = coeffs + swap(coeffs, 2)
    grad, high, low, held, first, marks = pl.pallas_call(
        lambda *refs: prepare_kernel(rep_count, *refs),
        out_shape=[
            shape((blocks // 2, rows, columns), f32),
            shape((slots, rank, width), bf16),
            shape((slots, rank, width), bf16),
            shape(momentum_owned.shape, f32),
            shape(weights_owned.shape[1:], f32),
            shape((blocks * own_count * slots, 128), f32),
        ],
        in_specs=[SMEM, SMEM, VMEM, HBM, HBM, HBM],
        out_specs=[VMEM] * 6,
        scratch_shapes=[
            pltpu.VMEM((blocks // 2 * rows, layers * rank), f32),
            pltpu.VMEM((layers, rank, columns), f32),
            pltpu.VMEM((slots, rank, width), f32),
            pltpu.SemaphoreType.DMA((3 + slots,)),
        ],
        compiler_params=params(basis, replica_delta, replica_delta, momentum_owned, momentum_owned),
        name="prepare",
    )(owner_of, layer_of, coeffs, stay(basis), momentum, weights)

    def after(array, done):
        return pl.pallas_call(
            after_kernel,
            out_shape=shape(array.shape, f32),
            in_specs=[ANY, ANY],
            out_specs=ANY,
            input_output_aliases={0: 0},
            compiler_params=params(),
            name="after",
        )(array, done)

    near = after(near, grad)
    partial = near[:, :, columns:]
    partial = (partial + swap(partial, 1)) + (swap(partial, 2) + swap(partial, 3))
    chosen = pl.pallas_call(
        select_kernel,
        out_shape=shape((blocks // 2, rows, columns), f32),
        in_specs=[VMEM] * 3,
        out_specs=VMEM,
        compiler_params=params(near, near, marks),
        name="select",
    )(near, grad, marks)
    far = swap(chosen, 1)
    near_across = swap(chosen, 2)
    far_across = swap(near_across, 1)
    new_weights, new_momentum, replica_weights = pl.pallas_call(
        lambda *refs: final_kernel(rep_count, *refs),
        out_shape=[
            shape(weights_owned.shape, f32),
            shape(weights_owned.shape, f32),
            shape((blocks, rows, width), f32),
        ],
        in_specs=[HBM, HBM] + [VMEM] * 9 + [HBM],
        out_specs=[HBM] * 3,
        scratch_shapes=[
            pltpu.SMEM(owner_of.shape, jnp.int32),
            pltpu.SMEM(layer_of.shape, jnp.int32),
            pltpu.VMEM(weights_owned.shape, f32),
            pltpu.VMEM(weights_owned.shape, f32),
            pltpu.VMEM(weights_owned.shape, f32),
            pltpu.VMEM((blocks, rows, width), f32),
            pltpu.SemaphoreType.DMA((1 + slots,)),
            pltpu.SemaphoreType.DMA((slots, 2)),
            pltpu.SemaphoreType.DMA(()),
        ],
        compiler_params=params(basis, weights_owned, weights_owned, weights_owned, replica_delta),
        name="final",
    )(
        stay(owner_of), stay(layer_of), partial, high, low, held, first,
        chosen, near_across, far, far_across, weights,
    )
    return (new_weights, new_momentum, replica_weights)


def solution(mesh):
    placed = (
        P("rep", None, "own", None),
        P(),
        P(),
        P(),
        P("own", None, None),
        P("own", None, None),
    )
    return jax.shard_map(
        local,
        mesh=mesh,
        in_specs=placed,
        out_specs=(P("own", None, None), P("own", None, None), P(None, "own", None)),
        check_vma=False,
    )
```

time: 29.7 us -> 29.1 us (0.980)
  waiting for transfers between devices: 8.06 us -> 7.36 us
    all_to_all x1, waiting for transfers between devices: 2.19 us -> 1.26 us  [local(): near = lax.all_to_all(sent, 'own', split_axis=0, concat_axis=0, tiled=True)]
  transfers between devices with their start and end apart: 9 -> 9, of which waited for: 6 -> 6; matrix products, arithmetic and copies ran while one was open for 0% -> 0% of each run, Pallas kernels for 8% -> 9%
where the time goes in v5:
time: 29.1 us; the launch traced here: 28.9 us
  starting transfers between devices  12.5 us (43%)
  Pallas kernels  8.32 us (29%)
  waiting for transfers between devices  7.36 us (25%)
  between operations  0.7 us (2%)
    all_to_all x1, starting transfers between devices, local(): near = lax.all_to_all(sent, 'own', split_axis=0, concat_axis=0, tiled=True)  7.29 us
    ppermute x8, waiting for transfers between devices, swap(): return lax.ppermute(array, 'rep', pairs)  6.1 us
    ppermute x8, starting transfers between devices, swap(): return lax.ppermute(array, 'rep', pairs)  5.16 us
    pallas_call x1, Pallas kernels, local(): pl.pallas_call(outset_kernel, out_shape=[shape((own_count, rows, total),...  3.23 us
    pallas_call x1, Pallas kernels, local(): pl.pallas_call(lambda *refs: prepare_kernel(rep_count, *refs), out_shape=...  2.5 us
    pallas_call x1, Pallas kernels, local(): pl.pallas_call(lambda *refs: final_kernel(rep_count, *refs), out_shape=[s...  2.34 us
    all_to_all x1, waiting for transfers between devices, local(): near = lax.all_to_all(sent, 'own', split_axis=0, concat_axis=0, tiled=True)  1.26 us
  transfers between devices with their start and end apart: 9, of which 6 were waited for; matrix products, arithmetic and copies ran while one was open for 0% of the time, Pallas kernels for 9%

profile of v5, /device:TPU:0, one launch (start us, length us, event | category | flops | bytes accessed | tf_op | source)
XLA Modules:
  0.0 28.9 jit_solution(3719276275848288452)
XLA Ops:
  0.6 0.0 copy-start
  0.6 0.0 copy-start.1
  0.7 3.2 %outset.1 = (f32[8,8,1024]{2,1,0:T(8,128)}, f32[8,8,128]{2,1,0:T(8,128)S(1)}) custom-call(s32[8]{0:T(128)} %refs_0_.3, s32[8]{0:T(128)} %refs_1_.3, f32[8,8,1792]{2,1,0:T(8,128)} %bitcast.4, f32[4,64,1792]{2,1,0:T(8,128)} %bitcast.2, f32[2,64,1792]{2,1,0:T(8,128)} %refs_11_.1, f32[2,64,1792]{2,1,0:T(8,128)} %refs_4_.1), custom_call_target="tpu_custom_call" | custom-call | tf_op jit(solution)/shard_map/outset/pallas_call | solution.py:317
  3.9 7.3 %all-to-all-start = ((f32[8,8,1024]{2,1,0:T(8,128)}), f32[8,8,1024]{2,1,0:T(8,128)S(1)}, u32[]{:S(2)}, u32[]{:S(2)}) async-start(f32[8,8,1024]{2,1,0:T(8,128)} %get-tuple-element.11), calls=%async_computation | async-start | bytes 524288 | tf_op jit(solution)/shard_map/all_to_all | solution.py:339
  11.2 0.0 collective-permute-start
  11.2 1.2 %collective-permute-done = f32[8,8,128]{2,1,0:T(8,128)S(1)} collective-permute-done((f32[8,8,128]{2,1,0:T(8,128)S(1)}, f32[8,8,128]{2,1,0:T(8,128)S(1)}, u32[]{:S(2)}, u32[]{:S(2)}) %collective-permute-start) | collective-permute-done | bytes 32800 | tf_op jit(solution)/shard_map/ppermute | solution.py:315
  12.4 1.5 %collective-permute-start.1 = (f32[8,8,128]{2,1,0:T(8,128)S(1)}, f32[8,8,128]{2,1,0:T(8,128)S(1)}, u32[]{:S(2)}, u32[]{:S(2)}) collective-permute-start(f32[8,8,128]{2,1,0:T(8,128)S(1)} %add.15), channel_id=1, source_target_pairs={{0,16},{8,24},{16,0},{24,8},{1,17},{9,25},{17,1},{25,9},{2,18},{10... | collective-permute-start | bytes 98312 | tf_op jit(solution)/shard_map/ppermute | solution.py:315
  13.9 2.4 %collective-permute-done.1 = f32[8,8,128]{2,1,0:T(8,128)S(1)} collective-permute-done((f32[8,8,128]{2,1,0:T(8,128)S(1)}, f32[8,8,128]{2,1,0:T(8,128)S(1)}, u32[]{:S(2)}, u32[]{:S(2)}) %collective-permute-start.1) | collective-permute-done | bytes 32800 | tf_op jit(solution)/shard_map/ppermute | solution.py:315
  16.3 0.0 copy-done
  16.3 0.0 copy-done.1
  16.3 2.5 %prepare.1 = (f32[4,8,896]{2,1,0:T(8,128)S(1)}, bf16[2,64,1792]{2,1,0:T(8,128)(2,1)S(1)}, bf16[2,64,1792]{2,1,0:T(8,128)(2,1)S(1)}, f32[2,64,1792]{2,1,0:T(8,128...) custom-call(s32[8]{0:T(128)S(1)} %copy-done, s32[8]{0:T(128)S(1)} %copy-done.1, f32[8,8,128]{2,1,0:T(8,128)S(1)} %add.16.refs_2_, ...), custom_call_target="tpu_custom_call" | custom-call | tf_op jit(solution)/shard_map/prepare/pallas_call | solution.py:343
  18.8 1.3 %all-to-all-done.rows_ref = f32[8,8,1024]{2,1,0:T(8,128)S(1)} async-done(((f32[8,8,1024]{2,1,0:T(8,128)}), f32[8,8,1024]{2,1,0:T(8,128)S(1)}, u32[]{:S(2)}, u32[]{:S(2)}) %all-to-all-start) | async-done | bytes 262176 | tf_op jit(solution)/shard_map/all_to_all | solution.py:339
  20.1 0.3 select.1.refs_7_
  20.4 1.5 %collective-permute-start.5 = (f32[4,8,896]{2,1,0:T(8,128)S(1)}, f32[4,8,896]{2,1,0:T(8,128)S(1)}, u32[]{:S(2)}, u32[]{:S(2)}) collective-permute-start(f32[4,8,896]{2,1,0:T(8,128)S(1)} %select.1.refs_7_), channel_id=1, source_target_pairs={{0,16},{8,24},{16,0},{24,8},{1,17},{9,25},{17,1},{25,9},{2,18},{10... | collective-permute-start | bytes 344072 | tf_op jit(solution)/shard_map/ppermute | solution.py:315
  21.9 0.6 %collective-permute-start.3 = (f32[8,8,128]{2,1,0:T(8,128)S(1)}, f32[8,8,128]{2,1,0:T(8,128)S(1)}, u32[]{:S(2)}, u32[]{:S(2)}) collective-permute-start(f32[8,8,128]{2,1,0:T(8,128)S(1)} %slice.4), channel_id=1, source_target_pairs={{0,16},{8,24},{16,0},{24,8},{1,17},{9,25},{17,1},{25,9},{2,18},{10... | collective-permute-start | bytes 98312 | tf_op jit(solution)/shard_map/ppermute | solution.py:315
  22.5 0.0 collective-permute-start.4
  22.5 1.6 %collective-permute-start.2 = (f32[8,8,128]{2,1,0:T(8,128)S(1)}, f32[8,8,128]{2,1,0:T(8,128)S(1)}, u32[]{:S(2)}, u32[]{:S(2)}) collective-permute-start(f32[8,8,128]{2,1,0:T(8,128)S(1)} %slice.4), channel_id=1, source_target_pairs={{0,8},{8,0},{16,24},{24,16},{1,9},{9,1},{17,25},{25,17},{2,10},{10... | collective-permute-start | bytes 98312 | tf_op jit(solution)/shard_map/ppermute | solution.py:315
  24.0 0.0 collective-permute-start.6
  24.0 1.2 %collective-permute-done.5.refs_8_ = f32[4,8,896]{2,1,0:T(8,128)S(1)} collective-permute-done((f32[4,8,896]{2,1,0:T(8,128)S(1)}, f32[4,8,896]{2,1,0:T(8,128)S(1)}, u32[]{:S(2)}, u32[]{:S(2)}) %collective-permute-start.5) | collective-permute-done | bytes 114720 | tf_op jit(solution)/shard_map/ppermute | solution.py:315
  25.2 0.0 collective-permute-start.7
  25.2 0.9 %collective-permute-done.3 = f32[8,8,128]{2,1,0:T(8,128)S(1)} collective-permute-done((f32[8,8,128]{2,1,0:T(8,128)S(1)}, f32[8,8,128]{2,1,0:T(8,128)S(1)}, u32[]{:S(2)}, u32[]{:S(2)}) %collective-permute-start.3) | collective-permute-done | bytes 32800 | tf_op jit(solution)/shard_map/ppermute | solution.py:315
  26.1 0.0 collective-permute-done.4
  26.1 0.0 collective-permute-done.2
  26.2 0.0 collective-permute-done.6.refs_9_
  26.2 0.4 %collective-permute-done.7.refs_10_ = f32[4,8,896]{2,1,0:T(8,128)S(1)} collective-permute-done((f32[4,8,896]{2,1,0:T(8,128)S(1)}, f32[4,8,896]{2,1,0:T(8,128)S(1)}, u32[]{:S(2)}, u32[]{:S(2)}) %collective-permute-start.7) | collective-permute-done | bytes 114720 | tf_op jit(solution)/shard_map/ppermute | solution.py:315
  26.5 2.3 %final.1 = (f32[2,64,1792]{2,1,0:T(8,128)}, f32[2,64,1792]{2,1,0:T(8,128)}, f32[8,8,1792]{2,1,0:T(8,128)}) custom-call(s32[8]{0:T(128)} %refs_0_.3, s32[8]{0:T(128)} %refs_1_.3, f32[8,8,128]{2,1,0:T(8,128)S(1)} %add_add_fusion.refs_2_, bf16[2,64,1792]{2,1,0:T(8,128)(2,1)S(1)} %get-tuple-element.14.refs_3_, ...), custom_call_target="tpu_custom_call" | custom-call | tf_op jit(solution)/shard_map/final/pallas_call | solution.py:390
  (5 shorter events, 0.0 us)
Async XLA Ops:
  0.6 15.7 %copy-start = (s32[8]{0:T(128)S(1)}, s32[8]{0:T(128)}, u32[]{:S(2)}) copy-start(s32[8]{0:T(128)} %refs_0_.3) | copy-start | bytes 100
  0.6 15.7 %copy-start.1 = (s32[8]{0:T(128)S(1)}, s32[8]{0:T(128)}, u32[]{:S(2)}) copy-start(s32[8]{0:T(128)} %refs_1_.3) | copy-start | bytes 100
  3.9 16.2 %all-to-all-start = ((f32[8,8,1024]{2,1,0:T(8,128)}), f32[8,8,1024]{2,1,0:T(8,128)S(1)}, u32[]{:S(2)}, u32[]{:S(2)}) async-start(f32[8,8,1024]{2,1,0:T(8,128)} %get-tuple-element.11), calls=%async_computation | async-start | bytes 524288 | tf_op jit(solution)/shard_map/all_to_all | solution.py:339
  11.2 1.2 %collective-permute-start = (f32[8,8,128]{2,1,0:T(8,128)S(1)}, f32[8,8,128]{2,1,0:T(8,128)S(1)}, u32[]{:S(2)}, u32[]{:S(2)}) collective-permute-start(f32[8,8,128]{2,1,0:T(8,128)S(1)} %get-tuple-element.12), channel_id=1, source_target_pairs={{0,8},{8,0},{16,24},{24,16},{1,9},{9,1},{17,25},{25,17},{2,10},{10... | collective-permute-start | bytes 98312 | tf_op jit(solution)/shard_map/ppermute | solution.py:315
  12.4 3.9 %collective-permute-start.1 = (f32[8,8,128]{2,1,0:T(8,128)S(1)}, f32[8,8,128]{2,1,0:T(8,128)S(1)}, u32[]{:S(2)}, u32[]{:S(2)}) collective-permute-start(f32[8,8,128]{2,1,0:T(8,128)S(1)} %add.15), channel_id=1, source_target_pairs={{0,16},{8,24},{16,0},{24,8},{1,17},{9,25},{17,1},{25,9},{2,18},{10... | collective-permute-start | bytes 98312 | tf_op jit(solution)/shard_map/ppermute | solution.py:315
  20.4 4.9 %collective-permute-start.5 = (f32[4,8,896]{2,1,0:T(8,128)S(1)}, f32[4,8,896]{2,1,0:T(8,128)S(1)}, u32[]{:S(2)}, u32[]{:S(2)}) collective-permute-start(f32[4,8,896]{2,1,0:T(8,128)S(1)} %select.1.refs_7_), channel_id=1, source_target_pairs={{0,16},{8,24},{16,0},{24,8},{1,17},{9,25},{17,1},{25,9},{2,18},{10... | collective-permute-start | bytes 344072 | tf_op jit(solution)/shard_map/ppermute | solution.py:315
  21.9 4.2 %collective-permute-start.3 = (f32[8,8,128]{2,1,0:T(8,128)S(1)}, f32[8,8,128]{2,1,0:T(8,128)S(1)}, u32[]{:S(2)}, u32[]{:S(2)}) collective-permute-start(f32[8,8,128]{2,1,0:T(8,128)S(1)} %slice.4), channel_id=1, source_target_pairs={{0,16},{8,24},{16,0},{24,8},{1,17},{9,25},{17,1},{25,9},{2,18},{10... | collective-permute-start | bytes 98312 | tf_op jit(solution)/shard_map/ppermute | solution.py:315
  22.5 3.7 %collective-permute-start.4 = (f32[8,8,128]{2,1,0:T(8,128)S(1)}, f32[8,8,128]{2,1,0:T(8,128)S(1)}, u32[]{:S(2)}, u32[]{:S(2)}) collective-permute-start(f32[8,8,128]{2,1,0:T(8,128)S(1)} %slice.4), channel_id=1, source_target_pairs={{0,24},{8,16},{16,8},{24,0},{1,25},{9,17},{17,9},{25,1},{2,26},{10... | collective-permute-start | bytes 98312 | tf_op jit(solution)/shard_map/ppermute | solution.py:315
  22.5 3.7 %collective-permute-start.2 = (f32[8,8,128]{2,1,0:T(8,128)S(1)}, f32[8,8,128]{2,1,0:T(8,128)S(1)}, u32[]{:S(2)}, u32[]{:S(2)}) collective-permute-start(f32[8,8,128]{2,1,0:T(8,128)S(1)} %slice.4), channel_id=1, source_target_pairs={{0,8},{8,0},{16,24},{24,16},{1,9},{9,1},{17,25},{25,17},{2,10},{10... | collective-permute-start | bytes 98312 | tf_op jit(solution)/shard_map/ppermute | solution.py:315
  24.0 2.1 %collective-permute-start.6 = (f32[4,8,896]{2,1,0:T(8,128)S(1)}, f32[4,8,896]{2,1,0:T(8,128)S(1)}, u32[]{:S(2)}, u32[]{:S(2)}) collective-permute-start(f32[4,8,896]{2,1,0:T(8,128)S(1)} %select.1.refs_7_), channel_id=1, source_target_pairs={{0,8},{8,0},{16,24},{24,16},{1,9},{9,1},{17,25},{25,17},{2,10},{10... | collective-permute-start | bytes 344072 | tf_op jit(solution)/shard_map/ppermute | solution.py:315
  25.2 1.3 %collective-permute-start.7 = (f32[4,8,896]{2,1,0:T(8,128)S(1)}, f32[4,8,896]{2,1,0:T(8,128)S(1)}, u32[]{:S(2)}, u32[]{:S(2)}) collective-permute-start(f32[4,8,896]{2,1,0:T(8,128)S(1)} %collective-permute-done.5.refs_8_), channel_id=1, source_target_pairs={{0,8},{8,0},{16,24},{24,16},{1,9},{9,1},{17,25},{25,17},{2,10},{10... | collective-permute-start | bytes 344072 | tf_op jit(solution)/shard_map/ppermute | solution.py:315

commit v6 on v5

--- a/solution.py
+++ b/solution.py
@@ -77,9 +77,12 @@
             (momentum_ref.at[:, :, part], m_ref),
         ))
     ]
-    for load in loads:
+    for load in loads[:-2]:
         load.start()
-    for load in loads[2:-2]:
+    loads[2].wait()
+    loads[-2].start()
+    loads[-1].start()
+    for load in loads[3:-2]:
         load.wait()
     high, low = split(basis_vmem[...].reshape(layers * rank, width))
     products = product(delta_vmem[...].reshape(blocks * rows, width), high, low, ((1,), (1,)))
@@ -188,6 +191,15 @@
         low_ref[slot] = slot_low
     loads[-2].wait()
     loads[-1].wait()
+    for slot in range(slots):
+
+        @pl.when(found[slot][0] == 0)
+        def _():
+            high_ref[slot] = jnp.zeros_like(high_ref[slot])
+            low_ref[slot] = jnp.zeros_like(low_ref[slot])
+            held_ref[slot] = jnp.zeros_like(held_ref[slot])
+            if slot == 0:
+                first_ref[...] = jnp.zeros_like(first_ref)
 
 
 def select_kernel(near_ref, grad_ref, marks_ref, chosen_ref):
@@ -238,6 +250,27 @@
     ]
     for load in loads:
         load.start()
+    stores = []
+    averaged = coeffs_ref[...].reshape(rows, slots * rank) * (1.0 / reps)
+
+    def send(source, target, slot, which):
+        store = pltpu.make_async_copy(source.at[slot], target.at[slot], out_sems.at[slot, which])
+        store.start()
+        stores.append(store)
+
+    for slot in range(slots):
+        grad = product(
+            averaged[:, slot * rank:(slot + 1) * rank], high_ref[slot], low_ref[slot]
+        )
+        momentum = momentum_decay * momentum_ref[slot] + grad
+        m_ref[slot] = momentum
+        send(m_ref, new_momentum_ref, slot, 0)
+        change = outer_rate * (grad + momentum_decay * momentum)
+        if slot == 0:
+            w_ref[0] = first_ref[...] - change
+            send(w_ref, new_weights_ref, 0, 1)
+        else:
+            change_ref[slot] = change
     upper = lax.broadcasted_iota(jnp.int32, (tile, columns), 0) < tile // 2
     for near_core in range(2):
         for near_across in range(2):
@@ -261,33 +294,13 @@
 
     store = pltpu.make_async_copy(rows_ref, replica_ref, rows_sem)
     store.start()
-    stores = [store]
-    averaged = coeffs_ref[...].reshape(rows, slots * rank) * (1.0 / reps)
-    loads[0].wait()
-    loads[1].wait()
-    used = [held_by(me, slot, owner_smem, layer_smem)[0] for slot in range(slots)]
-
-    def send(source, target, slot, which):
-        store = pltpu.make_async_copy(source.at[slot], target.at[slot], out_sems.at[slot, which])
-        store.start()
-        stores.append(store)
-
-    for slot in range(slots):
-        grad = product(
-            averaged[:, slot * rank:(slot + 1) * rank], high_ref[slot], low_ref[slot]
-        )
-        momentum = momentum_decay * momentum_ref[slot] + grad
-        m_ref[slot] = jnp.where(used[slot] == 1, momentum, 0.0)
-        send(m_ref, new_momentum_ref, slot, 0)
-        change = outer_rate * (grad + momentum_decay * momentum)
-        if slot == 0:
-            w_ref[0] = jnp.where(used[0] == 1, first_ref[...] - change, 0.0)
-            send(w_ref, new_weights_ref, 0, 1)
-        else:
-            change_ref[slot] = change
+    stores.append(store)
+    for load in loads[:2]:
+        load.wait()
     for slot in range(1, slots):
+        used, _ = held_by(me, slot, owner_smem, layer_smem)
         loads[1 + slot].wait()
-        w_ref[slot] = jnp.where(used[slot] == 1, w_ref[slot] - change_ref[slot], 0.0)
+        w_ref[slot] = jnp.where(used == 1, w_ref[slot] - change_ref[slot], 0.0)
         send(w_ref, new_weights_ref, slot, 1)
     for store in stores:
         store.wait()

time: 29.1 us -> 28.8 us (0.990)
  Pallas kernels: 8.32 us -> 7.94 us
    pallas_call x1, Pallas kernels: 2.34 us -> 1.92 us  [local(): pl.pallas_call(lambda *refs: final_kernel(rep_count, *refs), out_shape=[s...]
where the time goes in v6:
time: 28.8 us; the launch traced here: 28.5 us
  starting transfers between devices  12.5 us (43%)
  Pallas kernels  7.94 us (28%)
  waiting for transfers between devices  7.37 us (26%)
  between operations  0.7 us (2%)
    all_to_all x1, starting transfers between devices, local(): near = lax.all_to_all(sent, 'own', split_axis=0, concat_axis=0, tiled=True)  7.29 us
    ppermute x8, waiting for transfers between devices, swap(): return lax.ppermute(array, 'rep', pairs)  6.11 us
    ppermute x8, starting transfers between devices, swap(): return lax.ppermute(array, 'rep', pairs)  5.16 us
    pallas_call x1, Pallas kernels, local(): pl.pallas_call(outset_kernel, out_shape=[shape((own_count, rows, total),...  3.27 us
    pallas_call x1, Pallas kernels, local(): pl.pallas_call(lambda *refs: prepare_kernel(rep_count, *refs), out_shape=...  2.5 us
    pallas_call x1, Pallas kernels, local(): pl.pallas_call(lambda *refs: final_kernel(rep_count, *refs), out_shape=[s...  1.92 us
    all_to_all x1, waiting for transfers between devices, local(): near = lax.all_to_all(sent, 'own', split_axis=0, concat_axis=0, tiled=True)  1.26 us
  transfers between devices with their start and end apart: 9, of which 6 were waited for; matrix products, arithmetic and copies ran while one was open for 0% of the time, Pallas kernels for 9%

profile of v6, /device:TPU:0, one launch (start us, length us, event | category | flops | bytes accessed | tf_op | source)
XLA Modules:
  0.0 28.5 jit_solution(13759251973315557220)
XLA Ops:
  0.6 0.0 copy-start
  0.6 0.0 copy-start.1
  0.7 3.3 %outset.1 = (f32[8,8,1024]{2,1,0:T(8,128)}, f32[8,8,128]{2,1,0:T(8,128)S(1)}) custom-call(s32[8]{0:T(128)} %refs_0_.3, s32[8]{0:T(128)} %refs_1_.3, f32[8,8,1792]{2,1,0:T(8,128)} %bitcast.4, f32[4,64,1792]{2,1,0:T(8,128)} %bitcast.2, f32[2,64,1792]{2,1,0:T(8,128)} %refs_11_.1, f32[2,64,1792]{2,1,0:T(8,128)} %refs_4_.1), custom_call_target="tpu_custom_call" | custom-call | tf_op jit(solution)/shard_map/outset/pallas_call | solution.py:330
  3.9 7.3 %all-to-all-start = ((f32[8,8,1024]{2,1,0:T(8,128)}), f32[8,8,1024]{2,1,0:T(8,128)S(1)}, u32[]{:S(2)}, u32[]{:S(2)}) async-start(f32[8,8,1024]{2,1,0:T(8,128)} %get-tuple-element.11), calls=%async_computation | async-start | bytes 524288 | tf_op jit(solution)/shard_map/all_to_all | solution.py:352
  11.2 0.0 collective-permute-start
  11.2 1.2 %collective-permute-done = f32[8,8,128]{2,1,0:T(8,128)S(1)} collective-permute-done((f32[8,8,128]{2,1,0:T(8,128)S(1)}, f32[8,8,128]{2,1,0:T(8,128)S(1)}, u32[]{:S(2)}, u32[]{:S(2)}) %collective-permute-start) | collective-permute-done | bytes 32800 | tf_op jit(solution)/shard_map/ppermute | solution.py:328
  12.4 1.5 %collective-permute-start.1 = (f32[8,8,128]{2,1,0:T(8,128)S(1)}, f32[8,8,128]{2,1,0:T(8,128)S(1)}, u32[]{:S(2)}, u32[]{:S(2)}) collective-permute-start(f32[8,8,128]{2,1,0:T(8,128)S(1)} %add.15), channel_id=1, source_target_pairs={{0,16},{8,24},{16,0},{24,8},{1,17},{9,25},{17,1},{25,9},{2,18},{10... | collective-permute-start | bytes 98312 | tf_op jit(solution)/shard_map/ppermute | solution.py:328
  13.9 2.4 %collective-permute-done.1 = f32[8,8,128]{2,1,0:T(8,128)S(1)} collective-permute-done((f32[8,8,128]{2,1,0:T(8,128)S(1)}, f32[8,8,128]{2,1,0:T(8,128)S(1)}, u32[]{:S(2)}, u32[]{:S(2)}) %collective-permute-start.1) | collective-permute-done | bytes 32800 | tf_op jit(solution)/shard_map/ppermute | solution.py:328
  16.4 0.0 copy-done
  16.4 0.0 copy-done.1
  16.4 2.5 %prepare.1 = (f32[4,8,896]{2,1,0:T(8,128)S(1)}, bf16[2,64,1792]{2,1,0:T(8,128)(2,1)S(1)}, bf16[2,64,1792]{2,1,0:T(8,128)(2,1)S(1)}, f32[2,64,1792]{2,1,0:T(8,128...) custom-call(s32[8]{0:T(128)S(1)} %copy-done, s32[8]{0:T(128)S(1)} %copy-done.1, f32[8,8,128]{2,1,0:T(8,128)S(1)} %add.16.refs_2_, ...), custom_call_target="tpu_custom_call" | custom-call | tf_op jit(solution)/shard_map/prepare/pallas_call | solution.py:356
  18.9 1.3 %all-to-all-done.rows_ref = f32[8,8,1024]{2,1,0:T(8,128)S(1)} async-done(((f32[8,8,1024]{2,1,0:T(8,128)}), f32[8,8,1024]{2,1,0:T(8,128)S(1)}, u32[]{:S(2)}, u32[]{:S(2)}) %all-to-all-start) | async-done | bytes 262176 | tf_op jit(solution)/shard_map/all_to_all | solution.py:352
  20.1 0.3 select.1.refs_7_
  20.4 1.5 %collective-permute-start.5 = (f32[4,8,896]{2,1,0:T(8,128)S(1)}, f32[4,8,896]{2,1,0:T(8,128)S(1)}, u32[]{:S(2)}, u32[]{:S(2)}) collective-permute-start(f32[4,8,896]{2,1,0:T(8,128)S(1)} %select.1.refs_7_), channel_id=1, source_target_pairs={{0,16},{8,24},{16,0},{24,8},{1,17},{9,25},{17,1},{25,9},{2,18},{10... | collective-permute-start | bytes 344072 | tf_op jit(solution)/shard_map/ppermute | solution.py:328
  21.9 0.6 %collective-permute-start.3 = (f32[8,8,128]{2,1,0:T(8,128)S(1)}, f32[8,8,128]{2,1,0:T(8,128)S(1)}, u32[]{:S(2)}, u32[]{:S(2)}) collective-permute-start(f32[8,8,128]{2,1,0:T(8,128)S(1)} %slice.4), channel_id=1, source_target_pairs={{0,16},{8,24},{16,0},{24,8},{1,17},{9,25},{17,1},{25,9},{2,18},{10... | collective-permute-start | bytes 98312 | tf_op jit(solution)/shard_map/ppermute | solution.py:328
  22.5 0.0 collective-permute-start.4
  22.5 1.6 %collective-permute-start.2 = (f32[8,8,128]{2,1,0:T(8,128)S(1)}, f32[8,8,128]{2,1,0:T(8,128)S(1)}, u32[]{:S(2)}, u32[]{:S(2)}) collective-permute-start(f32[8,8,128]{2,1,0:T(8,128)S(1)} %slice.4), channel_id=1, source_target_pairs={{0,8},{8,0},{16,24},{24,16},{1,9},{9,1},{17,25},{25,17},{2,10},{10... | collective-permute-start | bytes 98312 | tf_op jit(solution)/shard_map/ppermute | solution.py:328
  24.1 0.0 collective-permute-start.6
  24.1 1.2 %collective-permute-done.5.refs_8_ = f32[4,8,896]{2,1,0:T(8,128)S(1)} collective-permute-done((f32[4,8,896]{2,1,0:T(8,128)S(1)}, f32[4,8,896]{2,1,0:T(8,128)S(1)}, u32[]{:S(2)}, u32[]{:S(2)}) %collective-permute-start.5) | collective-permute-done | bytes 114720 | tf_op jit(solution)/shard_map/ppermute | solution.py:328
  25.3 0.0 collective-permute-start.7
  25.3 0.9 %collective-permute-done.3 = f32[8,8,128]{2,1,0:T(8,128)S(1)} collective-permute-done((f32[8,8,128]{2,1,0:T(8,128)S(1)}, f32[8,8,128]{2,1,0:T(8,128)S(1)}, u32[]{:S(2)}, u32[]{:S(2)}) %collective-permute-start.3) | collective-permute-done | bytes 32800 | tf_op jit(solution)/shard_map/ppermute | solution.py:328
  26.2 0.0 collective-permute-done.4
  26.2 0.0 collective-permute-done.2
  26.2 0.0 collective-permute-done.6.refs_9_
  26.2 0.4 %collective-permute-done.7.refs_10_ = f32[4,8,896]{2,1,0:T(8,128)S(1)} collective-permute-done((f32[4,8,896]{2,1,0:T(8,128)S(1)}, f32[4,8,896]{2,1,0:T(8,128)S(1)}, u32[]{:S(2)}, u32[]{:S(2)}) %collective-permute-start.7) | collective-permute-done | bytes 114720 | tf_op jit(solution)/shard_map/ppermute | solution.py:328
  26.6 1.9 %final.1 = (f32[2,64,1792]{2,1,0:T(8,128)}, f32[2,64,1792]{2,1,0:T(8,128)}, f32[8,8,1792]{2,1,0:T(8,128)}) custom-call(s32[8]{0:T(128)} %refs_0_.3, s32[8]{0:T(128)} %refs_1_.3, f32[8,8,128]{2,1,0:T(8,128)S(1)} %add_add_fusion.refs_2_, bf16[2,64,1792]{2,1,0:T(8,128)(2,1)S(1)} %get-tuple-element.14.refs_3_, ...), custom_call_target="tpu_custom_call" | custom-call | tf_op jit(solution)/shard_map/final/pallas_call | solution.py:403
  (5 shorter events, 0.0 us)
Async XLA Ops:
  0.6 15.7 %copy-start = (s32[8]{0:T(128)S(1)}, s32[8]{0:T(128)}, u32[]{:S(2)}) copy-start(s32[8]{0:T(128)} %refs_0_.3) | copy-start | bytes 100
  0.6 15.7 %copy-start.1 = (s32[8]{0:T(128)S(1)}, s32[8]{0:T(128)}, u32[]{:S(2)}) copy-start(s32[8]{0:T(128)} %refs_1_.3) | copy-start | bytes 100
  3.9 16.2 %all-to-all-start = ((f32[8,8,1024]{2,1,0:T(8,128)}), f32[8,8,1024]{2,1,0:T(8,128)S(1)}, u32[]{:S(2)}, u32[]{:S(2)}) async-start(f32[8,8,1024]{2,1,0:T(8,128)} %get-tuple-element.11), calls=%async_computation | async-start | bytes 524288 | tf_op jit(solution)/shard_map/all_to_all | solution.py:352
  11.2 1.2 %collective-permute-start = (f32[8,8,128]{2,1,0:T(8,128)S(1)}, f32[8,8,128]{2,1,0:T(8,128)S(1)}, u32[]{:S(2)}, u32[]{:S(2)}) collective-permute-start(f32[8,8,128]{2,1,0:T(8,128)S(1)} %get-tuple-element.12), channel_id=1, source_target_pairs={{0,8},{8,0},{16,24},{24,16},{1,9},{9,1},{17,25},{25,17},{2,10},{10... | collective-permute-start | bytes 98312 | tf_op jit(solution)/shard_map/ppermute | solution.py:328
  12.4 3.9 %collective-permute-start.1 = (f32[8,8,128]{2,1,0:T(8,128)S(1)}, f32[8,8,128]{2,1,0:T(8,128)S(1)}, u32[]{:S(2)}, u32[]{:S(2)}) collective-permute-start(f32[8,8,128]{2,1,0:T(8,128)S(1)} %add.15), channel_id=1, source_target_pairs={{0,16},{8,24},{16,0},{24,8},{1,17},{9,25},{17,1},{25,9},{2,18},{10... | collective-permute-start | bytes 98312 | tf_op jit(solution)/shard_map/ppermute | solution.py:328
  20.4 4.9 %collective-permute-start.5 = (f32[4,8,896]{2,1,0:T(8,128)S(1)}, f32[4,8,896]{2,1,0:T(8,128)S(1)}, u32[]{:S(2)}, u32[]{:S(2)}) collective-permute-start(f32[4,8,896]{2,1,0:T(8,128)S(1)} %select.1.refs_7_), channel_id=1, source_target_pairs={{0,16},{8,24},{16,0},{24,8},{1,17},{9,25},{17,1},{25,9},{2,18},{10... | collective-permute-start | bytes 344072 | tf_op jit(solution)/shard_map/ppermute | solution.py:328
  21.9 4.2 %collective-permute-start.3 = (f32[8,8,128]{2,1,0:T(8,128)S(1)}, f32[8,8,128]{2,1,0:T(8,128)S(1)}, u32[]{:S(2)}, u32[]{:S(2)}) collective-permute-start(f32[8,8,128]{2,1,0:T(8,128)S(1)} %slice.4), channel_id=1, source_target_pairs={{0,16},{8,24},{16,0},{24,8},{1,17},{9,25},{17,1},{25,9},{2,18},{10... | collective-permute-start | bytes 98312 | tf_op jit(solution)/shard_map/ppermute | solution.py:328
  22.5 3.7 %collective-permute-start.4 = (f32[8,8,128]{2,1,0:T(8,128)S(1)}, f32[8,8,128]{2,1,0:T(8,128)S(1)}, u32[]{:S(2)}, u32[]{:S(2)}) collective-permute-start(f32[8,8,128]{2,1,0:T(8,128)S(1)} %slice.4), channel_id=1, source_target_pairs={{0,24},{8,16},{16,8},{24,0},{1,25},{9,17},{17,9},{25,1},{2,26},{10... | collective-permute-start | bytes 98312 | tf_op jit(solution)/shard_map/ppermute | solution.py:328
  22.5 3.7 %collective-permute-start.2 = (f32[8,8,128]{2,1,0:T(8,128)S(1)}, f32[8,8,128]{2,1,0:T(8,128)S(1)}, u32[]{:S(2)}, u32[]{:S(2)}) collective-permute-start(f32[8,8,128]{2,1,0:T(8,128)S(1)} %slice.4), channel_id=1, source_target_pairs={{0,8},{8,0},{16,24},{24,16},{1,9},{9,1},{17,25},{25,17},{2,10},{10... | collective-permute-start | bytes 98312 | tf_op jit(solution)/shard_map/ppermute | solution.py:328
  24.1 2.1 %collective-permute-start.6 = (f32[4,8,896]{2,1,0:T(8,128)S(1)}, f32[4,8,896]{2,1,0:T(8,128)S(1)}, u32[]{:S(2)}, u32[]{:S(2)}) collective-permute-start(f32[4,8,896]{2,1,0:T(8,128)S(1)} %select.1.refs_7_), channel_id=1, source_target_pairs={{0,8},{8,0},{16,24},{24,16},{1,9},{9,1},{17,25},{25,17},{2,10},{10... | collective-permute-start | bytes 344072 | tf_op jit(solution)/shard_map/ppermute | solution.py:328
  25.3 1.3 %collective-permute-start.7 = (f32[4,8,896]{2,1,0:T(8,128)S(1)}, f32[4,8,896]{2,1,0:T(8,128)S(1)}, u32[]{:S(2)}, u32[]{:S(2)}) collective-permute-start(f32[4,8,896]{2,1,0:T(8,128)S(1)} %collective-permute-done.5.refs_8_), channel_id=1, source_target_pairs={{0,8},{8,0},{16,24},{24,16},{1,9},{9,1},{17,25},{25,17},{2,10},{10... | collective-permute-start | bytes 344072 | tf_op jit(solution)/shard_map/ppermute | solution.py:328

commit v7 on v6

--- a/solution.py
+++ b/solution.py
@@ -69,46 +69,37 @@
     loads = [
         pltpu.make_async_copy(source, target, in_sems.at[index])
         for index, (source, target) in enumerate((
-            (owner_ref, owner_smem),
-            (layer_ref, layer_smem),
             (delta_ref, delta_vmem),
             *[(basis_ref.at[layer], basis_vmem.at[layer]) for layer in range(layers)],
             (weights_ref.at[:, :, part], w_ref),
             (momentum_ref.at[:, :, part], m_ref),
+            (owner_ref, owner_smem),
+            (layer_ref, layer_smem),
         ))
     ]
-    for load in loads[:-2]:
+    for load in loads:
         load.start()
-    loads[2].wait()
-    loads[-2].start()
-    loads[-1].start()
-    for load in loads[3:-2]:
+    for load in loads[:1 + layers]:
         load.wait()
     high, low = split(basis_vmem[...].reshape(layers * rank, width))
     products = product(delta_vmem[...].reshape(blocks * rows, width), high, low, ((1,), (1,)))
-    loads[-2].wait()
-    loads[-1].wait()
+    for load in loads[1 + layers:]:
+        load.wait()
     upper = lax.broadcasted_iota(jnp.int32, (rows, columns), 0) < rows // 2
     for owner in range(owners):
         here = pl.ds(owner * rows, rows)
         first, second = [
             w_ref[slot, here, :] - carried * m_ref[slot, here, :] for slot in range(2)
         ]
-        for side in range(2):
-
-            @pl.when(across == side)
-            def _():
-                if side == 0:
-                    tile = jnp.where(upper, first, pltpu.roll(second, rows // 2, 0))
-                else:
-                    tile = jnp.where(upper, pltpu.roll(first, rows // 2, 0), second)
-                made_ref[owner, :, :columns] = tile
+        made_ref[owner, :, :columns] = jnp.where(
+            across == 0,
+            jnp.where(upper, first, pltpu.roll(second, rows // 2, 0)),
+            jnp.where(upper, pltpu.roll(first, rows // 2, 0), second),
+        )
     early = pltpu.make_async_copy(
         made_ref.at[:, :, :columns], sent_ref.at[:, :, :columns], out_sems.at[0]
     )
     early.start()
-    loads[0].wait()
-    loads[1].wait()
     lane = lax.broadcasted_iota(jnp.int32, (rows, 2 * rank), 1)
     coeffs_ref[...] = jnp.zeros_like(coeffs_ref)
     for block in range(blocks):
@@ -118,8 +109,7 @@
             own = products[block * rows:(block + 1) * rows, 2 * rank * pair:2 * rank * (pair + 1)]
             folded = folded + jnp.where(2 * pair + lane // rank == layer_smem[block], own, 0.0)
         folded = folded + pltpu.roll(folded, rank, 1)
-        placed = jnp.where(lane // rank == slot, folded, 0.0)
-        coeffs_ref[owner] = coeffs_ref[owner] + placed
+        pltpu.store(coeffs_ref.at[owner], folded, mask=lane // rank == slot)
     made_ref[:, :, columns:] = coeffs_ref[...]
     late = pltpu.make_async_copy(
         made_ref.at[:, :, columns:], sent_ref.at[:, :, columns:], out_sems.at[1]

time: 28.8 us -> 28.7 us (level)
  no operation moved by 1% of the time
where the time goes in v7:
time: 28.7 us; the launch traced here: 28.4 us
  starting transfers between devices  12.5 us (44%)
  Pallas kernels  7.89 us (27%)
  waiting for transfers between devices  7.26 us (25%)
  between operations  0.7 us (2%)
    all_to_all x1, starting transfers between devices, local(): near = lax.all_to_all(sent, 'own', split_axis=0, concat_axis=0, tiled=True)  7.29 us
    ppermute x8, waiting for transfers between devices, swap(): return lax.ppermute(array, 'rep', pairs)  6.06 us
    ppermute x8, starting transfers between devices, swap(): return lax.ppermute(array, 'rep', pairs)  5.2 us
    pallas_call x1, Pallas kernels, local(): pl.pallas_call(outset_kernel, out_shape=[shape((own_count, rows, total),...  3.16 us
    pallas_call x1, Pallas kernels, local(): pl.pallas_call(lambda *refs: prepare_kernel(rep_count, *refs), out_shape=...  2.56 us
    pallas_call x1, Pallas kernels, local(): pl.pallas_call(lambda *refs: final_kernel(rep_count, *refs), out_shape=[s...  1.92 us
    all_to_all x1, waiting for transfers between devices, local(): near = lax.all_to_all(sent, 'own', split_axis=0, concat_axis=0, tiled=True)  1.2 us
  transfers between devices with their start and end apart: 9, of which 6 were waited for; matrix products, arithmetic and copies ran while one was open for 0% of the time, Pallas kernels for 9%

profile of v7, /device:TPU:0, one launch (start us, length us, event | category | flops | bytes accessed | tf_op | source)
XLA Modules:
  0.0 28.4 jit_solution(7627347795134663515)
XLA Ops:
  0.6 0.0 copy-start
  0.6 0.0 copy-start.1
  0.7 3.2 %outset.1 = (f32[8,8,1024]{2,1,0:T(8,128)}, f32[8,8,128]{2,1,0:T(8,128)S(1)}) custom-call(s32[8]{0:T(128)} %refs_0_.3, s32[8]{0:T(128)} %refs_1_.3, f32[8,8,1792]{2,1,0:T(8,128)} %bitcast.4, f32[4,64,1792]{2,1,0:T(8,128)} %bitcast.2, f32[2,64,1792]{2,1,0:T(8,128)} %refs_11_.1, f32[2,64,1792]{2,1,0:T(8,128)} %refs_4_.1), custom_call_target="tpu_custom_call" | custom-call | tf_op jit(solution)/shard_map/outset/pallas_call | solution.py:320
  3.8 7.3 %all-to-all-start = ((f32[8,8,1024]{2,1,0:T(8,128)}), f32[8,8,1024]{2,1,0:T(8,128)S(1)}, u32[]{:S(2)}, u32[]{:S(2)}) async-start(f32[8,8,1024]{2,1,0:T(8,128)} %get-tuple-element.11), calls=%async_computation | async-start | bytes 524288 | tf_op jit(solution)/shard_map/all_to_all | solution.py:342
  11.1 0.0 collective-permute-start
  11.1 1.2 %collective-permute-done = f32[8,8,128]{2,1,0:T(8,128)S(1)} collective-permute-done((f32[8,8,128]{2,1,0:T(8,128)S(1)}, f32[8,8,128]{2,1,0:T(8,128)S(1)}, u32[]{:S(2)}, u32[]{:S(2)}) %collective-permute-start) | collective-permute-done | bytes 32800 | tf_op jit(solution)/shard_map/ppermute | solution.py:318
  12.3 1.5 %collective-permute-start.1 = (f32[8,8,128]{2,1,0:T(8,128)S(1)}, f32[8,8,128]{2,1,0:T(8,128)S(1)}, u32[]{:S(2)}, u32[]{:S(2)}) collective-permute-start(f32[8,8,128]{2,1,0:T(8,128)S(1)} %add.15), channel_id=1, source_target_pairs={{0,16},{8,24},{16,0},{24,8},{1,17},{9,25},{17,1},{25,9},{2,18},{10... | collective-permute-start | bytes 98312 | tf_op jit(solution)/shard_map/ppermute | solution.py:318
  13.8 2.4 %collective-permute-done.1 = f32[8,8,128]{2,1,0:T(8,128)S(1)} collective-permute-done((f32[8,8,128]{2,1,0:T(8,128)S(1)}, f32[8,8,128]{2,1,0:T(8,128)S(1)}, u32[]{:S(2)}, u32[]{:S(2)}) %collective-permute-start.1) | collective-permute-done | bytes 32800 | tf_op jit(solution)/shard_map/ppermute | solution.py:318
  16.2 0.0 copy-done
  16.2 0.0 copy-done.1
  16.3 2.6 %prepare.1 = (f32[4,8,896]{2,1,0:T(8,128)S(1)}, bf16[2,64,1792]{2,1,0:T(8,128)(2,1)S(1)}, bf16[2,64,1792]{2,1,0:T(8,128)(2,1)S(1)}, f32[2,64,1792]{2,1,0:T(8,128...) custom-call(s32[8]{0:T(128)S(1)} %copy-done, s32[8]{0:T(128)S(1)} %copy-done.1, f32[8,8,128]{2,1,0:T(8,128)S(1)} %add.16.refs_2_, ...), custom_call_target="tpu_custom_call" | custom-call | tf_op jit(solution)/shard_map/prepare/pallas_call | solution.py:346
  18.8 1.2 %all-to-all-done.rows_ref = f32[8,8,1024]{2,1,0:T(8,128)S(1)} async-done(((f32[8,8,1024]{2,1,0:T(8,128)}), f32[8,8,1024]{2,1,0:T(8,128)S(1)}, u32[]{:S(2)}, u32[]{:S(2)}) %all-to-all-start) | async-done | bytes 262176 | tf_op jit(solution)/shard_map/all_to_all | solution.py:342
  20.0 0.3 select.1.refs_7_
  20.3 1.6 %collective-permute-start.5 = (f32[4,8,896]{2,1,0:T(8,128)S(1)}, f32[4,8,896]{2,1,0:T(8,128)S(1)}, u32[]{:S(2)}, u32[]{:S(2)}) collective-permute-start(f32[4,8,896]{2,1,0:T(8,128)S(1)} %select.1.refs_7_), channel_id=1, source_target_pairs={{0,16},{8,24},{16,0},{24,8},{1,17},{9,25},{17,1},{25,9},{2,18},{10... | collective-permute-start | bytes 344072 | tf_op jit(solution)/shard_map/ppermute | solution.py:318
  21.9 0.5 %collective-permute-start.3 = (f32[8,8,128]{2,1,0:T(8,128)S(1)}, f32[8,8,128]{2,1,0:T(8,128)S(1)}, u32[]{:S(2)}, u32[]{:S(2)}) collective-permute-start(f32[8,8,128]{2,1,0:T(8,128)S(1)} %slice.4), channel_id=1, source_target_pairs={{0,16},{8,24},{16,0},{24,8},{1,17},{9,25},{17,1},{25,9},{2,18},{10... | collective-permute-start | bytes 98312 | tf_op jit(solution)/shard_map/ppermute | solution.py:318
  22.4 0.0 collective-permute-start.4
  22.4 1.6 %collective-permute-start.2 = (f32[8,8,128]{2,1,0:T(8,128)S(1)}, f32[8,8,128]{2,1,0:T(8,128)S(1)}, u32[]{:S(2)}, u32[]{:S(2)}) collective-permute-start(f32[8,8,128]{2,1,0:T(8,128)S(1)} %slice.4), channel_id=1, source_target_pairs={{0,8},{8,0},{16,24},{24,16},{1,9},{9,1},{17,25},{25,17},{2,10},{10... | collective-permute-start | bytes 98312 | tf_op jit(solution)/shard_map/ppermute | solution.py:318
  24.0 0.0 collective-permute-start.6
  24.0 1.1 %collective-permute-done.5.refs_8_ = f32[4,8,896]{2,1,0:T(8,128)S(1)} collective-permute-done((f32[4,8,896]{2,1,0:T(8,128)S(1)}, f32[4,8,896]{2,1,0:T(8,128)S(1)}, u32[]{:S(2)}, u32[]{:S(2)}) %collective-permute-start.5) | collective-permute-done | bytes 114720 | tf_op jit(solution)/shard_map/ppermute | solution.py:318
  25.1 0.0 collective-permute-start.7
  25.1 0.9 %collective-permute-done.3 = f32[8,8,128]{2,1,0:T(8,128)S(1)} collective-permute-done((f32[8,8,128]{2,1,0:T(8,128)S(1)}, f32[8,8,128]{2,1,0:T(8,128)S(1)}, u32[]{:S(2)}, u32[]{:S(2)}) %collective-permute-start.3) | collective-permute-done | bytes 32800 | tf_op jit(solution)/shard_map/ppermute | solution.py:318
  26.1 0.0 collective-permute-done.4
  26.1 0.0 collective-permute-done.2
  26.1 0.0 collective-permute-done.6.refs_9_
  26.1 0.4 %collective-permute-done.7.refs_10_ = f32[4,8,896]{2,1,0:T(8,128)S(1)} collective-permute-done((f32[4,8,896]{2,1,0:T(8,128)S(1)}, f32[4,8,896]{2,1,0:T(8,128)S(1)}, u32[]{:S(2)}, u32[]{:S(2)}) %collective-permute-start.7) | collective-permute-done | bytes 114720 | tf_op jit(solution)/shard_map/ppermute | solution.py:318
  26.5 1.9 %final.1 = (f32[2,64,1792]{2,1,0:T(8,128)}, f32[2,64,1792]{2,1,0:T(8,128)}, f32[8,8,1792]{2,1,0:T(8,128)}) custom-call(s32[8]{0:T(128)} %refs_0_.3, s32[8]{0:T(128)} %refs_1_.3, f32[8,8,128]{2,1,0:T(8,128)S(1)} %add_add_fusion.refs_2_, bf16[2,64,1792]{2,1,0:T(8,128)(2,1)S(1)} %get-tuple-element.14.refs_3_, ...), custom_call_target="tpu_custom_call" | custom-call | tf_op jit(solution)/shard_map/final/pallas_call | solution.py:393
  (5 shorter events, 0.0 us)
Async XLA Ops:
  0.6 15.6 %copy-start = (s32[8]{0:T(128)S(1)}, s32[8]{0:T(128)}, u32[]{:S(2)}) copy-start(s32[8]{0:T(128)} %refs_0_.3) | copy-start | bytes 100
  0.6 15.6 %copy-start.1 = (s32[8]{0:T(128)S(1)}, s32[8]{0:T(128)}, u32[]{:S(2)}) copy-start(s32[8]{0:T(128)} %refs_1_.3) | copy-start | bytes 100
  3.8 16.2 %all-to-all-start = ((f32[8,8,1024]{2,1,0:T(8,128)}), f32[8,8,1024]{2,1,0:T(8,128)S(1)}, u32[]{:S(2)}, u32[]{:S(2)}) async-start(f32[8,8,1024]{2,1,0:T(8,128)} %get-tuple-element.11), calls=%async_computation | async-start | bytes 524288 | tf_op jit(solution)/shard_map/all_to_all | solution.py:342
  11.1 1.2 %collective-permute-start = (f32[8,8,128]{2,1,0:T(8,128)S(1)}, f32[8,8,128]{2,1,0:T(8,128)S(1)}, u32[]{:S(2)}, u32[]{:S(2)}) collective-permute-start(f32[8,8,128]{2,1,0:T(8,128)S(1)} %get-tuple-element.12), channel_id=1, source_target_pairs={{0,8},{8,0},{16,24},{24,16},{1,9},{9,1},{17,25},{25,17},{2,10},{10... | collective-permute-start | bytes 98312 | tf_op jit(solution)/shard_map/ppermute | solution.py:318
  12.3 3.9 %collective-permute-start.1 = (f32[8,8,128]{2,1,0:T(8,128)S(1)}, f32[8,8,128]{2,1,0:T(8,128)S(1)}, u32[]{:S(2)}, u32[]{:S(2)}) collective-permute-start(f32[8,8,128]{2,1,0:T(8,128)S(1)} %add.15), channel_id=1, source_target_pairs={{0,16},{8,24},{16,0},{24,8},{1,17},{9,25},{17,1},{25,9},{2,18},{10... | collective-permute-start | bytes 98312 | tf_op jit(solution)/shard_map/ppermute | solution.py:318
  20.3 4.9 %collective-permute-start.5 = (f32[4,8,896]{2,1,0:T(8,128)S(1)}, f32[4,8,896]{2,1,0:T(8,128)S(1)}, u32[]{:S(2)}, u32[]{:S(2)}) collective-permute-start(f32[4,8,896]{2,1,0:T(8,128)S(1)} %select.1.refs_7_), channel_id=1, source_target_pairs={{0,16},{8,24},{16,0},{24,8},{1,17},{9,25},{17,1},{25,9},{2,18},{10... | collective-permute-start | bytes 344072 | tf_op jit(solution)/shard_map/ppermute | solution.py:318
  21.9 4.2 %collective-permute-start.3 = (f32[8,8,128]{2,1,0:T(8,128)S(1)}, f32[8,8,128]{2,1,0:T(8,128)S(1)}, u32[]{:S(2)}, u32[]{:S(2)}) collective-permute-start(f32[8,8,128]{2,1,0:T(8,128)S(1)} %slice.4), channel_id=1, source_target_pairs={{0,16},{8,24},{16,0},{24,8},{1,17},{9,25},{17,1},{25,9},{2,18},{10... | collective-permute-start | bytes 98312 | tf_op jit(solution)/shard_map/ppermute | solution.py:318
  22.4 3.7 %collective-permute-start.4 = (f32[8,8,128]{2,1,0:T(8,128)S(1)}, f32[8,8,128]{2,1,0:T(8,128)S(1)}, u32[]{:S(2)}, u32[]{:S(2)}) collective-permute-start(f32[8,8,128]{2,1,0:T(8,128)S(1)} %slice.4), channel_id=1, source_target_pairs={{0,24},{8,16},{16,8},{24,0},{1,25},{9,17},{17,9},{25,1},{2,26},{10... | collective-permute-start | bytes 98312 | tf_op jit(solution)/shard_map/ppermute | solution.py:318
  22.4 3.7 %collective-permute-start.2 = (f32[8,8,128]{2,1,0:T(8,128)S(1)}, f32[8,8,128]{2,1,0:T(8,128)S(1)}, u32[]{:S(2)}, u32[]{:S(2)}) collective-permute-start(f32[8,8,128]{2,1,0:T(8,128)S(1)} %slice.4), channel_id=1, source_target_pairs={{0,8},{8,0},{16,24},{24,16},{1,9},{9,1},{17,25},{25,17},{2,10},{10... | collective-permute-start | bytes 98312 | tf_op jit(solution)/shard_map/ppermute | solution.py:318
  24.0 2.1 %collective-permute-start.6 = (f32[4,8,896]{2,1,0:T(8,128)S(1)}, f32[4,8,896]{2,1,0:T(8,128)S(1)}, u32[]{:S(2)}, u32[]{:S(2)}) collective-permute-start(f32[4,8,896]{2,1,0:T(8,128)S(1)} %select.1.refs_7_), channel_id=1, source_target_pairs={{0,8},{8,0},{16,24},{24,16},{1,9},{9,1},{17,25},{25,17},{2,10},{10... | collective-permute-start | bytes 344072 | tf_op jit(solution)/shard_map/ppermute | solution.py:318
  25.1 1.3 %collective-permute-start.7 = (f32[4,8,896]{2,1,0:T(8,128)S(1)}, f32[4,8,896]{2,1,0:T(8,128)S(1)}, u32[]{:S(2)}, u32[]{:S(2)}) collective-permute-start(f32[4,8,896]{2,1,0:T(8,128)S(1)} %collective-permute-done.5.refs_8_), channel_id=1, source_target_pairs={{0,8},{8,0},{16,24},{24,16},{1,9},{9,1},{17,25},{25,17},{2,10},{10... | collective-permute-start | bytes 344072 | tf_op jit(solution)/shard_map/ppermute | solution.py:318

commit v8 on v7

--- a/solution.py
+++ b/solution.py
@@ -1,3 +1,4 @@
+import functools
 import math
 
 import jax
@@ -53,6 +54,15 @@
     for earlier in range(block):
         slot = slot + jnp.where(owner_ref[earlier] == owner, 1, 0)
     return owner, slot
+
+
+def shared(places, block):
+    owner, _ = places[block]
+    held, before = jnp.int32(0), jnp.int32(0)
+    for other_owner, other_slot in places:
+        held = held + jnp.where(other_owner == owner, 1, 0)
+        before = before + jnp.where((other_slot == 1) & (other_owner < owner), 1, 0)
+    return held == 2, before
 
 
 def outset_kernel(
@@ -86,16 +96,21 @@
     for load in loads[1 + layers:]:
         load.wait()
     upper = lax.broadcasted_iota(jnp.int32, (rows, columns), 0) < rows // 2
+    me = lax.axis_index("own")
+    held = jnp.int32(0)
+    for block in range(blocks):
+        held = held + jnp.where(owner_smem[block] == me, 1, 0)
     for owner in range(owners):
         here = pl.ds(owner * rows, rows)
         first, second = [
             w_ref[slot, here, :] - carried * m_ref[slot, here, :] for slot in range(2)
         ]
-        made_ref[owner, :, :columns] = jnp.where(
+        halves = jnp.where(
             across == 0,
             jnp.where(upper, first, pltpu.roll(second, rows // 2, 0)),
             jnp.where(upper, pltpu.roll(first, rows // 2, 0), second),
         )
+        made_ref[owner, :, :columns] = jnp.where(held == 2, halves, first)
     early = pltpu.make_async_copy(
         made_ref.at[:, :, :columns], sent_ref.at[:, :, :columns], out_sems.at[0]
     )
@@ -131,14 +146,13 @@
 
 def prepare_kernel(
     reps, owner_ref, layer_ref, coeffs_ref, basis_ref, momentum_ref, weights_ref,
-    grad_ref, high_ref, low_ref, held_ref, first_ref, marks_ref,
+    grad_ref, high_ref, low_ref, held_ref, first_ref, marks_ref, codes_ref,
     wide_ref, basis_vmem, slot_vmem, sems,
 ):
-    pairs, rows, columns = grad_ref.shape
+    owners, rows, columns = grad_ref.shape
     blocks = owner_ref.shape[0]
     layers, rank, width = basis_ref.shape
     slots = momentum_ref.shape[0]
-    places = coeffs_ref.shape[0] * slots
     me = lax.axis_index("own")
     core, across = position()
     part = pl.ds(pl.multiple_of(core * columns, 128), columns)
@@ -154,26 +168,36 @@
         load.start()
     lane = lax.broadcasted_iota(jnp.int32, (rows, 2 * rank), 1)
     wide_lane = lax.broadcasted_iota(jnp.int32, (rows, layers * rank), 1)
-    place_row = lax.broadcasted_iota(jnp.int32, (places, marks_ref.shape[1]), 0)
-    upper = lax.broadcasted_iota(jnp.int32, (rows, layers * rank), 0) < rows // 2
-    for pair in range(pairs):
-        parts = []
-        for odd in range(2):
-            block = 2 * pair + odd
-            owner, slot = place_of(owner_ref, block)
-            both = jnp.where(lane // rank == slot, coeffs_ref[owner], 0.0)
-            both = both + pltpu.roll(both, rank, 1)
-            wide = jnp.concatenate([both] * (layers // 2), axis=1)
-            wide = jnp.where(wide_lane // rank == layer_ref[block], wide, 0.0)
-            parts.append(jnp.where(across == odd, wide, pltpu.roll(wide, rows // 2, 0)))
-            marks_ref[pl.ds(block * places, places), :] = jnp.where(
-                place_row == owner * slots + slot, 1.0, 0.0
+    half = lax.broadcasted_iota(jnp.int32, (rows, layers * rank), 0) // (rows // 2)
+    wide_ref[...] = jnp.zeros_like(wide_ref)
+    marks_ref[...] = jnp.zeros_like(marks_ref)
+    places = [place_of(owner_ref, block) for block in range(blocks)]
+    for block in range(blocks):
+        owner, slot = places[block]
+        two, before = shared(places, block)
+        both = jnp.where(lane // rank == slot, coeffs_ref[owner], 0.0)
+        both = both + pltpu.roll(both, rank, 1)
+        wide = jnp.concatenate([both] * (layers // 2), axis=1)
+        wide = jnp.where(wide_lane // rank == layer_ref[block], wide, 0.0)
+        codes_ref[4 * block] = owner
+        codes_ref[4 * block + 1] = slot
+        codes_ref[4 * block + 2] = jnp.where(two, 1, 0)
+        codes_ref[4 * block + 3] = jnp.where(two, before, 0)
+        halves = jnp.where(slot == across, wide, pltpu.roll(wide, rows // 2, 0))
+        halves = jnp.where(half == slot, halves, 0.0)
+        wide_ref[owner] = wide_ref[owner] + jnp.where(two, halves, wide)
+
+        @pl.when(slot == 1)
+        def _():
+            marks_ref[pl.ds(before * owners + owner, 1), :] = jnp.ones(
+                (1, marks_ref.shape[1]), jnp.float32
             )
-        wide_ref[pl.ds(pair * rows, rows), :] = jnp.where(upper, parts[0], parts[1])
+
     loads[0].wait()
     high, low = split(basis_vmem[...].reshape(layers * rank, columns))
-    grad = product(wide_ref[...] * (total_rate / reps), high, low)
-    grad_ref[...] = grad.reshape(pairs, rows, columns)
+    wide = wide_ref[...].reshape(owners * rows, layers * rank)
+    grad = product(wide * (total_rate / reps), high, low)
+    grad_ref[...] = grad.reshape(owners, rows, columns)
     for slot in range(slots):
         loads[1 + slot].wait()
         slot_high, slot_low = split(slot_vmem[slot])
@@ -182,6 +206,7 @@
     loads[-2].wait()
     loads[-1].wait()
     for slot in range(slots):
+        codes_ref[4 * blocks + slot] = found[slot][0]
 
         @pl.when(found[slot][0] == 0)
         def _():
@@ -192,29 +217,22 @@
                 first_ref[...] = jnp.zeros_like(first_ref)
 
 
-def select_kernel(near_ref, grad_ref, marks_ref, chosen_ref):
-    pairs, rows, columns = chosen_ref.shape
-    owners = near_ref.shape[0]
+def select_kernel(near_ref, grad_ref, marks_ref, new_ref, given_ref):
+    owners, rows, columns = new_ref.shape
     lanes = marks_ref.shape[1]
-    upper = lax.broadcasted_iota(jnp.int32, (rows, columns), 0) < rows // 2
-
-    def one(pair, carry):
-        parts = []
-        for odd in range(2):
-            first = (2 * pair + odd) * 2 * owners
-            sums = []
-            for slot in range(2):
-                total = jnp.zeros((rows, columns), jnp.float32)
-                for owner in range(owners):
-                    mark = marks_ref[pl.ds(first + 2 * owner + slot, 1), :]
-                    mark = jnp.concatenate([mark] * (columns // lanes), axis=1)
-                    total = total + mark * near_ref[owner, :, :columns]
-                sums.append(total)
-            parts.append(sums[odd] + pltpu.roll(sums[1 - odd], rows // 2, 0))
-        chosen_ref[pair] = jnp.where(upper, parts[0], parts[1]) - grad_ref[pair]
+    for owner in range(owners):
+        new_ref[owner] = near_ref[owner, :, :columns] - grad_ref[owner]
+
+    def one(place, carry):
+        total = jnp.zeros((rows, columns), jnp.float32)
+        for owner in range(owners):
+            mark = marks_ref[pl.ds(place * owners + owner, 1), :]
+            mark = jnp.concatenate([mark] * (columns // lanes), axis=1)
+            total = total + mark * new_ref[owner]
+        given_ref[place] = total
         return carry
 
-    lax.fori_loop(0, pairs, one, 0, unroll=pairs <= 4)
+    lax.fori_loop(0, given_ref.shape[0], one, 0, unroll=given_ref.shape[0] <= 4)
 
 
 def after_kernel(rows_ref, done_ref, same_ref):
@@ -222,26 +240,26 @@
 
 
 def final_kernel(
-    reps, owner_ref, layer_ref, coeffs_ref, high_ref, low_ref, momentum_ref, first_ref,
+    reps, codes_ref, coeffs_ref, high_ref, low_ref, momentum_ref, first_ref,
     near_ref, near_across_ref, far_ref, far_across_ref, weights_ref,
     new_weights_ref, new_momentum_ref, replica_ref,
-    owner_smem, layer_smem, w_ref, m_ref, change_ref, rows_ref, in_sems, out_sems, rows_sem,
+    codes_smem, w_ref, m_ref, change_ref, rows_ref, in_sems, out_sems, rows_sem,
 ):
     slots, rows, width = weights_ref.shape
     rank = high_ref.shape[1]
-    pairs, tile, columns = near_ref.shape
-    me = lax.axis_index("own")
+    blocks = replica_ref.shape[0]
+    _, tile, columns = near_ref.shape
     core, across = position()
-    sources = [(owner_ref, owner_smem), (layer_ref, layer_smem)]
-    sources += [(weights_ref.at[slot], w_ref.at[slot]) for slot in range(1, slots)]
+    sources = [(weights_ref.at[slot], w_ref.at[slot]) for slot in range(1, slots)]
+    sources.append((codes_ref, codes_smem))
     loads = [
         pltpu.make_async_copy(source, target, in_sems.at[index])
         for index, (source, target) in enumerate(sources)
     ]
     for load in loads:
         load.start()
+    averaged = coeffs_ref[...].reshape(rows, slots * rank) * (1.0 / reps)
     stores = []
-    averaged = coeffs_ref[...].reshape(rows, slots * rank) * (1.0 / reps)
 
     def send(source, target, slot, which):
         store = pltpu.make_async_copy(source.at[slot], target.at[slot], out_sems.at[slot, which])
@@ -261,35 +279,39 @@
             send(w_ref, new_weights_ref, 0, 1)
         else:
             change_ref[slot] = change
-    upper = lax.broadcasted_iota(jnp.int32, (tile, columns), 0) < tile // 2
+    loads[-1].wait()
+    half = lax.broadcasted_iota(jnp.int32, (tile, columns), 0) // (tile // 2)
     for near_core in range(2):
-        for near_across in range(2):
-
-            @pl.when((core == near_core) & (across == near_across))
-            def _():
-                for side, sources in (
-                    (near_core, (near_ref, near_across_ref)),
-                    (1 - near_core, (far_ref, far_across_ref)),
+
+        @pl.when(core == near_core)
+        def _():
+            for block in range(blocks):
+                owner, slot = codes_smem[4 * block], codes_smem[4 * block + 1]
+                two, place = codes_smem[4 * block + 2] == 1, codes_smem[4 * block + 3]
+                for side, whole, other in (
+                    (near_core, near_ref, near_across_ref),
+                    (1 - near_core, far_ref, far_across_ref),
                 ):
-                    top, bottom = sources if near_across == 0 else sources[::-1]
-                    here = pl.ds(side * columns, columns)
-                    for pair in range(pairs):
-                        above, below = top[pair], bottom[pair]
-                        rows_ref[2 * pair, :, here] = jnp.where(
-                            upper, above, pltpu.roll(below, tile // 2, 0)
-                        )
-                        rows_ref[2 * pair + 1, :, here] = jnp.where(
-                            upper, pltpu.roll(above, tile // 2, 0), below
-                        )
+                    here = slice(side * columns, (side + 1) * columns)
+
+                    @pl.when(jnp.logical_not(two))
+                    def _():
+                        rows_ref[block, :, here] = whole[owner]
+
+                    @pl.when(two)
+                    def _():
+                        mine, theirs = whole[owner], other[place]
+                        keep = slot == across
+                        mine = jnp.where(keep, mine, pltpu.roll(mine, tile // 2, 0))
+                        theirs = jnp.where(keep, pltpu.roll(theirs, tile // 2, 0), theirs)
+                        rows_ref[block, :, here] = jnp.where(half == across, mine, theirs)
 
     store = pltpu.make_async_copy(rows_ref, replica_ref, rows_sem)
     store.start()
     stores.append(store)
-    for load in loads[:2]:
-        load.wait()
     for slot in range(1, slots):
-        used, _ = held_by(me, slot, owner_smem, layer_smem)
-        loads[1 + slot].wait()
+        loads[slot - 1].wait()
+        used = codes_smem[4 * blocks + slot]
         w_ref[slot] = jnp.where(used == 1, w_ref[slot] - change_ref[slot], 0.0)
         send(w_ref, new_weights_ref, slot, 1)
     for store in stores:
@@ -343,20 +365,22 @@
 
     coeffs = coeffs + swap(coeffs, 1)
     coeffs = coeffs + swap(coeffs, 2)
-    grad, high, low, held, first, marks = pl.pallas_call(
+    most = blocks // 2
+    grad, high, low, held, first, marks, codes = pl.pallas_call(
         lambda *refs: prepare_kernel(rep_count, *refs),
         out_shape=[
-            shape((blocks // 2, rows, columns), f32),
+            shape((own_count, rows, columns), f32),
             shape((slots, rank, width), bf16),
             shape((slots, rank, width), bf16),
             shape(momentum_owned.shape, f32),
             shape(weights_owned.shape[1:], f32),
-            shape((blocks * own_count * slots, 128), f32),
+            shape((most * own_count, 128), f32),
+            shape((4 * blocks + slots,), jnp.int32),
         ],
         in_specs=[SMEM, SMEM, VMEM, HBM, HBM, HBM],
-        out_specs=[VMEM] * 6,
+        out_specs=[VMEM] * 6 + [SMEM],
         scratch_shapes=[
-            pltpu.VMEM((blocks // 2 * rows, layers * rank), f32),
+            pltpu.VMEM((own_count, rows, layers * rank), f32),
             pltpu.VMEM((layers, rank, columns), f32),
             pltpu.VMEM((slots, rank, width), f32),
             pltpu.SemaphoreType.DMA((3 + slots,)),
@@ -377,46 +401,58 @@
         )(array, done)
 
     near = after(near, grad)
-    partial = near[:, :, columns:]
-    partial = (partial + swap(partial, 1)) + (swap(partial, 2) + swap(partial, 3))
-    chosen = pl.pallas_call(
+    new, given = pl.pallas_call(
         select_kernel,
-        out_shape=shape((blocks // 2, rows, columns), f32),
+        out_shape=[
+            shape((own_count, rows, columns), f32),
+            shape((most, rows, columns), f32),
+        ],
         in_specs=[VMEM] * 3,
-        out_specs=VMEM,
-        compiler_params=params(near, near, marks),
+        out_specs=[VMEM] * 2,
+        compiler_params=params(near, near, near, marks),
         name="select",
     )(near, grad, marks)
-    far = swap(chosen, 1)
-    near_across = swap(chosen, 2)
-    far_across = swap(near_across, 1)
-    new_weights, new_momentum, replica_weights = pl.pallas_call(
-        lambda *refs: final_kernel(rep_count, *refs),
-        out_shape=[
-            shape(weights_owned.shape, f32),
-            shape(weights_owned.shape, f32),
-            shape((blocks, rows, width), f32),
-        ],
-        in_specs=[HBM, HBM] + [VMEM] * 9 + [HBM],
-        out_specs=[HBM] * 3,
-        scratch_shapes=[
-            pltpu.SMEM(owner_of.shape, jnp.int32),
-            pltpu.SMEM(layer_of.shape, jnp.int32),
-            pltpu.VMEM(weights_owned.shape, f32),
-            pltpu.VMEM(weights_owned.shape, f32),
-            pltpu.VMEM(weights_owned.shape, f32),
-            pltpu.VMEM((blocks, rows, width), f32),
-            pltpu.SemaphoreType.DMA((1 + slots,)),
-            pltpu.SemaphoreType.DMA((slots, 2)),
-            pltpu.SemaphoreType.DMA(()),
-        ],
-        compiler_params=params(basis, weights_owned, weights_owned, weights_owned, replica_delta),
-        name="final",
-    )(
-        stay(owner_of), stay(layer_of), partial, high, low, held, first,
-        chosen, near_across, far, far_across, weights,
-    )
-    return (new_weights, new_momentum, replica_weights)
+
+    def finish(count, codes, near, new, given, high, low, held, first, weights_owned):
+        partial = near[:, :, columns:]
+        partial = (partial + swap(partial, 1)) + (swap(partial, 2) + swap(partial, 3))
+        far = swap(new, 1)
+        near_across = swap(given[:count], 2)
+        far_across = swap(near_across, 1)
+        return pl.pallas_call(
+            lambda *refs: final_kernel(rep_count, *refs),
+            out_shape=[
+                shape(weights_owned.shape, f32),
+                shape(weights_owned.shape, f32),
+                shape((blocks, rows, width), f32),
+            ],
+            in_specs=[HBM] + [VMEM] * 9 + [HBM],
+            out_specs=[HBM] * 3,
+            scratch_shapes=[
+                pltpu.SMEM(codes.shape, jnp.int32),
+                pltpu.VMEM(weights_owned.shape, f32),
+                pltpu.VMEM(weights_owned.shape, f32),
+                pltpu.VMEM(weights_owned.shape, f32),
+                pltpu.VMEM((blocks, rows, width), f32),
+                pltpu.SemaphoreType.DMA((slots,)),
+                pltpu.SemaphoreType.DMA((slots, 2)),
+                pltpu.SemaphoreType.DMA(()),
+            ],
+            compiler_params=params(basis, *[weights_owned] * 3, replica_delta, replica_delta),
+            name="final",
+        )(
+            stay(codes), partial, high, low, held, first,
+            new, near_across, far, far_across, stay(weights_owned),
+        )
+
+    pairs = jnp.sum(owner_of[:, None] == owner_of[None, :], dtype=jnp.int32) - blocks
+    unit = max(1, most // 4)
+    counts = [min(most, unit * (index + 1)) for index in range(-(-most // unit))]
+    return tuple(lax.switch(
+        (pairs // 2 + unit - 1) // unit - 1,
+        [functools.partial(finish, count) for count in counts],
+        codes, near, new, given, high, low, held, first, weights_owned,
+    ))
 
 
 def solution(mesh):

time: 28.7 us -> 29.7 us (1.035)
  waiting for transfers between devices: 7.26 us -> 6.46 us
  other arithmetic: 0.02 us -> 0.72 us
  between operations: 0.7 us -> 1.36 us
  Pallas kernels: 7.89 us -> 8.36 us
    reduce_sum x0 -> x1, other arithmetic: none -> 0.7 us  [local(): jnp.sum(owner_of[:, None] == owner_of[None, :], dtype=jnp.int32) - blocks]
    pallas_call x1, Pallas kernels: 2.56 us -> 3.11 us  [local(): pl.pallas_call(lambda *refs: prepare_kernel(rep_count, *refs), out_shape=...]
    all_to_all x1, waiting for transfers between devices: 1.2 us -> 0.66 us  [local(): near = lax.all_to_all(sent, 'own', split_axis=0, concat_axis=0, tiled=True)]
  transfers between devices with their start and end apart: 9 -> 9, of which waited for: 6 -> 5; matrix products, arithmetic and copies ran while one was open for 0% -> 2% of each run, Pallas kernels for 9% -> 11%
where the time goes in v8:
time: 29.7 us; the launch traced here: 29.5 us
  starting transfers between devices  12.5 us (42%)
  Pallas kernels  8.36 us (28%)
  waiting for transfers between devices  6.46 us (22%)
  between operations  1.36 us (5%)
  other arithmetic  0.72 us (2%)
    all_to_all x1, starting transfers between devices, local(): near = lax.all_to_all(sent, 'own', split_axis=0, concat_axis=0, tiled=True)  7.29 us
    ppermute x8, waiting for transfers between devices, swap(): return lax.ppermute(array, 'rep', pairs)  5.79 us
    ppermute x8, starting transfers between devices, swap(): return lax.ppermute(array, 'rep', pairs)  5.2 us
    pallas_call x1, Pallas kernels, local(): pl.pallas_call(outset_kernel, out_shape=[shape((own_count, rows, total),...  3.16 us
    pallas_call x1, Pallas kernels, local(): pl.pallas_call(lambda *refs: prepare_kernel(rep_count, *refs), out_shape=...  3.11 us
    pallas_call x1, Pallas kernels, finish(): pl.pallas_call(lambda *refs: final_kernel(rep_count, *refs), out_shape=[s...  2 us
    reduce_sum x1, other arithmetic, local(): jnp.sum(owner_of[:, None] == owner_of[None, :], dtype=jnp.int32) - blocks  0.7 us
    all_to_all x1, waiting for transfers between devices, local(): near = lax.all_to_all(sent, 'own', split_axis=0, concat_axis=0, tiled=True)  0.66 us
  transfers between devices with their start and end apart: 9, of which 5 were waited for; matrix products, arithmetic and copies ran while one was open for 2% of the time, Pallas kernels for 11%

profile of v8, /device:TPU:0, one launch (start us, length us, event | category | flops | bytes accessed | tf_op | source)
XLA Modules:
  0.0 29.5 jit_solution(797321980282031191)
XLA Ops:
  0.6 0.0 copy-start
  0.6 0.0 copy-start.1
  0.7 3.2 %outset.1 = (f32[8,8,1024]{2,1,0:T(8,128)}, f32[8,8,128]{2,1,0:T(8,128)S(1)}) custom-call(s32[8]{0:T(128)} %refs_0_.1, s32[8]{0:T(128)} %refs_1_.1, f32[8,8,1792]{2,1,0:T(8,128)} %bitcast.4, f32[4,64,1792]{2,1,0:T(8,128)} %bitcast.2, f32[2,64,1792]{2,1,0:T(8,128)} %refs_5_.1, f32[2,64,1792]{2,1,0:T(8,128)} %refs_4_.1), custom_call_target="tpu_custom_call" | custom-call | tf_op jit(solution)/shard_map/outset/pallas_call | solution.py:342
  3.8 7.3 %all-to-all-start = ((f32[8,8,1024]{2,1,0:T(8,128)}), f32[8,8,1024]{2,1,0:T(8,128)S(1)}, u32[]{:S(2)}, u32[]{:S(2)}) async-start(f32[8,8,1024]{2,1,0:T(8,128)} %get-tuple-element.122), calls=%async_computation | async-start | bytes 524288 | tf_op jit(solution)/shard_map/all_to_all | solution.py:364
  11.1 0.0 collective-permute-start.24
  11.1 1.2 %collective-permute-done.24 = f32[8,8,128]{2,1,0:T(8,128)S(1)} collective-permute-done((f32[8,8,128]{2,1,0:T(8,128)S(1)}, f32[8,8,128]{2,1,0:T(8,128)S(1)}, u32[]{:S(2)}, u32[]{:S(2)}) %collective-permute-start.24) | collective-permute-done | bytes 32800 | tf_op jit(solution)/shard_map/ppermute | solution.py:340
  12.3 1.5 %collective-permute-start.25 = (f32[8,8,128]{2,1,0:T(8,128)S(1)}, f32[8,8,128]{2,1,0:T(8,128)S(1)}, u32[]{:S(2)}, u32[]{:S(2)}) collective-permute-start(f32[8,8,128]{2,1,0:T(8,128)S(1)} %add.50), channel_id=1, source_target_pairs={{0,16},{8,24},{16,0},{24,8},{1,17},{9,25},{17,1},{25,9},{2,18},{10... | collective-permute-start | bytes 98312 | tf_op jit(solution)/shard_map/ppermute | solution.py:340
  13.8 0.0 copy-done
  13.8 0.7 %convert_reduce_fusion = s32[]{:T(128)} fusion(s32[8]{0:T(128)S(1)} %copy-done), kind=kLoop, calls=%fused_computation.4 | loop fusion | flops 191 | bytes 36 | tf_op jit(solution)/shard_map/reduce_sum | solution.py:448
  15.2 1.0 %collective-permute-done.25 = f32[8,8,128]{2,1,0:T(8,128)S(1)} collective-permute-done((f32[8,8,128]{2,1,0:T(8,128)S(1)}, f32[8,8,128]{2,1,0:T(8,128)S(1)}, u32[]{:S(2)}, u32[]{:S(2)}) %collective-permute-start.25) | collective-permute-done | bytes 32800 | tf_op jit(solution)/shard_map/ppermute | solution.py:340
  16.2 0.0 copy-done.1
  16.3 3.1 %prepare.1 = (f32[8,8,896]{2,1,0:T(8,128)S(1)}, bf16[2,64,1792]{2,1,0:T(8,128)(2,1)S(1)}, bf16[2,64,1792]{2,1,0:T(8,128)(2,1)S(1)}, f32[2,64,1792]{2,1,0:T(8,128...) custom-call(s32[8]{0:T(128)S(1)} %copy-done, s32[8]{0:T(128)S(1)} %copy-done.1, ...), custom_call_target="tpu_custom_call" | custom-call | tf_op jit(solution)/shard_map/prepare/pallas_call | solution.py:369
  19.4 0.7 %all-to-all-done.rows_ref = f32[8,8,1024]{2,1,0:T(8,128)S(1)} async-done(((f32[8,8,1024]{2,1,0:T(8,128)}), f32[8,8,1024]{2,1,0:T(8,128)S(1)}, u32[]{:S(2)}, u32[]{:S(2)}) %all-to-all-start) | async-done | bytes 262176 | tf_op jit(solution)/shard_map/all_to_all | solution.py:364
  20.0 0.1 select.7
  20.1 9.3 %conditional.1 = ((f32[2,64,1792]{2,1,0:T(8,128)}, f32[2,64,1792]{2,1,0:T(8,128)}, f32[8,8,1792]{2,1,0:T(8,128)})) conditional(s32[]{:T(128)} %clamp.3, (f32[8,8,1024]{2,1,0:T(8,128)S(1)}, f32[4,8,896]{2,1,0:T(8,128)S(1)}, f32[8,8,896]{2,1,0:T(8,128)S(1)}, s32[34]{0:T(128)}, bf16[2,64,1792]{2,1,0:T(8,128)(2,1)S(1)}, ...), branch_computations={%region_1.2_spmd, %region_2.3_spmd, %region_3.4_spmd, %region_4.5_... | conditional | flops 24576 | bytes 2457848 | solution.py:451
  20.2 1.6 %collective-permute-start.1 = (f32[8,8,128]{2,1,0:T(8,128)S(1)}, f32[8,8,128]{2,1,0:T(8,128)S(1)}, u32[]{:S(2)}, u32[]{:S(2)}) collective-permute-start(f32[8,8,128]{2,1,0:T(8,128)S(1)} %slice.14), channel_id=1, source_target_pairs={{0,16},{8,24},{16,0},{24,8},{1,17},{9,25},{17,1},{25,9},{2,18},{10... | collective-permute-start | bytes 98312 | tf_op jit(solution)/shard_map/cond/branch_0_fun/ppermute | solution.py:340
  21.7 0.0 collective-permute-start.2
  21.7 0.6 %collective-permute-start = (f32[8,8,128]{2,1,0:T(8,128)S(1)}, f32[8,8,128]{2,1,0:T(8,128)S(1)}, u32[]{:S(2)}, u32[]{:S(2)}) collective-permute-start(f32[8,8,128]{2,1,0:T(8,128)S(1)} %slice.14), channel_id=1, source_target_pairs={{0,8},{8,0},{16,24},{24,16},{1,9},{9,1},{17,25},{25,17},{2,10},{10... | collective-permute-start | bytes 98312 | tf_op jit(solution)/shard_map/cond/branch_0_fun/ppermute | solution.py:340
  22.4 1.5 %collective-permute-start.3 = (f32[1,8,896]{2,1,0:T(8,128)S(1)}, f32[1,8,896]{2,1,0:T(8,128)S(1)}, u32[]{:S(2)}, u32[]{:S(2)}) collective-permute-start(f32[1,8,896]{2,1,0:T(8,128)S(1)} %slice.15), channel_id=1, source_target_pairs={{0,16},{8,24},{16,0},{24,8},{1,17},{9,25},{17,1},{25,9},{2,18},{10... | collective-permute-start | bytes 86024 | tf_op jit(solution)/shard_map/cond/branch_0_fun/ppermute | solution.py:340
  23.9 0.0 collective-permute-start.4
  23.9 2.4 %collective-permute-done.3.refs_7_ = f32[1,8,896]{2,1,0:T(8,128)S(1)} collective-permute-done((f32[1,8,896]{2,1,0:T(8,128)S(1)}, f32[1,8,896]{2,1,0:T(8,128)S(1)}, u32[]{:S(2)}, u32[]{:S(2)}) %collective-permute-start.3) | collective-permute-done | bytes 28704 | tf_op jit(solution)/shard_map/cond/branch_0_fun/ppermute | solution.py:340
  26.2 0.0 collective-permute-start.5
  26.2 0.0 collective-permute-done.1
  26.2 0.0 collective-permute-done.2
  26.3 0.0 collective-permute-done
  26.3 1.2 %collective-permute-done.5.refs_9_ = f32[1,8,896]{2,1,0:T(8,128)S(1)} collective-permute-done((f32[1,8,896]{2,1,0:T(8,128)S(1)}, f32[1,8,896]{2,1,0:T(8,128)S(1)}, u32[]{:S(2)}, u32[]{:S(2)}) %collective-permute-start.5) | collective-permute-done | bytes 28704 | tf_op jit(solution)/shard_map/cond/branch_0_fun/ppermute | solution.py:340
  27.4 0.0 collective-permute-done.4.refs_8_
  27.4 2.0 %final.4 = (f32[2,64,1792]{2,1,0:T(8,128)}, f32[2,64,1792]{2,1,0:T(8,128)}, f32[8,8,1792]{2,1,0:T(8,128)}) custom-call(s32[34]{0:T(128)} %get-tuple-element.72.refs_0_, f32[8,8,128]{2,1,0:T(8,128)S(1)} %add_add_fusion.refs_1_, bf16[2,64,1792]{2,1,0:T(8,128)(2,1)S(1)} %get-tuple-element.74.refs_2_, bf16[2,64,1792]{2,1,0:T(8,128)(2,1)S(1)} %get-tuple-element.75.refs_3_, ...), custom_call_target="tpu_custom_call" | custom-call | tf_op jit(solution)/shard_map/cond/branch_0_fun/final/pallas_call | solution.py:422
  (6 shorter events, 0.0 us)
Async XLA Ops:
  0.6 13.2 %copy-start = (s32[8]{0:T(128)S(1)}, s32[8]{0:T(128)}, u32[]{:S(2)}) copy-start(s32[8]{0:T(128)} %refs_0_.1) | copy-start | bytes 100
  0.6 15.6 %copy-start.1 = (s32[8]{0:T(128)S(1)}, s32[8]{0:T(128)}, u32[]{:S(2)}) copy-start(s32[8]{0:T(128)} %refs_1_.1) | copy-start | bytes 100
  3.8 16.2 %all-to-all-start = ((f32[8,8,1024]{2,1,0:T(8,128)}), f32[8,8,1024]{2,1,0:T(8,128)S(1)}, u32[]{:S(2)}, u32[]{:S(2)}) async-start(f32[8,8,1024]{2,1,0:T(8,128)} %get-tuple-element.122), calls=%async_computation | async-start | bytes 524288 | tf_op jit(solution)/shard_map/all_to_all | solution.py:364
  11.1 1.2 %collective-permute-start.24 = (f32[8,8,128]{2,1,0:T(8,128)S(1)}, f32[8,8,128]{2,1,0:T(8,128)S(1)}, u32[]{:S(2)}, u32[]{:S(2)}) collective-permute-start(f32[8,8,128]{2,1,0:T(8,128)S(1)} %get-tuple-element.123), channel_id=1, source_target_pairs={{0,8},{8,0},{16,24},{24,16},{1,9},{9,1},{17,25},{25,17},{2,10},{10... | collective-permute-start | bytes 98312 | tf_op jit(solution)/shard_map/ppermute | solution.py:340
  12.3 3.9 %collective-permute-start.25 = (f32[8,8,128]{2,1,0:T(8,128)S(1)}, f32[8,8,128]{2,1,0:T(8,128)S(1)}, u32[]{:S(2)}, u32[]{:S(2)}) collective-permute-start(f32[8,8,128]{2,1,0:T(8,128)S(1)} %add.50), channel_id=1, source_target_pairs={{0,16},{8,24},{16,0},{24,8},{1,17},{9,25},{17,1},{25,9},{2,18},{10... | collective-permute-start | bytes 98312 | tf_op jit(solution)/shard_map/ppermute | solution.py:340
  20.2 6.1 %collective-permute-start.1 = (f32[8,8,128]{2,1,0:T(8,128)S(1)}, f32[8,8,128]{2,1,0:T(8,128)S(1)}, u32[]{:S(2)}, u32[]{:S(2)}) collective-permute-start(f32[8,8,128]{2,1,0:T(8,128)S(1)} %slice.14), channel_id=1, source_target_pairs={{0,16},{8,24},{16,0},{24,8},{1,17},{9,25},{17,1},{25,9},{2,18},{10... | collective-permute-start | bytes 98312 | tf_op jit(solution)/shard_map/cond/branch_0_fun/ppermute | solution.py:340
  21.7 4.5 %collective-permute-start.2 = (f32[8,8,128]{2,1,0:T(8,128)S(1)}, f32[8,8,128]{2,1,0:T(8,128)S(1)}, u32[]{:S(2)}, u32[]{:S(2)}) collective-permute-start(f32[8,8,128]{2,1,0:T(8,128)S(1)} %slice.14), channel_id=1, source_target_pairs={{0,24},{8,16},{16,8},{24,0},{1,25},{9,17},{17,9},{25,1},{2,26},{10... | collective-permute-start | bytes 98312 | tf_op jit(solution)/shard_map/cond/branch_0_fun/ppermute | solution.py:340
  21.7 4.5 %collective-permute-start = (f32[8,8,128]{2,1,0:T(8,128)S(1)}, f32[8,8,128]{2,1,0:T(8,128)S(1)}, u32[]{:S(2)}, u32[]{:S(2)}) collective-permute-start(f32[8,8,128]{2,1,0:T(8,128)S(1)} %slice.14), channel_id=1, source_target_pairs={{0,8},{8,0},{16,24},{24,16},{1,9},{9,1},{17,25},{25,17},{2,10},{10... | collective-permute-start | bytes 98312 | tf_op jit(solution)/shard_map/cond/branch_0_fun/ppermute | solution.py:340
  22.4 3.9 %collective-permute-start.3 = (f32[1,8,896]{2,1,0:T(8,128)S(1)}, f32[1,8,896]{2,1,0:T(8,128)S(1)}, u32[]{:S(2)}, u32[]{:S(2)}) collective-permute-start(f32[1,8,896]{2,1,0:T(8,128)S(1)} %slice.15), channel_id=1, source_target_pairs={{0,16},{8,24},{16,0},{24,8},{1,17},{9,25},{17,1},{25,9},{2,18},{10... | collective-permute-start | bytes 86024 | tf_op jit(solution)/shard_map/cond/branch_0_fun/ppermute | solution.py:340
  23.9 3.6 %collective-permute-start.4 = (f32[8,8,896]{2,1,0:T(8,128)S(1)}, f32[8,8,896]{2,1,0:T(8,128)S(1)}, u32[]{:S(2)}, u32[]{:S(2)}) collective-permute-start(f32[8,8,896]{2,1,0:T(8,128)S(1)} %get-tuple-element.78.refs_6_), channel_id=1, source_target_pairs={{0,8},{8,0},{16,24},{24,16},{1,9},{9,1},{17,25},{25,17},{2,10},{10... | collective-permute-start | bytes 688136 | tf_op jit(solution)/shard_map/cond/branch_0_fun/ppermute | solution.py:340
  26.2 1.2 %collective-permute-start.5 = (f32[1,8,896]{2,1,0:T(8,128)S(1)}, f32[1,8,896]{2,1,0:T(8,128)S(1)}, u32[]{:S(2)}, u32[]{:S(2)}) collective-permute-start(f32[1,8,896]{2,1,0:T(8,128)S(1)} %collective-permute-done.3.refs_7_), channel_id=1, source_target_pairs={{0,8},{8,0},{16,24},{24,16},{1,9},{9,1},{17,25},{25,17},{2,10},{10... | collective-permute-start | bytes 86024 | tf_op jit(solution)/shard_map/cond/branch_0_fun/ppermute | solution.py:340
